TPU v7x, 32 devices: a whole 2x2x4 slice. The times are simulated.
32 devices in a mesh: groups: 2 (over x), seq: 16 (over z, y, core).
Axes of the slice: x: 2, y: 2, z: 4, core: 2. Of those that a mesh axis runs over, the one named last changes fastest.
Arguments:
- x_in: bfloat16 [4096, 4096], P(('groups', 'seq')), parts along dimension 0, may hold values from -6 to 6
- bc_in: bfloat16 [4096, 1024], P(('groups', 'seq')), parts along dimension 0, may hold values from -6 to 6
- z_in: bfloat16 [4096, 4096], P(('groups', 'seq')), parts along dimension 0, may hold values from -6 to 6
- dt_in: bfloat16 [4096, 128], P(('groups', 'seq')), parts along dimension 0, may hold values from -4 to 4
- conv_weight: float32 [4, 5120], replicated, may hold values from -3 to 3
- conv_bias: float32 [5120], replicated, may hold values from -3 to 3
- dt_bias: float32 [128], replicated, may hold values from -4 to -2
- a_log: float32 [128], replicated, may hold values from -11.5 to 0
- d_skip: float32 [128], replicated, may hold values from 0.5 to 1.5
- norm_gain: float32 [4096], replicated, may hold values from 0.5 to 1.5
- conv_cache: bfloat16 [6, 5120], P('groups'), parts along dimension 0, may hold values from -6 to 6
- cache_state: float32 [256, 32, 64], P('groups'), parts along dimension 0, may hold values from -6 to 6
- lengths: int32 [2], P('groups'), parts along dimension 0, may hold values from 1924 to 2048
Outputs:
- mixed: bfloat16 [4096, 4096], P(('groups', 'seq')), parts along dimension 0
- final_state: float32 [256, 32, 64], P(('groups', 'seq')), parts along dimension 0
There are 2 independent parts, one for each index of `groups`. A program takes and returns all parts, laid end to end along the dimension named above; an argument that names none is the same for every part. Nothing has to cross between parts.
All inputs are finite; a program needn't handle non-finite values.
Results may differ from a plain program's by a relative error of at most 0.0085.
Values may be sent and summed in bfloat16 or wider, within the bound.
No kernel may reach another device: no remote copies, remote signals or barrier semaphores. Data moves between devices by JAX's collectives and lax.ppermute only.
A program may use at most 64 MiB of HBM per device.

v0:
```python
import jax
import jax.numpy as jnp
from jax import lax
from jax.sharding import PartitionSpec as P

STATE = 64
GROUPS = 8
CONV_W = 4


def shifted(block, axis, distance):
    devices = range(lax.axis_size(axis))
    route = [(i - distance, i) for i in devices if i - distance in devices]
    return lax.ppermute(block, axis, route)


def conv_silu(extended, conv_weight, conv_bias, count):
    total = jnp.zeros((count, extended.shape[1]), jnp.float32) + conv_bias[None, :]
    for offset in range(CONV_W):
        total = (
            total
            + extended[offset : offset + count].astype(jnp.float32) * conv_weight[offset][None, :]
        )
    return jax.nn.silu(total).astype(jnp.bfloat16)


def block_parts(x_block, b_block, c_block, dt_block, decay_rate):
    block_len, head_count, head_dim = x_block.shape
    group_count = b_block.shape[1]
    per_group = head_count // group_count
    cum_rate = jnp.cumsum(dt_block * decay_rate[None, :], axis=0)
    lower_mask = jnp.arange(block_len)[:, None] >= jnp.arange(block_len)[None, :]
    gap_rate = cum_rate.T[:, :, None] - cum_rate.T[:, None, :]
    decay = jnp.exp(jnp.where(lower_mask[None], gap_rate, -1e30))
    c_dot_b = jnp.einsum("tgn,sgn->gts", c_block, b_block, preferred_element_type=jnp.float32)
    decay_grouped = decay.reshape(group_count, per_group, block_len, block_len)
    dt_grouped = dt_block.T.reshape(group_count, per_group, 1, block_len)
    weight = (c_dot_b[:, None] * decay_grouped * dt_grouped).astype(jnp.bfloat16)
    x_grouped = x_block.reshape(block_len, group_count, per_group, head_dim)
    y_diag = jnp.einsum("gkts,sgkp->tgkp", weight, x_grouped, preferred_element_type=jnp.float32)
    y_diag = y_diag.reshape(block_len, head_count, head_dim)
    tail = jnp.exp(cum_rate[-1][None, :] - cum_rate) * dt_block
    tail_grouped = tail.reshape(block_len, group_count, per_group)
    b_weighted = (b_block.astype(jnp.float32)[:, :, None, :] * tail_grouped[:, :, :, None]).astype(
        jnp.bfloat16
    )
    local = jnp.einsum("sgkp,sgkn->gkpn", x_grouped, b_weighted, preferred_element_type=jnp.float32)
    local = local.reshape(head_count, head_dim, b_block.shape[2])
    return (y_diag, cum_rate, local)


def entering_terms(c_block, cum_rate, state):
    block_len, group_count, state_size = c_block.shape
    head_count, head_dim = (state.shape[0], state.shape[1])
    state_grouped = state.reshape(group_count, head_count // group_count, head_dim, state_size)
    product = jnp.einsum(
        "tgn,gkpn->tgkp",
        c_block.astype(jnp.float32),
        state_grouped,
        precision=lax.Precision.HIGHEST,
    )
    return jnp.exp(cum_rate)[:, :, None] * product.reshape(block_len, head_count, head_dim)


def combine(earlier, later):
    return (earlier[0] * later[0], later[0][..., None, None] * earlier[1] + later[1])


def body(
    x_in,
    bc_in,
    z_in,
    dt_in,
    conv_weight,
    conv_bias,
    dt_bias,
    a_log,
    d_skip,
    norm_gain,
    conv_cache,
    cache_state,
    lengths,
):
    tok_rows, inner_width = x_in.shape
    head_count = dt_in.shape[1]
    head_dim = inner_width // head_count
    devices = lax.axis_size("seq")
    seq_index = lax.axis_index("seq")
    rim_rows = CONV_W - 1
    x_rim, bc_rim = shifted((x_in[tok_rows - rim_rows :], bc_in[tok_rows - rim_rows :]), "seq", 1)
    is_first = seq_index == 0
    x_rim = jnp.where(is_first, conv_cache[:, :inner_width], x_rim)
    bc_rim = jnp.where(is_first, conv_cache[:, inner_width:], bc_rim)
    x_conv = conv_silu(
        jnp.concatenate([x_rim, x_in], axis=0),
        conv_weight[:, :inner_width],
        conv_bias[:inner_width],
        tok_rows,
    )
    bc_conv = conv_silu(
        jnp.concatenate([bc_rim, bc_in], axis=0),
        conv_weight[:, inner_width:],
        conv_bias[inner_width:],
        tok_rows,
    )
    decay_rate = -jnp.exp(a_log)
    share = head_count // devices
    x_send = x_conv.reshape(tok_rows, devices, share * head_dim)
    bc_grouped = bc_conv.reshape(tok_rows, 2, GROUPS, STATE).transpose(0, 2, 1, 3)
    bc_send = jnp.repeat(bc_grouped, devices // GROUPS, axis=1).reshape(
        tok_rows, devices, 2 * STATE
    )
    dt_send = dt_in.reshape(tok_rows, devices, share)
    x_heads, bc_heads, dt_heads = (
        lax.all_to_all(x_send, "seq", split_axis=1, concat_axis=0, tiled=True),
        lax.all_to_all(bc_send, "seq", split_axis=1, concat_axis=0, tiled=True),
        lax.all_to_all(dt_send, "seq", split_axis=1, concat_axis=0, tiled=True),
    )
    x_heads = x_heads.reshape(devices, tok_rows, share, head_dim)
    bc_heads = bc_heads.reshape(devices, tok_rows, 2, STATE)
    b_heads = bc_heads[:, :, 0:1, :]
    c_heads = bc_heads[:, :, 1:2, :]
    my_bias = lax.dynamic_slice_in_dim(dt_bias, seq_index * share, share, 0)
    my_rate = lax.dynamic_slice_in_dim(decay_rate, seq_index * share, share, 0)
    my_skip = lax.dynamic_slice_in_dim(d_skip, seq_index * share, share, 0)
    my_cache = lax.dynamic_slice_in_dim(cache_state, seq_index * share, share, 0)
    positions = jnp.arange(devices * tok_rows).reshape(devices, tok_rows)
    live = (positions < lengths[0]).astype(jnp.float32)
    step_size = (
        jax.nn.softplus(dt_heads.reshape(devices, tok_rows, share).astype(jnp.float32) + my_bias)
        * live[:, :, None]
    )
    parts_fn = jax.vmap(block_parts, in_axes=(0, 0, 0, 0, None))
    y_diag, cum_rate, local = parts_fn(x_heads, b_heads, c_heads, step_size, my_rate)
    block_decay = jnp.exp(cum_rate[:, -1, :])
    incl_decay, incl_state = lax.associative_scan(combine, (block_decay, local))
    before_decay = jnp.concatenate([jnp.ones((1, share), jnp.float32), incl_decay[:-1]], axis=0)
    before_state = jnp.concatenate([jnp.zeros_like(local[:1]), incl_state[:-1]], axis=0)
    entering = before_state + before_decay[:, :, None, None] * my_cache[None]
    y_full = (
        y_diag
        + jax.vmap(entering_terms)(c_heads, cum_rate, entering)
        + my_skip[None, None, :, None] * x_heads.astype(jnp.float32)
    )
    y_heads = (y_full * live[:, :, None, None]).astype(jnp.bfloat16)
    y_back = lax.all_to_all(
        y_heads.reshape(devices * tok_rows, 1, share * head_dim),
        "seq",
        split_axis=0,
        concat_axis=1,
        tiled=True,
    )
    y_out = y_back.reshape(tok_rows, inner_width)
    final_state = incl_state[-1] + incl_decay[-1][:, None, None] * my_cache
    gated = y_out.astype(jnp.float32) * jax.nn.silu(z_in.astype(jnp.float32))
    grouped = gated.reshape(tok_rows, GROUPS, inner_width // GROUPS)
    scale = lax.rsqrt(jnp.mean(grouped * grouped, axis=-1, keepdims=True) + 1e-05)
    mixed = (grouped * scale).reshape(tok_rows, inner_width) * norm_gain[None, :]
    return (mixed.astype(jnp.bfloat16), final_state)


def solution(mesh):
    in_specs = (
        P(("groups", "seq"), None),
        P(("groups", "seq"), None),
        P(("groups", "seq"), None),
        P(("groups", "seq"), None),
        P(),
        P(),
        P(),
        P(),
        P(),
        P(),
        P("groups", None),
        P("groups", None, None),
        P("groups"),
    )
    out_specs = (P(("groups", "seq"), None), P(("groups", "seq"), None, None))
    return jax.shard_map(body, mesh=mesh, in_specs=in_specs, out_specs=out_specs, check_vma=False)
```

profile of v0, /device:TPU:9, one launch (start us, length us, event | category | flops | bytes accessed | tf_op | source)
XLA Modules:
  0.0 283.9 jit_solution(17015971120254956565)
XLA Ops:
  0.6 1.6 copy.228
  2.2 6.6 %all-to-all-start.2 = ((bf16[128,16,8]{0,2,1:T(8,128)(2,1)}), bf16[128,16,8]{0,2,1:T(8,128)(2,1)S(1)}, u32[]{:S(2)}, u32[]{:S(2)}) async-start(bf16[128,16,8]{0,2,1:T(8,128)(2,1)} %bitcast.22), calls=%async_computation.2 | async-start | bytes 65536 | tf_op jit(solution)/shard_map/all_to_all | solution.py:117
  8.8 1.5 slice.205
  10.3 3.3 %collective-permute-start = (bf16[3,4096]{1,0:T(4,128)(2,1)}, bf16[3,4096]{1,0:T(4,128)(2,1)}, u32[]{:S(2)}, u32[]{:S(2)}) collective-permute-start(bf16[3,4096]{1,0:T(4,128)(2,1)} %slice.205), channel_id=1, source_target_pairs={{0,1},{1,2},{2,3},{3,4},{4,5},{5,6},{6,7},{7,8},{8,9},{9,10},{10,1... | collective-permute-start | bytes 73736 | tf_op jit(solution)/shard_map/ppermute | solution.py:14
  15.2 2.0 collective-permute-start.1
  17.3 1.7 fusion.59
  18.9 1.5 fusion.58
  23.9 1.6 copy.219
  30.8 2.5 multiply_convert_fusion.7
  34.0 2.1 copy.218
  36.2 1.4 broadcast_select_fusion
  37.5 1.9 broadcast_in_dim.10
  39.4 5.1 %all-to-all-start.1 = ((bf16[128,16,128]{0,2,1:T(8,128)(2,1)}), bf16[128,16,128]{0,2,1:T(8,128)(2,1)S(1)}, u32[]{:S(2)}, u32[]{:S(2)}) async-start(bf16[128,16,128]{0,2,1:T(8,128)(2,1)} %bitcast.14), calls=%async_computation.1 | async-start | bytes 1048576 | tf_op jit(solution)/shard_map/all_to_all | solution.py:116
  44.5 5.7 %multiply_convert_fusion.4 = bf16[128,4096]{0,1:T(8,128)(2,1)} fusion(bf16[128,4096]{0,1:T(8,128)(2,1)S(1)} %copy.219, bf16[3,4096]{0,1:T(8,128)(2,1)S(1)} %broadcast_select_fusion, f32[4096]{0:T(1024)S(1)} %bitcast.153, f32[4096]{0:T(1024)S(1)} %bitcast.154, f32[4096]{0:T(1024)S(1)} %bitcast.155, f32[4096]{0:T(1024)S(1)} %bitcast.152, f32[4096]{0:T(1024)S(1)} %slice-done.3), kind=kLoop, calls=%fused_computation.35 | loop fusion | flops 13631488 | bytes 2203648 | tf_op jit(solution)/shard_map/convert_element_type | solution.py:24
  50.8 23.3 %fusion.61 = f32[16,128,8]{2,0,1:T(8,128)S(1)} fusion(f32[16,128,8]{2,0,1:T(8,128)S(1)} %copy.229), kind=kOutput, calls=%fused_computation.119 | output fusion | flops 2080768 | bytes 131072 | tf_op jit(solution)/shard_map/vmap(jit(cumsum))/reduce_window_sum | solution.py:31
  75.6 6.0 %all-to-all-start = ((bf16[128,16,256]{0,2,1:T(8,128)(2,1)}), bf16[128,16,256]{0,2,1:T(8,128)(2,1)S(1)}, u32[]{:S(2)}, u32[]{:S(2)}) async-start(bf16[128,16,256]{0,2,1:T(8,128)(2,1)} %bitcast.4), calls=%async_computation | async-start | bytes 2097152 | tf_op jit(solution)/shard_map/all_to_all | solution.py:115
  87.3 1.5 mul.383
  88.8 3.0 %copy.245 = f32[2048,1,256]{2,0,1:T(8,128)} copy(f32[2048,1,256]{0,2,1:T(8,128)} %mul.383) | data formatting | bytes 4194304 | tf_op jit(solution)/shard_map/vmap()/mul | solution.py:62
  94.7 11.7 %all-to-all-done = bf16[128,16,256]{0,2,1:T(8,128)(2,1)S(1)} async-done(((bf16[128,16,256]{0,2,1:T(8,128)(2,1)}), bf16[128,16,256]{0,2,1:T(8,128)(2,1)S(1)}, u32[]{:S(2)}, u32[]{:S(2)}) %all-to-all-start) | async-done | bytes 1048608 | tf_op jit(solution)/shard_map/all_to_all | solution.py:115
  106.4 2.2 fusion.11
  111.2 8.7 %pad.54 = f32[4,8,32,64]{3,2,1,0:T(8,128)} pad(f32[2,8,32,64]{3,2,1,0:T(8,128)} %pad_maximum_fusion.4, f32[]{:T(128)} %constant.17.clone.1), padding=0_1_1x0_0_0x0_0_0x0_0_0 | pad | bytes 393220 | tf_op jit(solution)/shard_map/pad | solution.py:136
  119.9 8.7 %pad.55 = f32[4,8,32,64]{3,2,1,0:T(8,128)} pad(f32[2,8,32,64]{3,2,1,0:T(8,128)} %pad_add_fusion, f32[]{:T(128)} %constant.17.clone.1), padding=1_0_1x0_0_0x0_0_0x0_0_0 | pad | bytes 393220 | tf_op jit(solution)/shard_map/pad | solution.py:136
  128.6 2.1 add.221
  130.7 15.6 %pad.57 = f32[8,8,32,64]{3,2,1,0:T(8,128)} pad(f32[4,8,32,64]{3,2,1,0:T(8,128)} %add.221, f32[]{:T(128)} %constant.17.clone.1), padding=1_0_1x0_0_0x0_0_0x0_0_0 | pad | bytes 786436 | tf_op jit(solution)/shard_map/pad | solution.py:136
  146.3 1.3 fusion.32
  148.5 15.6 %pad.56 = f32[8,8,32,64]{3,2,1,0:T(8,128)} pad(f32[4,8,32,64]{3,2,1,0:T(8,128)} %pad_maximum_fusion.2, f32[]{:T(128)} %constant.17.clone.1), padding=0_1_1x0_0_0x0_0_0x0_0_0 | pad | bytes 786436 | tf_op jit(solution)/shard_map/pad | solution.py:136
  164.2 2.9 %add.223 = f32[8,8,32,64]{3,2,1,0:T(8,128)} add(f32[8,8,32,64]{3,2,1,0:T(8,128)} %pad.56, f32[8,8,32,64]{3,2,1,0:T(8,128)} %pad.57) | non-fusion elementwise | flops 131072 | bytes 1572864 | tf_op jit(solution)/shard_map/add | solution.py:136
  167.4 20.5 %pad.58 = f32[16,8,32,64]{3,2,1,0:T(8,128)} pad(f32[8,8,32,64]{3,2,1,0:T(8,128)S(1)} %pad_maximum_fusion.1, f32[]{:T(128)} %constant.17.clone.1), padding=0_1_1x0_0_0x0_0_0x0_0_0 | pad | bytes 1572868 | tf_op jit(solution)/shard_map/pad | solution.py:136
  188.0 20.6 %pad.59 = f32[16,8,32,64]{3,2,1,0:T(8,128)} pad(f32[8,8,32,64]{3,2,1,0:T(8,128)S(1)} %copy-done.2, f32[]{:T(128)} %constant.17.clone.1), padding=1_0_1x0_0_0x0_0_0x0_0_0 | pad | bytes 1572868 | tf_op jit(solution)/shard_map/pad | solution.py:136
  208.6 2.6 slice_add_fusion
  211.2 1.4 fusion.24
  212.6 2.6 copy.244
  215.2 6.2 %copy.246 = f32[2048,1,256]{2,0,1:T(8,128)} copy(f32[2048,1,256]{0,1,2:T(1,128)} %bitcast.143) | data formatting | bytes 4194304 | tf_op jit(solution)/shard_map/vmap()/reshape | solution.py:62
  221.4 2.4 fusion.23
  223.8 2.6 copy.232
  226.4 6.1 %copy.247 = f32[2048,1,256]{2,0,1:T(8,128)} copy(f32[2048,1,256]{0,1,2:T(1,128)} %bitcast.144) | data formatting | bytes 4194304 | tf_op jit(solution)/shard_map/vmap()/reshape | solution.py:41
  232.4 1.6 bitcast_convert_fusion
  234.0 3.0 %copy.248 = f32[16,128,1,256]{3,1,0,2:T(8,128)} copy(f32[16,128,1,256]{1,3,0,2:T(8,128)} %bitcast_convert_fusion) | data formatting | bytes 4194304 | tf_op jit(solution)/shard_map/convert_element_type | solution.py:143
  237.0 3.9 %fusion.16 = bf16[2048,1,256]{2,0,1:T(8,128)(2,1)S(1)} fusion(f32[16,128,1,256]{3,1,0,2:T(8,128)} %copy.248, f32[2048,1,256]{2,0,1:T(8,128)} %copy.247, f32[2048,1,256]{2,0,1:T(8,128)} %copy.245, f32[2048,1,256]{2,0,1:T(8,128)} %copy.246, f32[2048]{0:T(1024)S(1)} %copy-done.17, f32[256]{0:T(256)S(1)} %copy-done.20), kind=kLoop, calls=%fused_computation.28 | loop fusion | flops 3145728 | bytes 9446400 | tf_op jit(solution)/shard_map/convert_element_type | solution.py:145
  241.4 1.4 reduce.6
  244.0 5.0 %all-to-all-start.3 = ((bf16[16,2,16384]{2,1,0:T(2,128)(2,1)}), bf16[16,2,16384]{2,1,0:T(2,128)(2,1)S(1)}, u32[]{:S(2)}, u32[]{:S(2)}) async-start(bf16[16,2,16384]{2,1,0:T(2,128)(2,1)} %reshape.300), calls=%async_computation.3 | async-start | bytes 2097152 | tf_op jit(solution)/shard_map/all_to_all | solution.py:146
  249.0 1.3 copy.252
  250.5 20.5 %pad.159 = f32[15,8,32,64]{3,2,1,0:T(8,128)} pad(f32[8,8,32,64]{3,2,1,0:T(8,128)S(1)} %copy-done.2, f32[]{:T(128)} %constant.17.clone.1), padding=0_0_1x0_0_0x0_0_0x0_0_0 | pad | bytes 1507332
  271.0 1.6 bitcast_add_fusion
  275.1 1.6 convert_bitcast_fusion
  276.7 2.0 copy.251
  279.9 1.7 fusion.13
  281.6 2.3 copy.253
  (153 shorter events, 30.1 us)
Async XLA Ops:
  0.6 22.3 %copy-start = (f32[128,32,64]{0,2,1:T(8,128)S(1)}, f32[128,32,64]{0,2,1:T(8,128)}, u32[]{:S(2)}) copy-start(f32[128,32,64]{0,2,1:T(8,128)} %param.24) | copy-start | bytes 3145732
  2.2 35.3 %all-to-all-start.2 = ((bf16[128,16,8]{0,2,1:T(8,128)(2,1)}), bf16[128,16,8]{0,2,1:T(8,128)(2,1)S(1)}, u32[]{:S(2)}, u32[]{:S(2)}) async-start(bf16[128,16,8]{0,2,1:T(8,128)(2,1)} %bitcast.22), calls=%async_computation.2 | async-start | bytes 65536 | tf_op jit(solution)/shard_map/all_to_all | solution.py:117
  10.3 23.7 %collective-permute-start = (bf16[3,4096]{1,0:T(4,128)(2,1)}, bf16[3,4096]{1,0:T(4,128)(2,1)}, u32[]{:S(2)}, u32[]{:S(2)}) collective-permute-start(bf16[3,4096]{1,0:T(4,128)(2,1)} %slice.205), channel_id=1, source_target_pairs={{0,1},{1,2},{2,3},{3,4},{4,5},{5,6},{6,7},{7,8},{8,9},{9,10},{10,1... | collective-permute-start | bytes 73736 | tf_op jit(solution)/shard_map/ppermute | solution.py:14
  15.2 14.5 %collective-permute-start.1 = (bf16[3,1024]{0,1:T(8,128)(2,1)}, bf16[3,1024]{0,1:T(8,128)(2,1)}, u32[]{:S(2)}, u32[]{:S(2)}) collective-permute-start(bf16[3,1024]{0,1:T(8,128)(2,1)} %copy.221), channel_id=1, source_target_pairs={{0,1},{1,2},{2,3},{3,4},{4,5},{5,6},{6,7},{7,8},{8,9},{9,10},{10,1... | collective-permute-start | bytes 18440 | tf_op jit(solution)/shard_map/ppermute | solution.py:14
  22.9 2.6 copy-start.13
  22.9 3.6 %slice-start.1 = ((bf16[3,5120]{1,0:T(4,128)(2,1)}), bf16[3,4096]{1,0:T(4,128)(2,1)S(1)}, s32[]{:S(2)}) async-start(bf16[3,5120]{1,0:T(4,128)(2,1)} %param.23), calls=%async_computation.5 | async-start | bytes 65536 | tf_op jit(solution)/shard_map/slice | solution.py:92
  23.3 3.1 %copy-start.25 = (f32[128]{0:T(128)S(1)}, f32[128]{0:T(128)}, u32[]{:S(2)}) copy-start(f32[128]{0:T(128)} %param.19) | copy-start | bytes 1540
  23.3 3.2 %copy-start.26 = (f32[128]{0:T(128)S(1)}, f32[128]{0:T(128)}, u32[]{:S(2)}) copy-start(f32[128]{0:T(128)} %exponential_negate_fusion) | copy-start | bytes 1540
  23.3 3.8 %slice-start.2 = ((bf16[3,5120]{1,0:T(4,128)(2,1)}), bf16[3,1024]{1,0:T(4,128)(2,1)S(1)}, s32[]{:S(2)}) async-start(bf16[3,5120]{1,0:T(4,128)(2,1)} %param.23), calls=%async_computation.6 | async-start | bytes 16384 | tf_op jit(solution)/shard_map/slice | solution.py:93
  25.5 5.2 %slice-start.4 = ((f32[5120]{0:T(1024)}), f32[1024]{0:T(1024)S(1)}, s32[]{:S(2)}) async-start(f32[5120]{0:T(1024)} %param.18), calls=%async_computation.8 | async-start | bytes 8192 | tf_op jit(solution)/shard_map/slice | solution.py:103
  26.5 23.7 %copy-start.21 = (f32[8]{0:T(128)}, f32[8]{0:T(128)S(1)}, u32[]{:S(2)}) copy-start(f32[8]{0:T(128)S(1)} %dynamic_slice.12) | copy-start | bytes 100
  36.1 8.4 %slice-start.3 = ((f32[5120]{0:T(1024)}), f32[4096]{0:T(1024)S(1)}, s32[]{:S(2)}) async-start(f32[5120]{0:T(1024)} %param.18), calls=%async_computation.7 | async-start | bytes 32768 | tf_op jit(solution)/shard_map/slice | solution.py:97
  36.1 8.4 %copy-start.14 = (f32[1,4096]{1,0:T(1,128)S(1)}, f32[1,4096]{1,0:T(1,128)}, u32[]{:S(2)}) copy-start(f32[1,4096]{1,0:T(1,128)} %get-tuple-element.25) | copy-start | bytes 49156
  39.4 35.3 %all-to-all-start.1 = ((bf16[128,16,128]{0,2,1:T(8,128)(2,1)}), bf16[128,16,128]{0,2,1:T(8,128)(2,1)S(1)}, u32[]{:S(2)}, u32[]{:S(2)}) async-start(bf16[128,16,128]{0,2,1:T(8,128)(2,1)} %bitcast.14), calls=%async_computation.1 | async-start | bytes 1048576 | tf_op jit(solution)/shard_map/all_to_all | solution.py:116
  74.7 0.9 copy-start.8
  75.6 30.9 %all-to-all-start = ((bf16[128,16,256]{0,2,1:T(8,128)(2,1)}), bf16[128,16,256]{0,2,1:T(8,128)(2,1)S(1)}, u32[]{:S(2)}, u32[]{:S(2)}) async-start(bf16[128,16,256]{0,2,1:T(8,128)(2,1)} %bitcast.4), calls=%async_computation | async-start | bytes 2097152 | tf_op jit(solution)/shard_map/all_to_all | solution.py:115
  88.8 3.0 %copy-start.22 = (f32[8]{0:T(128)S(1)}, f32[8]{0:T(128)}, u32[]{:S(2)}) copy-start(f32[8]{0:T(128)} %copy-done.21) | copy-start | bytes 100
  88.8 3.8 %copy-start.9 = (bf16[128,16,128]{0,2,1:T(8,128)(2,1)S(1)}, bf16[128,16,128]{0,2,1:T(8,128)(2,1)}, u32[]{:S(2)}) copy-start(bf16[128,16,128]{0,2,1:T(8,128)(2,1)} %copy-done.8) | copy-start | bytes 1572868
  108.9 1.6 copy-start.7
  108.9 0.7 copy-start.23
  108.9 1.5 copy-start.24
  128.6 19.1 %slice-start = ((f32[8,8,32,64]{3,2,1,0:T(8,128)}), f32[1,8,32,64]{3,2,1,0:T(8,128)S(1)}, s32[]{:S(2)}) async-start(f32[8,8,32,64]{3,2,1,0:T(8,128)} %copy-done.7), calls=%async_computation.4 | async-start | bytes 262144 | tf_op jit(solution)/shard_map/slice | solution.py:136
  164.2 2.9 %copy-start.5 = (f32[8,8,32,64]{3,2,1,0:T(8,128)S(1)}, f32[8,8,32,64]{3,2,1,0:T(8,128)}, u32[]{:S(2)}) copy-start(f32[8,8,32,64]{3,2,1,0:T(8,128)} %pad.57) | copy-start | bytes 1572868
  164.2 2.9 %copy-start.6 = (f32[8,8,32,64]{3,2,1,0:T(8,128)S(1)}, f32[8,8,32,64]{3,2,1,0:T(8,128)}, u32[]{:S(2)}) copy-start(f32[8,8,32,64]{3,2,1,0:T(8,128)} %pad.56) | copy-start | bytes 1572868
  167.4 20.5 %copy-start.2 = (f32[8,8,32,64]{3,2,1,0:T(8,128)S(1)}, f32[8,8,32,64]{3,2,1,0:T(8,128)}, u32[]{:S(2)}) copy-start(f32[8,8,32,64]{3,2,1,0:T(8,128)} %add.223) | copy-start | bytes 1572868
  208.6 2.6 copy-start.10
  215.2 6.2 %copy-start.11 = (f32[16,128,128]{2,1,0:T(8,128)S(1)}, f32[16,128,128]{2,1,0:T(8,128)}, u32[]{:S(2)}) copy-start(f32[16,128,128]{2,1,0:T(8,128)} %fusion.36) | copy-start | bytes 3145732
  215.2 6.2 %copy-start.15 = (f32[16,8,128]{2,1,0:T(8,128)S(1)}, f32[16,8,128]{2,1,0:T(8,128)}, u32[]{:S(2)}) copy-start(f32[16,8,128]{2,1,0:T(8,128)} %copy.230) | copy-start | bytes 196612
  215.2 6.2 %copy-start.16 = (f32[16,8,128]{2,1,0:T(8,128)S(1)}, f32[16,8,128]{2,1,0:T(8,128)}, u32[]{:S(2)}) copy-start(f32[16,8,128]{2,1,0:T(8,128)} %get-tuple-element.27) | copy-start | bytes 196612
  215.2 6.2 %copy-start.19 = (pred[128,128]{1,0:T(8,128)(4,1)S(1)}, pred[128,128]{1,0:T(8,128)(4,1)}, u32[]{:S(2)}) copy-start(pred[128,128]{1,0:T(8,128)(4,1)} %iota_compare_fusion) | copy-start | bytes 49156
  234.0 3.0 %copy-start.17 = (f32[2048]{0:T(1024)S(1)}, f32[2048]{0:T(1024)}, u32[]{:S(2)}) copy-start(f32[2048]{0:T(1024)} %fusion.52) | copy-start | bytes 24580
  234.0 3.0 %copy-start.20 = (f32[256]{0:T(256)S(1)}, f32[256]{0:T(256)}, u32[]{:S(2)}) copy-start(f32[256]{0:T(256)} %mul.417) | copy-start | bytes 3076
  242.9 6.1 %copy-start.12 = (bf16[128,4096]{1,0:T(8,128)(2,1)S(1)}, bf16[128,4096]{1,0:T(8,128)(2,1)}, u32[]{:S(2)}) copy-start(bf16[128,4096]{1,0:T(8,128)(2,1)} %param.15) | copy-start | bytes 3145732
  244.0 29.8 %all-to-all-start.3 = ((bf16[16,2,16384]{2,1,0:T(2,128)(2,1)}), bf16[16,2,16384]{2,1,0:T(2,128)(2,1)S(1)}, u32[]{:S(2)}, u32[]{:S(2)}) async-start(bf16[16,2,16384]{2,1,0:T(2,128)(2,1)} %reshape.300), calls=%async_computation.3 | async-start | bytes 2097152 | tf_op jit(solution)/shard_map/all_to_all | solution.py:146
  276.7 2.0 copy-start.3
  278.7 1.2 copy-start.4
  278.7 1.2 copy-start.18
  279.9 4.0 %copy-start.1 = (f32[128,32,64]{0,2,1:T(8,128)S(1)}, f32[128,32,64]{0,2,1:T(8,128)}, u32[]{:S(2)}) copy-start(f32[128,32,64]{0,2,1:T(8,128)} %param.24) | copy-start | bytes 3145732
where the time goes:
time: 289 us; the launch traced here: 284 us
  local copies, waits for them, and re-layouts  169 us (58%)
  other arithmetic  64.6 us (22%)
  starting transfers between devices  28.1 us (10%)
  waiting for transfers between devices  12.9 us (4%)
  matrix products  7.32 us (3%)
    pad x12, local copies, waits for them, and re-layouts, body(): incl_decay, incl_state = lax.associative_scan(combine, (block_decay, local))  90.2 us
    unnamed x64, local copies, waits for them, and re-layouts  32.5 us
    another operation x1, other arithmetic, block_parts(): cum_rate = jnp.cumsum(dt_block * decay_rate[None, :], axis=0)  23.3 us
    all_to_all x1, waiting for transfers between devices, body(): lax.all_to_all(x_send, 'seq', split_axis=1, concat_axis=0, tiled=True)  11.7 us
    add x8, other arithmetic, body(): incl_decay, incl_state = lax.associative_scan(combine, (block_decay, local))  8.5 us
    convert_element_type x2, other arithmetic, conv_silu(): return jax.nn.silu(total).astype(jnp.bfloat16)  8.19 us
    all_to_all x1, starting transfers between devices, body(): lax.all_to_all(dt_send, 'seq', split_axis=1, concat_axis=0, tiled=True)  6.61 us
    reshape x1, local copies, waits for them, and re-layouts, entering_terms(): product.reshape(block_len, head_count, head_dim)  6.16 us
  transfers between devices with their start and end apart: 6, of which 2 were waited for; matrix products, arithmetic and copies ran while one was open for 31% of the time, Pallas kernels for 0%

commit v1 on v0

v1 whole, which is shorter than its diff:
```python
import functools

import jax
import jax.numpy as jnp
from jax import lax
from jax.experimental import pallas as pl
from jax.experimental.pallas import tpu as pltpu
from jax.sharding import PartitionSpec as P

STATE = 64
GROUPS = 8
CONV_W = 4
RIM = CONV_W - 1
LOG2E = 1.4426950408889634
BF16 = jnp.bfloat16
F32 = jnp.float32
HI = lax.Precision.HIGHEST
SEQ = "seq"
PAIR = 2
TOP = 16


def silu(v):
    half = 0.5 * v
    return half + half * jnp.tanh(half)


def split2(v):
    hi = v.astype(BF16)
    return hi, (v - hi.astype(F32)).astype(BF16)


def grid_call(body, grid, in_specs, out_specs, out_shape, scratch=(), flops=0, nbytes=0, vmem=24):
    return pl.pallas_call(
        body,
        grid=grid,
        in_specs=in_specs,
        out_specs=out_specs,
        out_shape=out_shape,
        scratch_shapes=list(scratch),
        compiler_params=pltpu.CompilerParams(vmem_limit_bytes=vmem * 2**20),
        cost_estimate=pl.CostEstimate(flops=flops, bytes_accessed=nbytes, transcendentals=0),
    )


def conv_rows(ext, weights, bias, count, first, cols):
    total = jnp.broadcast_to(bias, (count, bias.shape[1]))
    for k in range(CONV_W):
        total = total + ext[pl.ds(first + k - RIM, count), cols] * weights[k : k + 1, :]
    return silu(total)


def conv_kernel(
    len_ref,
    x_ref,
    b_ref,
    c_ref,
    dt_ref,
    wx_ref,
    wb_ref,
    wc_ref,
    cx_ref,
    cb_ref,
    cc_ref,
    dtb_ref,
    alog_ref,
    xo_ref,
    bo_ref,
    co_ref,
    cum_ref,
    row_ref,
    tail_ref,
    ecum_ref,
    dec_ref,
    ext,
    *,
    heads,
    head_dim,
):
    step = pl.program_id(0)
    rows = x_ref.shape[0]
    per_step = heads // pl.num_programs(0)

    def conv(src, w, bias, dst):
        width = src.shape[1]
        for j in range(width // 128):
            cols = pl.ds(128 * j, 128)
            ext[8:, :] = src[:, cols].astype(F32)
            weights, offset = w[:, cols], bias[:, cols]
            dst[:, cols] = conv_rows(ext, weights, offset, rows, 8, slice(None)).astype(BF16)

    ext[0:8, :] = jnp.zeros((8, 128), F32)

    @pl.when(step == 0)
    def _():
        raw = dt_ref[...].astype(F32) + dtb_ref[...]
        soft = jnp.maximum(raw, 0.0) + jnp.log1p(jnp.exp(-jnp.abs(raw)))
        first = lax.axis_index(SEQ) * rows
        token = first + lax.broadcasted_iota(jnp.int32, (rows, heads), 0)
        dt = jnp.where(token < len_ref[0], soft, 0.0)
        rate = -jnp.exp(alog_ref[...]) * dt
        below = lax.broadcasted_iota(jnp.int32, (rows, rows), 0)
        across = lax.broadcasted_iota(jnp.int32, (rows, rows), 1)
        tri = (below >= across).astype(F32)
        cum = jnp.dot(tri, rate, precision=HI, preferred_element_type=F32)
        last = cum[rows - 1 : rows, :]
        tail = jnp.exp(last - cum) * dt
        ecum = jnp.exp(cum)
        cum_ref[...] = cum * LOG2E
        log_dt = jnp.where(dt > 0.0, jnp.log(jnp.maximum(dt, 1e-38)) * LOG2E, -1e30)
        row_ref[...] = (cum * LOG2E - log_dt).T
        tail_hi, tail_lo = split2(tail)
        ecum_hi, ecum_lo = split2(ecum)
        for i in range(heads // per_step):
            part = slice(i * per_step, (i + 1) * per_step)
            tail_ref[i] = jnp.concatenate([tail_hi[:, part], tail_lo[:, part]], axis=1)
            ecum_ref[i] = jnp.concatenate([ecum_hi[:, part], ecum_lo[:, part]], axis=1)
        steps = heads // per_step
        unit_heads = per_step // (2 * PAIR)
        unit_cols = unit_heads * head_dim
        owner = lax.broadcasted_iota(jnp.int32, (8, heads), 0)
        head = lax.broadcasted_iota(jnp.int32, (8, heads), 1)
        chosen = jnp.where(head // per_step == owner, jnp.exp(last), 0.0)
        head = lax.broadcasted_iota(jnp.int32, (heads, unit_cols), 0)
        lane = lax.broadcasted_iota(jnp.int32, (heads, unit_cols), 1)
        same = head % unit_heads == lane // head_dim
        for q in range(2 * PAIR):
            spread = jnp.where(same & ((head % per_step) // unit_heads == q), 1.0, 0.0)
            dec = jnp.dot(chosen, spread, precision=HI, preferred_element_type=F32)
            dec_ref[q] = pack_decay(dec)

    conv(x_ref, wx_ref, cx_ref, xo_ref)
    conv(b_ref, wb_ref, cb_ref, bo_ref)
    conv(c_ref, wc_ref, cc_ref, co_ref)


def pack_decay(dec):
    hi, lo = split2(dec)
    return jnp.concatenate([hi.astype(F32), lo.astype(F32)], axis=0).astype(BF16)


def unpack_decay(rows):
    both = rows.astype(F32)
    return both[0:8] + both[8:16]


def local_kernel(
    xc_ref,
    bc_ref,
    xtop_ref,
    btop_ref,
    ctop_ref,
    xrim_ref,
    brim_ref,
    crim_ref,
    xcache_ref,
    bcache_ref,
    ccache_ref,
    wx_ref,
    wb_ref,
    wc_ref,
    cx_ref,
    cb_ref,
    cc_ref,
    tail_ref,
    dec_ref,
    send_ref,
    keep_ref,
    xfix_ref,
    bfix_ref,
    cfix_ref,
    ext,
    *,
    head_dim,
):
    step = pl.program_id(0)
    steps = pl.num_programs(0)
    device = lax.axis_index(SEQ)
    core = device % 2
    rows, width = xc_ref.shape
    unit = width // (2 * PAIR)
    state_rows = steps * STATE

    def fix(top, rim, cache, w, bias, dst):
        cols = top.shape[1]
        ext[8 : 8 + TOP, 0:cols] = top[...].astype(F32)
        before = jnp.where(device == 0, cache[...].astype(F32), rim[...].astype(F32))
        ext[8 - RIM : 8, 0:cols] = before
        fixed = conv_rows(ext, w[...], bias[...], TOP, 8, pl.ds(0, cols)).astype(BF16)
        dst[...] = fixed
        return fixed

    xfix = fix(xtop_ref, xrim_ref, xcache_ref, wx_ref, cx_ref, xfix_ref)
    bfix = fix(btop_ref, brim_ref, bcache_ref, wb_ref, cb_ref, bfix_ref)
    fix(ctop_ref, crim_ref, ccache_ref, wc_ref, cc_ref, cfix_ref)
    b_all = jnp.concatenate([bfix, bc_ref[TOP:, :]], axis=0)
    b_turned = b_all.T
    per_step = tail_ref.shape[2] // 2
    head = lax.broadcasted_iota(jnp.int32, (2 * per_step, width), 0) % per_step
    lane = lax.broadcasted_iota(jnp.int32, (2 * per_step, width), 1)
    spread = jnp.where(head == lane // head_dim, 1.0, 0.0).astype(BF16)
    tail = jnp.dot(tail_ref[0], spread, preferred_element_type=F32)
    x_all = jnp.concatenate([xfix, xc_ref[TOP:, :]], axis=0)
    scaled = (x_all.astype(F32) * tail).astype(BF16)
    where = pl.ds(pl.multiple_of(step * STATE, STATE), STATE)
    for y in range(PAIR):
        lhs = b_turned[y * STATE : (y + 1) * STATE, :]
        both = jnp.dot(
            lhs, scaled[:, 2 * y * unit : 2 * (y + 1) * unit], preferred_element_type=F32
        ).astype(BF16)
        low, high = both[:, :unit], both[:, unit:]
        send_ref[y, where, :] = jnp.where(core == 0, high, low)
        keep_ref[y, where, :] = jnp.where(core == 0, low, high)

    @pl.when(step == 0)
    def _():
        for y in range(PAIR):
            send_ref[y, state_rows:, :] = dec_ref[2 * y + 1 - core]
            keep_ref[y, state_rows:, :] = dec_ref[2 * y + core]


def blocks_of(rows):
    return [(i, slice(i * STATE, (i + 1) * STATE)) for i in range(rows // STATE)]


def core_kernel(keep_ref, recv_ref, send_ref, own_ref):
    device = lax.axis_index(SEQ)
    core, side = device % 2, (device // 2) % 2
    rows = keep_ref.shape[1] - 16
    for out, pick in ((send_ref, 1 - side), (own_ref, side)):
        mine, other = keep_ref.at[pick], recv_ref.at[pick]
        join_totals(mine, other, core == 0, out, rows)


def join_totals(mine, other, mine_first, out, rows):
    d_mine = unpack_decay(mine[rows:, :])
    d_other = unpack_decay(other[rows:, :])
    d_later = jnp.where(mine_first, d_other, d_mine)
    f_mine = jnp.where(mine_first, d_later, 1.0)
    f_other = jnp.where(mine_first, 1.0, d_later)
    for i, part in blocks_of(rows):
        total = mine[part, :].astype(F32) * f_mine[i : i + 1] + other[part, :].astype(F32) * f_other[
            i : i + 1
        ]
        out[part, :] = total.astype(BF16)
    out[rows:, :] = pack_decay(d_mine * d_other)


def total_kernel(mine_ref, other_ref, out_ref, *, bit):
    device = lax.axis_index(SEQ)
    rows = mine_ref.shape[0] - 16
    join_totals(mine_ref, other_ref, (device // bit) % 2 == 0, out_ref, rows)


def prefix_kernel(mine_ref, other_ref, pre_ref, dpre_ref, out_ref, opre_ref, odpre_ref, *, bit):
    device = lax.axis_index(SEQ)
    rows = mine_ref.shape[0] - 16
    first = (device // bit) % 2 == 0
    join_totals(mine_ref, other_ref, first, out_ref, rows)
    d_other = unpack_decay(other_ref[rows:, :])
    d_pre = dpre_ref[...]
    gain = jnp.where(first, 0.0, d_pre)
    for i, part in blocks_of(rows):
        opre_ref[part, :] = pre_ref[part, :] + gain[i : i + 1] * other_ref[part, :].astype(F32)
    odpre_ref[...] = jnp.where(first, d_pre, d_pre * d_other)


def start_kernel(mine_ref, other_ref, out_ref, opre_ref, odpre_ref, *, bit):
    device = lax.axis_index(SEQ)
    rows = mine_ref.shape[0] - 16
    first = (device // bit) % 2 == 0
    join_totals(mine_ref, other_ref, first, out_ref, rows)
    d_other = unpack_decay(other_ref[rows:, :])
    opre_ref[...] = jnp.where(first, 0.0, other_ref[:rows, :].astype(F32))
    odpre_ref[...] = jnp.where(first, 1.0, d_other)


def enter_kernel(
    mine_ref, other_ref, pre_ref, dpre_ref, cache_ref, own_ref, recv_ref, send_ref, stay_ref, fin_ref, *, bit
):
    device = lax.axis_index(SEQ)
    side = (device // 2) % 2
    rows = mine_ref.shape[0] - 16
    first = (device // bit) % 2 == 0
    d_mine = unpack_decay(mine_ref[rows:, :])
    d_other = unpack_decay(other_ref[rows:, :])
    d_later = jnp.where(first, d_other, d_mine)
    f_mine = jnp.where(first, d_later, 1.0)
    f_other = jnp.where(first, 1.0, d_later)
    d_all = d_mine * d_other
    d_pre = dpre_ref[...]
    gain = jnp.where(first, 0.0, d_pre)
    d_before = jnp.where(first, d_pre, d_pre * d_other)
    d_first = jnp.where(side == 0, unpack_decay(own_ref[rows:, :]), unpack_decay(recv_ref[rows:, :]))
    for i, part in blocks_of(rows):
        cache = cache_ref[part, :]
        other = other_ref[part, :].astype(F32)
        mine = mine_ref[part, :].astype(F32)
        row = slice(i, i + 1)
        fin_ref[part, :] = d_all[row] * cache + mine * f_mine[row] + other * f_other[row]
        plane = d_before[row] * cache + pre_ref[part, :] + gain[row] * other
        t_first = jnp.where(side == 0, own_ref[part, :].astype(F32), recv_ref[part, :].astype(F32))
        second = d_first[row] * plane + t_first
        send_ref[part, :] = jnp.where(side == 0, second, plane).astype(BF16)
        stay_ref[part, :] = jnp.where(side == 0, plane, second).astype(BF16)


def chip_kernel(stay_ref, recv_ref, keep_ref, part_ref, send_ref, own_ref):
    device = lax.axis_index(SEQ)
    core, side = device % 2, (device // 2) % 2
    rows = stay_ref.shape[0]
    for y in range(PAIR):
        d_first = jnp.where(
            core == 0, unpack_decay(keep_ref[y, rows:, :]), unpack_decay(part_ref[y, rows:, :])
        )
        for i, part in blocks_of(rows):
            chip = jnp.where(side == y, stay_ref[part, :], recv_ref[part, :])
            local = jnp.where(core == 0, keep_ref[y, part, :], part_ref[y, part, :])
            second = (d_first[i : i + 1] * chip.astype(F32) + local.astype(F32)).astype(BF16)
            send_ref[y, part, :] = jnp.where(core == 0, second, chip)
            own_ref[y, part, :] = jnp.where(core == 0, chip, second)


def diag_kernel(
    xc_ref, xfix_ref, b_ref, bfix_ref, c_ref, cfix_ref, cum_ref, row_ref, skip_ref, out_ref, *, head_dim, first
):
    rows, width = xc_ref.shape
    per_group = width // head_dim // PAIR
    below = lax.broadcasted_iota(jnp.int32, (rows, rows), 0)
    across = lax.broadcasted_iota(jnp.int32, (rows, rows), 1)
    mask = below >= across
    b_all = jnp.concatenate([bfix_ref[...], b_ref[TOP:, :]], axis=0)
    c_all = jnp.concatenate([cfix_ref[...], c_ref[TOP:, :]], axis=0)
    b_turned = b_all.T
    quad = 128 // head_dim
    lane = lax.broadcasted_iota(jnp.int32, (rows, 128), 1) // head_dim
    heads = cum_ref.shape[1]
    base = (first + pl.program_id(0)) * PAIR * per_group
    cum = pltpu.roll(cum_ref[...], heads - base, axis=1)
    for y in range(PAIR):
        part = slice(y * STATE, (y + 1) * STATE)
        c_dot_b = jnp.dot(c_all[:, part], b_turned[part, :], preferred_element_type=F32)
        for q in range(per_group // quad):
            cols = pl.ds((y * per_group + q * quad) * head_dim, 128)
            x_quad = jnp.concatenate([xfix_ref[:, cols], xc_ref[TOP:, cols]], axis=0)
            lhs, rhs = [], []
            for k in range(quad):
                head = y * per_group + q * quad + k
                gap = cum[:, head : head + 1] - row_ref[head : head + 1, :]
                decay = jnp.exp2(jnp.where(mask, gap, -1e30))
                lhs.append((c_dot_b * decay).astype(BF16))
                rhs.append(jnp.where(lane == k, x_quad, jnp.zeros_like(x_quad)))
            inner = jnp.dot(
                jnp.concatenate(lhs, axis=1),
                jnp.concatenate(rhs, axis=0),
                preferred_element_type=F32,
            )
            out_ref[:, cols] = inner + skip_ref[:, cols] * x_quad.astype(F32)


def out_kernel(
    len_ref, diag_ref, c_ref, cfix_ref, ecum_ref, own_ref, recv_ref, z_ref, gain_ref, out_ref, *, head_dim
):
    device = lax.axis_index(SEQ)
    core = device % 2
    rows, width = diag_ref.shape
    unit = width // (2 * PAIR)
    c_all = jnp.concatenate([cfix_ref[...], c_ref[TOP:, :]], axis=0)
    per_step = ecum_ref.shape[2] // 2
    head = lax.broadcasted_iota(jnp.int32, (2 * per_step, width), 0) % per_step
    lane = lax.broadcasted_iota(jnp.int32, (2 * per_step, width), 1)
    spread = jnp.where(head == lane // head_dim, 1.0, 0.0).astype(BF16)
    grow = jnp.dot(ecum_ref[0], spread, preferred_element_type=F32)
    token = device * rows + lax.broadcasted_iota(jnp.int32, (rows, 1), 0)
    live = (token < len_ref[0]).astype(F32)
    for y in range(PAIR):
        own, recv = own_ref[y], recv_ref[y]
        state = jnp.concatenate(
            [jnp.where(core == 0, own, recv), jnp.where(core == 0, recv, own)], axis=1
        )
        cols = slice(2 * y * unit, 2 * (y + 1) * unit)
        entering = jnp.dot(
            c_all[:, y * STATE : (y + 1) * STATE], state, preferred_element_type=F32
        )
        y_all = (diag_ref[:, cols] + grow[:, cols] * entering) * live
        y_all = y_all.astype(BF16).astype(F32)
        gated = y_all * silu(z_ref[:, cols].astype(F32))
        scale = lax.rsqrt(jnp.mean(gated * gated, axis=1, keepdims=True) + 1e-05)
        out_ref[:, cols] = (gated * scale * gain_ref[:, cols]).astype(BF16)


def swap(value, mask):
    devices = range(lax.axis_size(SEQ))
    return lax.ppermute(value, SEQ, [(i, i ^ mask) for i in devices])


def whole(shape):
    return pl.BlockSpec(shape, lambda *_: (0,) * len(shape))


def plain_call(body, out_shape, *args, nbytes=2**20):
    return pl.pallas_call(
        body,
        out_shape=out_shape,
        in_specs=[pl.BlockSpec(memory_space=pltpu.VMEM)] * len(args),
        out_specs=jax.tree.map(lambda _: pl.BlockSpec(memory_space=pltpu.VMEM), out_shape),
        compiler_params=pltpu.CompilerParams(vmem_limit_bytes=12 * 2**20),
        cost_estimate=pl.CostEstimate(flops=0, bytes_accessed=nbytes, transcendentals=0),
    )(*args)


def body(
    x_in,
    bc_in,
    z_in,
    dt_in,
    conv_weight,
    conv_bias,
    dt_bias,
    a_log,
    d_skip,
    norm_gain,
    conv_cache,
    cache_state,
    lengths,
):
    rows, inner = x_in.shape
    heads = dt_in.shape[1]
    head_dim = inner // heads
    devices = lax.axis_size(SEQ)
    index = lax.axis_index(SEQ)
    share = heads // devices
    steps = GROUPS // PAIR
    per_step = heads // steps
    width = inner // steps
    bcw = PAIR * STATE
    b0, c0 = inner // bcw, inner // bcw + steps
    unit = width // (2 * PAIR)
    state_rows = steps * STATE
    msg_rows = state_rows + 16
    sds = jax.ShapeDtypeStruct
    smem = pl.BlockSpec(memory_space=pltpu.SMEM)

    bias2 = conv_bias.reshape(1, -1)
    rim = jnp.concatenate([x_in[rows - RIM :], bc_in[rows - RIM :]], axis=1)
    rim = lax.ppermute(rim, SEQ, [(i, (i + 1) % devices) for i in range(devices)])

    def at(r, c, off):
        return pl.BlockSpec((r, c), lambda i: (0, i + off))

    def lead(shape):
        return pl.BlockSpec((1,) + shape, lambda i: (i,) + (0,) * len(shape))

    weight_specs = [at(CONV_W, width, 0), at(CONV_W, bcw, b0), at(CONV_W, bcw, c0)]
    bias_specs = [at(1, width, 0), at(1, bcw, b0), at(1, bcw, c0)]
    xc, bc, cc, cum, row, tail, ecum, dec = grid_call(
        functools.partial(conv_kernel, heads=heads, head_dim=head_dim),
        (steps,),
        [smem, at(rows, width, 0), at(rows, bcw, 0), at(rows, bcw, steps), whole((rows, heads))]
        + weight_specs
        + bias_specs
        + [whole((1, heads))] * 2,
        [
            at(rows, width, 0),
            at(rows, bcw, 0),
            at(rows, bcw, 0),
            whole((rows, heads)),
            whole((heads, rows)),
            whole((steps, rows, 2 * per_step)),
            whole((steps, rows, 2 * per_step)),
            whole((2 * PAIR, 16, unit)),
        ],
        [
            sds((rows, inner), BF16),
            sds((rows, GROUPS * STATE), BF16),
            sds((rows, GROUPS * STATE), BF16),
            sds((rows, heads), F32),
            sds((heads, rows), F32),
            sds((steps, rows, 2 * per_step), BF16),
            sds((steps, rows, 2 * per_step), BF16),
            sds((2 * PAIR, 16, unit), BF16),
        ],
        scratch=[pltpu.VMEM((8 + rows, 128), F32)],
        nbytes=4 * 2**20,
    )(
        lengths,
        x_in,
        bc_in,
        bc_in,
        dt_in,
        conv_weight,
        conv_weight,
        conv_weight,
        bias2,
        bias2,
        bias2,
        dt_bias.reshape(1, -1),
        a_log.reshape(1, -1),
    )

    send, keep, xfix, bfix, cfix = grid_call(
        functools.partial(local_kernel, head_dim=head_dim),
        (steps,),
        [at(rows, width, 0), at(rows, bcw, 0)]
        + [at(TOP, width, 0), at(TOP, bcw, 0), at(TOP, bcw, steps)]
        + [at(RIM, width, 0), at(RIM, bcw, b0), at(RIM, bcw, c0)] * 2
        + weight_specs
        + bias_specs
        + [lead((rows, 2 * per_step)), whole((2 * PAIR, 16, unit))],
        [
            whole((PAIR, msg_rows, unit)),
            whole((PAIR, msg_rows, unit)),
            at(TOP, width, 0),
            at(TOP, bcw, 0),
            at(TOP, bcw, 0),
        ],
        [
            sds((PAIR, msg_rows, unit), BF16),
            sds((PAIR, msg_rows, unit), BF16),
            sds((TOP, inner), BF16),
            sds((TOP, GROUPS * STATE), BF16),
            sds((TOP, GROUPS * STATE), BF16),
        ],
        scratch=[pltpu.VMEM((8 + TOP, width), F32)],
        nbytes=2 * 2**20,
    )(
        xc,
        bc,
        x_in,
        bc_in,
        bc_in,
        rim,
        rim,
        rim,
        conv_cache,
        conv_cache,
        conv_cache,
        conv_weight,
        conv_weight,
        conv_weight,
        bias2,
        bias2,
        bias2,
        tail,
        dec,
    )

    message = sds((msg_rows, unit), BF16)
    part = swap(send, 1)
    send_y, own = plain_call(core_kernel, (message, message), keep, part)
    recv = swap(send_y, 2)
    total = plain_call(functools.partial(total_kernel, bit=2), message, own, recv)
    pre = None
    bit = 4
    pre_shape = (sds((state_rows, unit), F32), sds((8, unit), F32))
    while 2 * bit < devices:
        other = swap(total, 2 * bit - 4)
        if pre is None:
            total, *pre = plain_call(
                functools.partial(start_kernel, bit=bit), (message,) + pre_shape, total, other
            )
        else:
            total, *pre = plain_call(
                functools.partial(prefix_kernel, bit=bit), (message,) + pre_shape, total, other, *pre
            )
        bit *= 2
    if pre is None:
        pre = [jnp.zeros((state_rows, unit), F32), jnp.ones((8, unit), F32)]
    other = swap(total, 2 * bit - 4)
    quarter = index % (2 * PAIR)
    cache = cache_state.reshape(steps, 2 * PAIR, unit, STATE)
    cache = lax.dynamic_index_in_dim(cache, quarter, 1, keepdims=False)
    cache = cache.transpose(0, 2, 1).reshape(state_rows, unit)
    state_out = sds((state_rows, unit), BF16)
    send_y, stay, final = plain_call(
        functools.partial(enter_kernel, bit=bit),
        (state_out, state_out, sds((state_rows, unit), F32)),
        total,
        other,
        *pre,
        cache,
        own,
        recv,
    )
    recv_y = swap(send_y, 2)
    half = sds((PAIR, state_rows, unit), BF16)
    send_c, enter_own = plain_call(chip_kernel, (half, half), stay, recv_y, keep, part)
    enter_recv = swap(send_c, 1)

    diag = grid_call(
        functools.partial(diag_kernel, head_dim=head_dim, first=0),
        (steps,),
        [
            at(rows, width, 0),
            at(TOP, width, 0),
            at(rows, bcw, 0),
            at(TOP, bcw, 0),
            at(rows, bcw, 0),
            at(TOP, bcw, 0),
            whole((rows, heads)),
            pl.BlockSpec((per_step, rows), lambda i: (i, 0)),
            at(1, width, 0),
        ],
        at(rows, width, 0),
        sds((rows, inner), F32),
        nbytes=8 * 2**20,
    )(xc, xfix, bc, bfix, cc, cfix, cum, row, jnp.repeat(d_skip, head_dim).reshape(1, -1))

    def mid(shape):
        return pl.BlockSpec(shape, lambda i: (0, i, 0))

    mixed = grid_call(
        functools.partial(out_kernel, head_dim=head_dim),
        (steps,),
        [
            smem,
            at(rows, width, 0),
            at(rows, bcw, 0),
            at(TOP, bcw, 0),
            lead((rows, 2 * per_step)),
            mid((PAIR, STATE, unit)),
            mid((PAIR, STATE, unit)),
            at(rows, width, 0),
            at(1, width, 0),
        ],
        at(rows, width, 0),
        sds((rows, inner), BF16),
        nbytes=4 * 2**20,
    )(lengths, diag, cc, cfix, ecum, enter_own, enter_recv, z_in, norm_gain.reshape(1, -1))

    final = final.reshape(steps, STATE, unit)
    if share * head_dim == unit and devices == 2 * PAIR * steps:
        mine = lax.dynamic_index_in_dim(final, index // (2 * PAIR), 0, keepdims=False)
        mine = mine.T.reshape(share, head_dim, STATE)
    else:
        around = [[4 * i + j for j in range(4)] for i in range(devices // 4)]
        every = lax.all_gather(final, SEQ, axis=1, axis_index_groups=around)
        every = every.reshape(steps * 2 * PAIR, STATE, unit).transpose(0, 2, 1)
        every = every.reshape(heads, head_dim, STATE)
        mine = lax.dynamic_slice_in_dim(every, index * share, share, 0)
    return (mixed, mine)


def solution(mesh):
    in_specs = (
        P(("groups", "seq"), None),
        P(("groups", "seq"), None),
        P(("groups", "seq"), None),
        P(("groups", "seq"), None),
        P(),
        P(),
        P(),
        P(),
        P(),
        P(),
        P("groups", None),
        P("groups", None, None),
        P("groups"),
    )
    out_specs = (P(("groups", "seq"), None), P(("groups", "seq"), None, None))
    return jax.shard_map(body, mesh=mesh, in_specs=in_specs, out_specs=out_specs, check_vma=False)
```

time: 289 us -> 68.3 us (0.24)
  the two profiles are of different devices: /device:TPU:9 before, /device:TPU:0 now
where the time goes in v1:
time: 68.3 us; the launch traced here: 67.1 us
  local copies, waits for them, and re-layouts  27.4 us (40%)
  Pallas kernels  14 us (20%)
  waiting for transfers between devices  13.8 us (20%)
  starting transfers between devices  10.4 us (15%)
  between operations  1.47 us (2%)
    unnamed x53, local copies, waits for them, and re-layouts  20.9 us
    ppermute x6, waiting for transfers between devices, swap(): return lax.ppermute(value, SEQ, [(i, i ^ mask) for i in devices])  13.8 us
    ppermute x6, starting transfers between devices, swap(): return lax.ppermute(value, SEQ, [(i, i ^ mask) for i in devices])  9.91 us
    pallas_call x1, Pallas kernels, body(): grid_call(functools.partial(out_kernel, head_dim=head_dim), (steps,), [sm...  4.17 us
    pallas_call x1, Pallas kernels, body(): grid_call(functools.partial(diag_kernel, head_dim=head_dim, first=0), (st...  4.13 us
    dynamic_slice x2, local copies, waits for them, and re-layouts, body(): cache = lax.dynamic_index_in_dim(cache, quarter, 1, keepdims=False)  3.1 us
    pallas_call x1, Pallas kernels, body(): grid_call(functools.partial(conv_kernel, heads=heads, head_dim=head_dim),...  2.48 us
    pallas_call x1, Pallas kernels, body(): grid_call(functools.partial(local_kernel, head_dim=head_dim), (steps,), [...  1.89 us
  transfers between devices with their start and end apart: 7, of which 4 were waited for; matrix products, arithmetic and copies ran while one was open for 13% of the time, Pallas kernels for 10%

profile of v1, /device:TPU:0, one launch (start us, length us, event | category | flops | bytes accessed | tf_op | source)
XLA Modules:
  0.0 67.1 jit_solution(3145986736266864766)
XLA Ops:
  0.7 0.9 %slice.6 = bf16[3,4096]{1,0:T(4,128)(2,1)S(1)} slice(bf16[128,4096]{1,0:T(8,128)(2,1)} %xtop_ref.1), slice={[125:128], [0:4096]} | slice | bytes 49152 | tf_op jit(solution)/shard_map/slice | solution.py:445
  1.5 0.7 %slice.7 = bf16[3,1024]{1,0:T(4,128)(2,1)S(1)} slice(bf16[128,1024]{1,0:T(8,128)(2,1)} %ctop_ref.1), slice={[125:128], [0:1024]} | slice | bytes 12288 | tf_op jit(solution)/shard_map/slice | solution.py:445
  2.3 0.5 collective-permute-start
  3.5 1.2 %copy-done = bf16[128,4096]{1,0:T(8,128)(2,1)S(1)} copy-done((bf16[128,4096]{1,0:T(8,128)(2,1)S(1)}, bf16[128,4096]{1,0:T(8,128)(2,1)}, u32[]{:S(2)}) %copy-start) | copy-done | bytes 1048600
  4.7 0.9 %copy-done.1 = bf16[128,1024]{1,0:T(8,128)(2,1)S(1)} copy-done((bf16[128,1024]{1,0:T(8,128)(2,1)S(1)}, bf16[128,1024]{1,0:T(8,128)(2,1)}, u32[]{:S(2)}) %copy-start.1) | copy-done | bytes 262168
  5.6 0.9 %copy-done.2 = f32[4,5120]{1,0:T(4,128)S(1)} copy-done((f32[4,5120]{1,0:T(4,128)S(1)}, f32[4,5120]{1,0:T(4,128)}, u32[]{:S(2)}) %copy-start.2) | copy-done | bytes 81944
  6.5 0.7 %copy-done.5 = f32[5120]{0:T(1024)S(1)} copy-done((f32[5120]{0:T(1024)S(1)}, f32[5120]{0:T(1024)}, u32[]{:S(2)}) %copy-start.5) | copy-done | bytes 20504
  7.3 0.8 %copy-done.18 = bf16[128,128]{1,0:T(8,128)(2,1)S(1)} copy-done((bf16[128,128]{1,0:T(8,128)(2,1)S(1)}, bf16[128,128]{1,0:T(8,128)(2,1)}, u32[]{:S(2)}) %copy-start.18) | copy-done | bytes 32792
  8.0 0.7 copy-done.23
  8.7 0.7 copy-done.24
  9.3 2.5 %shard_map.140 = (bf16[128,4096]{1,0:T(8,128)(2,1)S(1)}, bf16[128,512]{1,0:T(8,128)(2,1)S(1)}, bf16[128,512]{1,0:T(8,128)(2,1)S(1)}, f32[128,128]{1,0:T(8,128)S(...) custom-call(s32[1]{0:T(128)S(6)} %copy.20.len_ref, ...), custom_call_target="tpu_custom_call" | custom-call | bytes 4194304 | tf_op jit(solution)/shard_map/pallas_call | solution.py:456
  11.8 0.7 copy-done.9
  12.5 0.6 copy-done.11
  13.1 0.6 copy-done.13
  13.7 1.9 %shard_map.141 = (bf16[2,272,256]{2,1,0:T(8,128)(2,1)S(1)}, bf16[2,272,256]{2,1,0:T(8,128)(2,1)S(1)}, bf16[16,4096]{1,0:T(8,128)(2,1)S(1)}, bf16[16,512]{1,0:T(8,128)(2,1)S(1)}, bf16[16,512]{1,0:T(8,128)(2,1)S(1)}) custom-call(bf16[128,4096]{1,0:T(8,128)(2,1)S(1)} %get-tuple-element.25.xc_ref, bf16[128,512]{1,0:T(8,128)(2,1)S(1)} %get-tuple-element.26.bc_ref.b_ref, ...), custom_call_target="tpu_custom_call" | custom-call | bytes 2097152 | tf_op jit(solution)/shard_map/pallas_call | solution.py:501
  15.6 2.7 %collective-permute-start.1 = (bf16[2,272,256]{2,1,0:T(8,128)(2,1)S(1)}, bf16[2,272,256]{2,1,0:T(8,128)(2,1)S(1)}, u32[]{:S(2)}, u32[]{:S(2)}) collective-permute-start(bf16[2,272,256]{2,1,0:T(8,128)(2,1)S(1)} %get-tuple-element.37), channel_id=1, source_target_pairs={{0,1},{1,0},{2,3},{3,2},{4,5},{5,4},{6,7},{7,6},{8,9},{9,8},{10,11... | collective-permute-start | bytes 835592 | tf_op jit(solution)/shard_map/ppermute | solution.py:394
  18.3 1.2 %collective-permute-done.1.recv_ref.part_ref = bf16[2,272,256]{2,1,0:T(8,128)(2,1)S(1)} collective-permute-done((bf16[2,272,256]{2,1,0:T(8,128)(2,1)S(1)}, bf16[2,272,256]{2,1,0:T(8,128)(2,1)S(1)}, u32[]{:S(2)}, u32[]{:S(2)}) %collective-permute-start.1) | collective-permute-done | bytes 278560 | tf_op jit(solution)/shard_map/ppermute | solution.py:394
  19.5 0.1 shard_map.143
  19.6 1.6 %collective-permute-start.2 = (bf16[272,256]{1,0:T(8,128)(2,1)S(1)}, bf16[272,256]{1,0:T(8,128)(2,1)S(1)}, u32[]{:S(2)}, u32[]{:S(2)}) collective-permute-start(bf16[272,256]{1,0:T(8,128)(2,1)S(1)} %get-tuple-element.39), channel_id=1, source_target_pairs={{0,2},{1,3},{2,0},{3,1},{4,6},{5,7},{6,4},{7,5},{8,10},{9,11},{10,... | collective-permute-start | bytes 417800 | tf_op jit(solution)/shard_map/ppermute | solution.py:394
  21.2 4.4 %collective-permute-done.2.other_ref.recv_ref = bf16[272,256]{1,0:T(8,128)(2,1)S(1)} collective-permute-done((bf16[272,256]{1,0:T(8,128)(2,1)S(1)}, bf16[272,256]{1,0:T(8,128)(2,1)S(1)}, u32[]{:S(2)}, u32[]{:S(2)}) %collective-permute-start.2) | collective-permute-done | bytes 139296 | tf_op jit(solution)/shard_map/ppermute | solution.py:394
  25.7 1.6 %collective-permute-start.3 = (bf16[272,256]{1,0:T(8,128)(2,1)S(1)}, bf16[272,256]{1,0:T(8,128)(2,1)S(1)}, u32[]{:S(2)}, u32[]{:S(2)}) collective-permute-start(bf16[272,256]{1,0:T(8,128)(2,1)S(1)} %shard_map.144.mine_ref), channel_id=1, source_target_pairs={{0,4},{1,5},{2,6},{3,7},{4,0},{5,1},{6,2},{7,3},{8,12},{9,13},{10,... | collective-permute-start | bytes 417800 | tf_op jit(solution)/shard_map/ppermute | solution.py:394
  27.4 3.6 %collective-permute-done.3.other_ref = bf16[272,256]{1,0:T(8,128)(2,1)S(1)} collective-permute-done((bf16[272,256]{1,0:T(8,128)(2,1)S(1)}, bf16[272,256]{1,0:T(8,128)(2,1)S(1)}, u32[]{:S(2)}, u32[]{:S(2)}) %collective-permute-start.3) | collective-permute-done | bytes 139296 | tf_op jit(solution)/shard_map/ppermute | solution.py:394
  30.9 0.1 shard_map.145
  31.0 3.7 %collective-permute-start.4 = (bf16[272,256]{1,0:T(8,128)(2,1)S(1)}, bf16[272,256]{1,0:T(8,128)(2,1)S(1)}, u32[]{:S(2)}, u32[]{:S(2)}) collective-permute-start(bf16[272,256]{1,0:T(8,128)(2,1)S(1)} %get-tuple-element.40.mine_ref), channel_id=1, source_target_pairs={{0,12},{1,13},{2,14},{3,15},{4,8},{5,9},{6,10},{7,11},{8,4},{9,5},... | collective-permute-start | bytes 417800 | tf_op jit(solution)/shard_map/ppermute | solution.py:394
  34.7 4.1 %copy.17 = f32[128,32,64]{2,1,0:T(8,128)} copy(f32[128,32,64]{0,2,1:T(8,128)} %param.24) | data formatting | bytes 2097152 | tf_op args[11]
  38.8 1.9 %constant_dynamic-slice_fusion = f32[4,1,256,64]{3,2,1,0:T(8,128)} fusion(f32[4,4,256,64]{3,2,1,0:T(8,128)} %bitcast.27, s32[]{:T(128)S(6)} %select_n.20), kind=kLoop, calls=%fused_computation.2 | loop fusion | bytes 524292 | tf_op jit(solution)/shard_map/jit(dynamic_index_in_dim)/dynamic_slice | solution.py:572
  40.7 1.2 %copy.18 = f32[4,1,256,64]{2,3,1,0:T(8,128)S(1)} copy(f32[4,1,256,64]{3,2,1,0:T(8,128)} %constant_dynamic-slice_fusion) | data formatting | bytes 524288 | tf_op jit(solution)/shard_map/jit(dynamic_index_in_dim)/dynamic_slice | solution.py:572
  41.9 0.2 shard_map.146
  42.1 0.7 %copy-done.21 = f32[256,256]{1,0:T(8,128)} copy-done((f32[256,256]{1,0:T(8,128)}, f32[256,256]{1,0:T(8,128)S(1)}, u32[]{:S(2)}) %copy-start.21) | copy-done | bytes 262168
  42.8 0.3 collective-permute-start.5
  43.1 4.7 %collective-permute-done.5.recv_ref = bf16[256,256]{1,0:T(8,128)(2,1)S(1)} collective-permute-done((bf16[256,256]{1,0:T(8,128)(2,1)S(1)}, bf16[256,256]{1,0:T(8,128)(2,1)S(1)}, u32[]{:S(2)}, u32[]{:S(2)}) %collective-permute-start.5) | collective-permute-done | bytes 131104 | tf_op jit(solution)/shard_map/ppermute | solution.py:394
  47.8 0.8 %shard_map.147 = (bf16[2,256,256]{2,1,0:T(8,128)(2,1)}, bf16[2,256,256]{2,1,0:T(8,128)(2,1)S(1)}) custom-call(bf16[256,256]{1,0:T(8,128)(2,1)S(1)} %get-tuple-element.43.stay_ref, bf16[256,256]{1,0:T(8,128)(2,1)S(1)} %collective-permute-done.5.recv_ref, bf16[2,272,256]{2,1,0:T(8,128)(2,1)S(1)} %get-tuple-element.36.keep_ref, ...), custom_call_target="tpu_custom_call" | custom-call | bytes 1048576 | tf_op jit(solution)/shard_map/pallas_call | solution.py:402
  48.6 0.7 %copy-done.7 = bf16[2,256,256]{2,1,0:T(8,128)(2,1)} copy-done((bf16[2,256,256]{2,1,0:T(8,128)(2,1)}, bf16[2,256,256]{2,1,0:T(8,128)(2,1)S(1)}, u32[]{:S(2)}) %copy-start.7) | copy-done | bytes 262168
  49.3 0.1 broadcast_in_dim.3
  49.4 0.1 reshape_reshape.3.skip_ref
  49.5 0.8 %copy-done.12 = f32[128,128]{1,0:T(8,128)S(1)} copy-done((f32[128,128]{1,0:T(8,128)S(1)}, f32[128,128]{1,0:T(8,128)}, u32[]{:S(2)}) %copy-start.12) | copy-done | bytes 65560
  50.4 0.8 %copy-done.14 = f32[128,128]{1,0:T(8,128)S(1)} copy-done((f32[128,128]{1,0:T(8,128)S(1)}, f32[128,128]{1,0:T(8,128)}, u32[]{:S(2)}) %copy-start.14) | copy-done | bytes 65560
  51.2 0.7 %copy-done.16 = bf16[16,512]{1,0:T(8,128)(2,1)S(1)} copy-done((bf16[16,512]{1,0:T(8,128)(2,1)S(1)}, bf16[16,512]{1,0:T(8,128)(2,1)}, u32[]{:S(2)}) %copy-start.16) | copy-done | bytes 16408
  51.9 0.7 %copy-done.20 = bf16[16,512]{1,0:T(8,128)(2,1)S(1)} copy-done((bf16[16,512]{1,0:T(8,128)(2,1)S(1)}, bf16[16,512]{1,0:T(8,128)(2,1)}, u32[]{:S(2)}) %copy-start.20) | copy-done | bytes 16408
  52.6 4.1 %shard_map.142.diag_ref = f32[128,4096]{1,0:T(8,128)S(1)} custom-call(bf16[128,4096]{1,0:T(8,128)(2,1)S(1)} %get-tuple-element.25.xc_ref, bf16[16,4096]{1,0:T(8,128)(2,1)S(1)} %get-tuple-element.29.xfix_ref, bf16[128,512]{1,0:T(8,128)(2,1)S(1)} %get-tuple-element.26.bc_ref.b_ref, bf16[16,512]{1,0:T(8,128)(2,1)S(1)} %copy-done.20, ...), custom_call_target="tpu_custom_call" | custom-call | bytes 8388608 | tf_op jit(solution)/shard_map/pallas_call | solution.py:590
  56.8 0.9 %dynamic-slice_bitcast_fusion = f32[256,64]{0,1:T(8,128)S(1)} fusion(f32[4,64,256]{2,1,0:T(8,128)} %bitcast.23, s32[]{:T(128)S(6)} %select_n.22), kind=kLoop, calls=%fused_computation | loop fusion | bytes 131076 | tf_op jit(solution)/shard_map/transpose | solution.py:634
  57.6 0.8 %copy.19 = f32[256,64]{1,0:T(8,128)} copy(f32[256,64]{0,1:T(8,128)S(1)} %dynamic-slice_bitcast_fusion) | data formatting | bytes 131072 | tf_op jit(solution)/shard_map/transpose | solution.py:634
  58.4 1.2 %copy-done.4 = bf16[128,4096]{1,0:T(8,128)(2,1)S(1)} copy-done((bf16[128,4096]{1,0:T(8,128)(2,1)S(1)}, bf16[128,4096]{1,0:T(8,128)(2,1)}, u32[]{:S(2)}) %copy-start.4) | copy-done | bytes 1048600
  59.6 0.9 %copy-done.8 = bf16[2,256,256]{2,1,0:T(8,128)(2,1)S(1)} copy-done((bf16[2,256,256]{2,1,0:T(8,128)(2,1)S(1)}, bf16[2,256,256]{2,1,0:T(8,128)(2,1)}, u32[]{:S(2)}) %copy-start.8) | copy-done | bytes 262168
  60.6 0.9 %copy-done.10 = bf16[4,128,64]{2,1,0:T(8,128)(2,1)S(1)} copy-done((bf16[4,128,64]{2,1,0:T(8,128)(2,1)S(1)}, bf16[4,128,64]{2,1,0:T(8,128)(2,1)}, u32[]{:S(2)}) %copy-start.10) | copy-done | bytes 65560
  61.5 0.7 %copy-done.17 = bf16[16,512]{1,0:T(8,128)(2,1)S(1)} copy-done((bf16[16,512]{1,0:T(8,128)(2,1)S(1)}, bf16[16,512]{1,0:T(8,128)(2,1)}, u32[]{:S(2)}) %copy-start.17) | copy-done | bytes 16408
  62.2 0.7 %copy-done.22 = f32[4096]{0:T(1024)S(1)} copy-done((f32[4096]{0:T(1024)S(1)}, f32[4096]{0:T(1024)}, u32[]{:S(2)}) %copy-start.22) | copy-done | bytes 16408
  62.9 4.2 %shard_map.148 = bf16[128,4096]{1,0:T(8,128)(2,1)} custom-call(s32[1]{0:T(128)S(6)} %copy.20.len_ref, f32[128,4096]{1,0:T(8,128)S(1)} %shard_map.142.diag_ref, bf16[128,512]{1,0:T(8,128)(2,1)S(1)} %get-tuple-element.31.c_ref, bf16[16,512]{1,0:T(8,128)(2,1)S(1)} %copy-done.17, bf16[4,128,64]{2,1,0:T(8,128)(2,1)S(1)} %copy-done.10, ...), custom_call_target="tpu_custom_call" | custom-call | bytes 4194304 | tf_op jit(solution)/shard_map/pallas_call | solution.py:612
  (37 shorter events, 0.2 us)
Async XLA Ops:
  0.6 13.1 %copy-start.3 = (f32[4,5120]{1,0:T(4,128)S(1)}, f32[4,5120]{1,0:T(4,128)}, u32[]{:S(2)}) copy-start(f32[4,5120]{1,0:T(4,128)} %wc_ref.3) | copy-start | bytes 245764
  0.6 13.1 %copy-start.6 = (bf16[3,5120]{1,0:T(4,128)(2,1)S(1)}, bf16[3,5120]{1,0:T(4,128)(2,1)}, u32[]{:S(2)}) copy-start(bf16[3,5120]{1,0:T(4,128)(2,1)} %ccache_ref.1) | copy-start | bytes 92164
  2.3 11.4 %collective-permute-start = (bf16[3,5120]{1,0:T(4,128)(2,1)S(1)}, bf16[3,5120]{1,0:T(4,128)(2,1)S(1)}, u32[]{:S(2)}, u32[]{:S(2)}) collective-permute-start(bf16[3,5120]{1,0:T(4,128)(2,1)S(1)} %pad_maximum_fusion), channel_id=1, source_target_pairs={{0,1},{1,2},{2,3},{3,4},{4,5},{5,6},{6,7},{7,8},{8,9},{9,10},{10,1... | collective-permute-start | bytes 92168 | tf_op jit(solution)/shard_map/ppermute | solution.py:446
  3.5 1.2 %copy-start = (bf16[128,4096]{1,0:T(8,128)(2,1)S(1)}, bf16[128,4096]{1,0:T(8,128)(2,1)}, u32[]{:S(2)}) copy-start(bf16[128,4096]{1,0:T(8,128)(2,1)} %xtop_ref.1) | copy-start | bytes 3145732
  4.7 0.9 %copy-start.1 = (bf16[128,1024]{1,0:T(8,128)(2,1)S(1)}, bf16[128,1024]{1,0:T(8,128)(2,1)}, u32[]{:S(2)}) copy-start(bf16[128,1024]{1,0:T(8,128)(2,1)} %ctop_ref.1) | copy-start | bytes 786436
  5.6 0.9 %copy-start.2 = (f32[4,5120]{1,0:T(4,128)S(1)}, f32[4,5120]{1,0:T(4,128)}, u32[]{:S(2)}) copy-start(f32[4,5120]{1,0:T(4,128)} %wc_ref.3) | copy-start | bytes 245764
  6.5 0.7 %copy-start.5 = (f32[5120]{0:T(1024)S(1)}, f32[5120]{0:T(1024)}, u32[]{:S(2)}) copy-start(f32[5120]{0:T(1024)} %param.18) | copy-start | bytes 61444
  7.2 0.8 %copy-start.18 = (bf16[128,128]{1,0:T(8,128)(2,1)S(1)}, bf16[128,128]{1,0:T(8,128)(2,1)}, u32[]{:S(2)}) copy-start(bf16[128,128]{1,0:T(8,128)(2,1)} %dt_ref.1) | copy-start | bytes 98308
  8.0 0.7 copy-start.23
  8.7 0.7 copy-start.24
  11.8 0.7 copy-start.9
  12.5 0.6 copy-start.11
  13.1 0.6 copy-start.13
  15.6 15.4 %copy-start.15 = (bf16[16,512]{1,0:T(8,128)(2,1)}, bf16[16,512]{1,0:T(8,128)(2,1)S(1)}, u32[]{:S(2)}) copy-start(bf16[16,512]{1,0:T(8,128)(2,1)S(1)} %get-tuple-element.32.cfix_ref) | copy-start | bytes 49156
  15.6 15.4 %copy-start.19 = (bf16[16,512]{1,0:T(8,128)(2,1)}, bf16[16,512]{1,0:T(8,128)(2,1)S(1)}, u32[]{:S(2)}) copy-start(bf16[16,512]{1,0:T(8,128)(2,1)S(1)} %get-tuple-element.30.bfix_ref) | copy-start | bytes 49156
  15.6 3.9 %collective-permute-start.1 = (bf16[2,272,256]{2,1,0:T(8,128)(2,1)S(1)}, bf16[2,272,256]{2,1,0:T(8,128)(2,1)S(1)}, u32[]{:S(2)}, u32[]{:S(2)}) collective-permute-start(bf16[2,272,256]{2,1,0:T(8,128)(2,1)S(1)} %get-tuple-element.37), channel_id=1, source_target_pairs={{0,1},{1,0},{2,3},{3,2},{4,5},{5,4},{6,7},{7,6},{8,9},{9,8},{10,11... | collective-permute-start | bytes 835592 | tf_op jit(solution)/shard_map/ppermute | solution.py:394
  19.6 6.0 %collective-permute-start.2 = (bf16[272,256]{1,0:T(8,128)(2,1)S(1)}, bf16[272,256]{1,0:T(8,128)(2,1)S(1)}, u32[]{:S(2)}, u32[]{:S(2)}) collective-permute-start(bf16[272,256]{1,0:T(8,128)(2,1)S(1)} %get-tuple-element.39), channel_id=1, source_target_pairs={{0,2},{1,3},{2,0},{3,1},{4,6},{5,7},{6,4},{7,5},{8,10},{9,11},{10,... | collective-permute-start | bytes 417800 | tf_op jit(solution)/shard_map/ppermute | solution.py:394
  25.7 5.2 %collective-permute-start.3 = (bf16[272,256]{1,0:T(8,128)(2,1)S(1)}, bf16[272,256]{1,0:T(8,128)(2,1)S(1)}, u32[]{:S(2)}, u32[]{:S(2)}) collective-permute-start(bf16[272,256]{1,0:T(8,128)(2,1)S(1)} %shard_map.144.mine_ref), channel_id=1, source_target_pairs={{0,4},{1,5},{2,6},{3,7},{4,0},{5,1},{6,2},{7,3},{8,12},{9,13},{10,... | collective-permute-start | bytes 417800 | tf_op jit(solution)/shard_map/ppermute | solution.py:394
  31.0 10.8 %collective-permute-start.4 = (bf16[272,256]{1,0:T(8,128)(2,1)S(1)}, bf16[272,256]{1,0:T(8,128)(2,1)S(1)}, u32[]{:S(2)}, u32[]{:S(2)}) collective-permute-start(bf16[272,256]{1,0:T(8,128)(2,1)S(1)} %get-tuple-element.40.mine_ref), channel_id=1, source_target_pairs={{0,12},{1,13},{2,14},{3,15},{4,8},{5,9},{6,10},{7,11},{8,4},{9,5},... | collective-permute-start | bytes 417800 | tf_op jit(solution)/shard_map/ppermute | solution.py:394
  38.8 10.6 %copy-start.25 = (f32[128]{0:T(128)S(1)}, f32[128]{0:T(128)}, u32[]{:S(2)}) copy-start(f32[128]{0:T(128)} %param.21) | copy-start | bytes 1540
  42.1 0.7 %copy-start.21 = (f32[256,256]{1,0:T(8,128)}, f32[256,256]{1,0:T(8,128)S(1)}, u32[]{:S(2)}) copy-start(f32[256,256]{1,0:T(8,128)S(1)} %get-tuple-element.47) | copy-start | bytes 786436
  42.8 5.0 %collective-permute-start.5 = (bf16[256,256]{1,0:T(8,128)(2,1)S(1)}, bf16[256,256]{1,0:T(8,128)(2,1)S(1)}, u32[]{:S(2)}, u32[]{:S(2)}) collective-permute-start(bf16[256,256]{1,0:T(8,128)(2,1)S(1)} %get-tuple-element.44), channel_id=1, source_target_pairs={{0,2},{1,3},{2,0},{3,1},{4,6},{5,7},{6,4},{7,5},{8,10},{9,11},{10,... | collective-permute-start | bytes 393224 | tf_op jit(solution)/shard_map/ppermute | solution.py:394
  48.6 0.7 %copy-start.7 = (bf16[2,256,256]{2,1,0:T(8,128)(2,1)}, bf16[2,256,256]{2,1,0:T(8,128)(2,1)S(1)}, u32[]{:S(2)}) copy-start(bf16[2,256,256]{2,1,0:T(8,128)(2,1)S(1)} %get-tuple-element.45.own_ref) | copy-start | bytes 786436
  49.3 9.1 %collective-permute-start.6 = (bf16[2,256,256]{2,1,0:T(8,128)(2,1)}, bf16[2,256,256]{2,1,0:T(8,128)(2,1)}, u32[]{:S(2)}, u32[]{:S(2)}) collective-permute-start(bf16[2,256,256]{2,1,0:T(8,128)(2,1)} %get-tuple-element.46), channel_id=1, source_target_pairs={{0,1},{1,0},{2,3},{3,2},{4,5},{5,4},{6,7},{7,6},{8,9},{9,8},{10,11... | collective-permute-start | bytes 786440 | tf_op jit(solution)/shard_map/ppermute | solution.py:394
  49.5 0.8 %copy-start.12 = (f32[128,128]{1,0:T(8,128)S(1)}, f32[128,128]{1,0:T(8,128)}, u32[]{:S(2)}) copy-start(f32[128,128]{1,0:T(8,128)} %copy-done.11) | copy-start | bytes 196612
  50.4 0.8 %copy-start.14 = (f32[128,128]{1,0:T(8,128)S(1)}, f32[128,128]{1,0:T(8,128)}, u32[]{:S(2)}) copy-start(f32[128,128]{1,0:T(8,128)} %copy-done.13) | copy-start | bytes 196612
  51.2 0.7 %copy-start.16 = (bf16[16,512]{1,0:T(8,128)(2,1)S(1)}, bf16[16,512]{1,0:T(8,128)(2,1)}, u32[]{:S(2)}) copy-start(bf16[16,512]{1,0:T(8,128)(2,1)} %copy-done.15) | copy-start | bytes 49156
  51.9 0.7 %copy-start.20 = (bf16[16,512]{1,0:T(8,128)(2,1)S(1)}, bf16[16,512]{1,0:T(8,128)(2,1)}, u32[]{:S(2)}) copy-start(bf16[16,512]{1,0:T(8,128)(2,1)} %copy-done.19) | copy-start | bytes 49156
  58.4 1.2 %copy-start.4 = (bf16[128,4096]{1,0:T(8,128)(2,1)S(1)}, bf16[128,4096]{1,0:T(8,128)(2,1)}, u32[]{:S(2)}) copy-start(bf16[128,4096]{1,0:T(8,128)(2,1)} %z_ref.1) | copy-start | bytes 3145732
  59.6 0.9 %copy-start.8 = (bf16[2,256,256]{2,1,0:T(8,128)(2,1)S(1)}, bf16[2,256,256]{2,1,0:T(8,128)(2,1)}, u32[]{:S(2)}) copy-start(bf16[2,256,256]{2,1,0:T(8,128)(2,1)} %copy-done.7) | copy-start | bytes 786436
  60.6 0.9 %copy-start.10 = (bf16[4,128,64]{2,1,0:T(8,128)(2,1)S(1)}, bf16[4,128,64]{2,1,0:T(8,128)(2,1)}, u32[]{:S(2)}) copy-start(bf16[4,128,64]{2,1,0:T(8,128)(2,1)} %copy-done.9) | copy-start | bytes 196612
  61.5 0.7 %copy-start.17 = (bf16[16,512]{1,0:T(8,128)(2,1)S(1)}, bf16[16,512]{1,0:T(8,128)(2,1)}, u32[]{:S(2)}) copy-start(bf16[16,512]{1,0:T(8,128)(2,1)} %copy-done.15) | copy-start | bytes 49156
  62.2 0.7 %copy-start.22 = (f32[4096]{0:T(1024)S(1)}, f32[4096]{0:T(1024)}, u32[]{:S(2)}) copy-start(f32[4096]{0:T(1024)} %param.22) | copy-start | bytes 49156

commit v2 on v1

v2 whole, which is shorter than its diff:
```python
import functools

import jax
import jax.numpy as jnp
from jax import lax
from jax.experimental import pallas as pl
from jax.experimental.pallas import tpu as pltpu
from jax.sharding import PartitionSpec as P

STATE = 64
GROUPS = 8
CONV_W = 4
RIM = CONV_W - 1
LOG2E = 1.4426950408889634
BF16 = jnp.bfloat16
F32 = jnp.float32
HI = lax.Precision.HIGHEST
SEQ = "seq"
PAIR = 2
TOP = 16


def silu(v):
    half = 0.5 * v
    return half + half * jnp.tanh(half)


def split2(v):
    hi = v.astype(BF16)
    return hi, (v - hi.astype(F32)).astype(BF16)


def grid_call(body, grid, in_specs, out_specs, out_shape, scratch=(), flops=0, nbytes=0, vmem=24):
    return pl.pallas_call(
        body,
        grid=grid,
        in_specs=in_specs,
        out_specs=out_specs,
        out_shape=out_shape,
        scratch_shapes=list(scratch),
        compiler_params=pltpu.CompilerParams(vmem_limit_bytes=vmem * 2**20),
        cost_estimate=pl.CostEstimate(flops=flops, bytes_accessed=nbytes, transcendentals=0),
    )


def rim_kernel(x_ref, bc_ref, out_ref, x_rows, bc_rows, sems):
    rows, inner = x_ref.shape
    copies = [
        pltpu.make_async_copy(x_ref.at[pl.ds(rows - TOP, TOP), :], x_rows, sems.at[0]),
        pltpu.make_async_copy(bc_ref.at[pl.ds(rows - TOP, TOP), :], bc_rows, sems.at[1]),
    ]
    for copy in copies:
        copy.start()
    for copy in copies:
        copy.wait()
    out_ref[:, :inner] = x_rows[...].astype(F32)[TOP - RIM :, :].astype(BF16)
    out_ref[:, inner:] = bc_rows[...].astype(F32)[TOP - RIM :, :].astype(BF16)


def pack_decay(dec):
    hi, lo = split2(dec)
    return jnp.concatenate([hi.astype(F32), lo.astype(F32)], axis=0).astype(BF16)


def unpack_decay(rows):
    both = rows.astype(F32)
    return both[0:8] + both[8:16]


def conv_kernel(
    len_ref,
    x_ref,
    b_ref,
    c_ref,
    dt_ref,
    wx_ref,
    wb_ref,
    wc_ref,
    cx_ref,
    cb_ref,
    cc_ref,
    dtb_ref,
    alog_ref,
    after_ref,
    xo_ref,
    bo_ref,
    co_ref,
    prex_ref,
    preb_ref,
    prec_ref,
    cum_ref,
    row_ref,
    ecum_ref,
    dec_ref,
    top_ref,
    local_ref,
    ext,
    tails,
    scaled,
    *,
    heads,
    head_dim,
):
    step = pl.program_id(0)
    rows = x_ref.shape[0]
    per_step = heads // pl.num_programs(0)

    def conv(src, w, bias, cols):
        ext[8:, :] = src[:, cols].astype(F32)
        total = jnp.broadcast_to(bias[:, cols], (rows, 128))
        for k in range(CONV_W):
            total = total + ext[pl.ds(8 + k - RIM, rows), :] * w[k : k + 1, cols]
        return total[0:8], silu(total).astype(BF16)

    ext[0:8, :] = jnp.zeros((8, 128), F32)

    @pl.when(step == 0)
    def _():
        raw = dt_ref[...].astype(F32) + dtb_ref[...]
        soft = jnp.maximum(raw, 0.0) + jnp.log1p(jnp.exp(-jnp.abs(raw)))
        first = lax.axis_index(SEQ) * rows
        token = first + lax.broadcasted_iota(jnp.int32, (rows, heads), 0)
        dt = jnp.where(token < len_ref[0], soft, 0.0)
        rate = -jnp.exp(alog_ref[...]) * dt
        below = lax.broadcasted_iota(jnp.int32, (rows, rows), 0)
        across = lax.broadcasted_iota(jnp.int32, (rows, rows), 1)
        tri = (below >= across).astype(F32)
        cum = jnp.dot(tri, rate, precision=HI, preferred_element_type=F32)
        last = cum[rows - 1 : rows, :]
        tail = jnp.exp(last - cum) * dt
        ecum = jnp.exp(cum)
        cum_ref[...] = cum * LOG2E
        log_dt = jnp.where(dt > 0.0, jnp.log(jnp.maximum(dt, 1e-38)) * LOG2E, -1e30)
        row_ref[...] = (cum * LOG2E - log_dt).T
        tail_hi, tail_lo = split2(tail)
        ecum_hi, ecum_lo = split2(ecum)
        for i in range(heads // per_step):
            part = slice(i * per_step, (i + 1) * per_step)
            tails[i] = jnp.concatenate([tail_hi[:, part], tail_lo[:, part]], axis=1)
            ecum_ref[i] = jnp.concatenate([ecum_hi[:, part], ecum_lo[:, part]], axis=1)
        unit_heads = per_step // (2 * PAIR)
        unit_cols = unit_heads * head_dim
        owner = lax.broadcasted_iota(jnp.int32, (8, heads), 0)
        head = lax.broadcasted_iota(jnp.int32, (8, heads), 1)
        chosen = jnp.where(head // per_step == owner, jnp.exp(last), 0.0)
        head = lax.broadcasted_iota(jnp.int32, (heads, unit_cols), 0)
        lane = lax.broadcasted_iota(jnp.int32, (heads, unit_cols), 1)
        same = head % unit_heads == lane // head_dim
        for q in range(2 * PAIR):
            spread = jnp.where(same & ((head % per_step) // unit_heads == q), 1.0, 0.0)
            dec = jnp.dot(chosen, spread, precision=HI, preferred_element_type=F32)
            dec_ref[q] = pack_decay(dec)

    for src, w, bias, dst, pre in (
        (b_ref, wb_ref, cb_ref, bo_ref, preb_ref),
        (c_ref, wc_ref, cc_ref, co_ref, prec_ref),
    ):
        pre[...], dst[...] = conv(src, w, bias, slice(None))
    early = lax.broadcasted_iota(jnp.int32, (8, 128), 0) < RIM
    head = lax.broadcasted_iota(jnp.int32, (2 * per_step, 128), 0) % per_step
    lane = lax.broadcasted_iota(jnp.int32, (2 * per_step, 128), 1) // head_dim
    for j in range(x_ref.shape[1] // 128):
        cols = pl.ds(128 * j, 128)
        prex_ref[:, cols], xj = conv(x_ref, wx_ref, cx_ref, cols)
        xo_ref[:, cols] = xj
        spread = jnp.where(head == lane + j * (128 // head_dim), 1.0, 0.0).astype(BF16)
        tail = jnp.dot(tails[step], spread, preferred_element_type=F32)
        top_ref[:, cols] = jnp.where(early, tail[0:8], 0.0)
        tail = jnp.concatenate([jnp.where(early, 0.0, tail[0:8]), tail[8:]], axis=0)
        scaled[:, cols] = (xj.astype(F32) * tail).astype(BF16)
    b_turned = bo_ref[...].T
    group = x_ref.shape[1] // PAIR
    for y in range(PAIR):
        local_ref[y] = jnp.dot(
            b_turned[y * STATE : (y + 1) * STATE, :],
            scaled[:, y * group : (y + 1) * group],
            preferred_element_type=F32,
        )


def fix_kernel(
    rim_ref,
    cache_ref,
    w_ref,
    prex_ref,
    preb_ref,
    prec_ref,
    xc_ref,
    bc_ref,
    cc_ref,
    top_ref,
    local_ref,
    dec_ref,
    send_ref,
    keep_ref,
    xfix_ref,
    bfix_ref,
    cfix_ref,
    ext,
):
    device = lax.axis_index(SEQ)
    core = device % 2
    inner = xc_ref.shape[1]
    side = bc_ref.shape[1]
    ext[8:, :] = jnp.zeros((8, ext.shape[1]), F32)
    ext[8 - RIM : 8, :] = jnp.where(
        device == 0, cache_ref[...].astype(F32), rim_ref[...].astype(F32)
    )

    def fix(pre, old, dst, first, count):
        cols = pl.ds(first, count)
        total = pre[...]
        for k in range(RIM):
            total = total + ext[pl.ds(8 - RIM + k, 8), cols] * w_ref[k : k + 1, cols]
        fixed = silu(total)
        dst[...] = jnp.concatenate([fixed, old[0:TOP, :].astype(F32)[8:, :]], axis=0).astype(BF16)
        return fixed.astype(BF16).astype(F32)

    x_top = fix(prex_ref, xc_ref, xfix_ref, 0, inner)
    b_top = fix(preb_ref, bc_ref, bfix_ref, inner, side)
    fix(prec_ref, cc_ref, cfix_ref, inner + side, side)
    scaled = x_top * top_ref[...]
    scaled = jnp.concatenate([scaled, jnp.zeros_like(scaled)], axis=0).astype(BF16)
    b_top = jnp.concatenate([b_top, jnp.zeros_like(b_top)], axis=0)
    b_turned = b_top.T.astype(BF16)
    groups, _, width = local_ref.shape
    unit = width // 2
    for g in range(groups):
        extra = jnp.dot(
            b_turned[g * STATE : (g + 1) * STATE, :],
            scaled[:, g * width : (g + 1) * width],
            preferred_element_type=F32,
        )
        whole_state = local_ref[g] + extra
        low, high = whole_state[:, :unit], whole_state[:, unit:]
        where = pl.ds((g // PAIR) * STATE, STATE)
        send_ref[g % PAIR, where, :] = jnp.where(core == 0, high, low).astype(BF16)
        keep_ref[g % PAIR, where, :] = jnp.where(core == 0, low, high).astype(BF16)
    where = pl.ds(groups // PAIR * STATE, 16)
    for y in range(PAIR):
        send_ref[y, where, :] = dec_ref[2 * y + 1 - core]
        keep_ref[y, where, :] = dec_ref[2 * y + core]


def cache_kernel(state_ref, after_ref, out_ref, held, *, unit_heads):
    step = pl.program_id(0)
    channels, size, heads = state_ref.shape
    per_tile = 128 // unit_heads
    quarters = 2 * PAIR
    steps = heads // (quarters * unit_heads)
    quarter = lax.axis_index(SEQ) % quarters
    lane = lax.broadcasted_iota(jnp.int32, (size, 128), 1) // unit_heads
    for k in range(channels):
        channel = step * channels + k
        tile, place = channel // per_tile, channel % per_tile
        value = state_ref[k]
        for i in range(steps):
            start = (i * quarters + quarter) * unit_heads
            moved = pltpu.roll(value, (place * unit_heads - start + heads) % heads, axis=1)
            held[tile, i] = jnp.where(lane == place, moved, held[tile, i])

    @pl.when(step == pl.num_programs(0) - 1)
    def _():
        unit = out_ref.shape[1]
        dim = unit // unit_heads
        source = lax.broadcasted_iota(jnp.int32, (unit, unit), 0)
        target = lax.broadcasted_iota(jnp.int32, (unit, unit), 1)
        chosen = source == (target % dim) * unit_heads + target // dim
        order = jnp.where(chosen, 1.0, 0.0).astype(BF16)
        for i in range(steps):
            value = jnp.concatenate([held[t, i] for t in range(unit // 128)], axis=1)
            hi = value.astype(BF16)
            rest = value - hi.astype(F32)
            mid = rest.astype(BF16)
            low = (rest - mid.astype(F32)).astype(BF16)
            parts = jnp.dot(
                jnp.concatenate([hi, mid, low], axis=0), order, preferred_element_type=F32
            )
            out_ref[i * size : (i + 1) * size, :] = (
                parts[:size] + parts[size : 2 * size] + parts[2 * size :]
            )


def blocks_of(rows):
    return [(i, slice(i * STATE, (i + 1) * STATE)) for i in range(rows // STATE)]


def core_kernel(keep_ref, recv_ref, send_ref, own_ref):
    device = lax.axis_index(SEQ)
    core, side = device % 2, (device // 2) % 2
    rows = keep_ref.shape[1] - 16
    for out, pick in ((send_ref, 1 - side), (own_ref, side)):
        mine, other = keep_ref.at[pick], recv_ref.at[pick]
        join_totals(mine, other, core == 0, out, rows)


def join_totals(mine, other, mine_first, out, rows):
    d_mine = unpack_decay(mine[rows:, :])
    d_other = unpack_decay(other[rows:, :])
    d_later = jnp.where(mine_first, d_other, d_mine)
    f_mine = jnp.where(mine_first, d_later, 1.0)
    f_other = jnp.where(mine_first, 1.0, d_later)
    for i, part in blocks_of(rows):
        total = mine[part, :].astype(F32) * f_mine[i : i + 1] + other[part, :].astype(F32) * f_other[
            i : i + 1
        ]
        out[part, :] = total.astype(BF16)
    out[rows:, :] = pack_decay(d_mine * d_other)


def total_kernel(mine_ref, other_ref, after_ref, out_ref, *, bit):
    device = lax.axis_index(SEQ)
    rows = mine_ref.shape[0] - 16
    join_totals(mine_ref, other_ref, (device // bit) % 2 == 0, out_ref, rows)


def prefix_kernel(mine_ref, other_ref, pre_ref, dpre_ref, out_ref, opre_ref, odpre_ref, *, bit):
    device = lax.axis_index(SEQ)
    rows = mine_ref.shape[0] - 16
    first = (device // bit) % 2 == 0
    join_totals(mine_ref, other_ref, first, out_ref, rows)
    d_other = unpack_decay(other_ref[rows:, :])
    d_pre = dpre_ref[...]
    gain = jnp.where(first, 0.0, d_pre)
    for i, part in blocks_of(rows):
        opre_ref[part, :] = pre_ref[part, :] + gain[i : i + 1] * other_ref[part, :].astype(F32)
    odpre_ref[...] = jnp.where(first, d_pre, d_pre * d_other)


def start_kernel(mine_ref, other_ref, out_ref, opre_ref, odpre_ref, *, bit):
    device = lax.axis_index(SEQ)
    rows = mine_ref.shape[0] - 16
    first = (device // bit) % 2 == 0
    join_totals(mine_ref, other_ref, first, out_ref, rows)
    d_other = unpack_decay(other_ref[rows:, :])
    opre_ref[...] = jnp.where(first, 0.0, other_ref[:rows, :].astype(F32))
    odpre_ref[...] = jnp.where(first, 1.0, d_other)


def enter_kernel(
    mine_ref,
    other_ref,
    pre_ref,
    dpre_ref,
    cache_ref,
    own_ref,
    recv_ref,
    after_ref,
    send_ref,
    stay_ref,
    fin_ref,
    *,
    bit,
):
    device = lax.axis_index(SEQ)
    side = (device // 2) % 2
    rows = mine_ref.shape[0] - 16
    first = (device // bit) % 2 == 0
    d_mine = unpack_decay(mine_ref[rows:, :])
    d_other = unpack_decay(other_ref[rows:, :])
    d_later = jnp.where(first, d_other, d_mine)
    f_mine = jnp.where(first, d_later, 1.0)
    f_other = jnp.where(first, 1.0, d_later)
    d_all = d_mine * d_other
    d_pre = dpre_ref[...]
    gain = jnp.where(first, 0.0, d_pre)
    d_before = jnp.where(first, d_pre, d_pre * d_other)
    d_first = jnp.where(side == 0, unpack_decay(own_ref[rows:, :]), unpack_decay(recv_ref[rows:, :]))
    for i, part in blocks_of(rows):
        cache = cache_ref[part, :]
        other = other_ref[part, :].astype(F32)
        mine = mine_ref[part, :].astype(F32)
        row = slice(i, i + 1)
        fin_ref[part, :] = d_all[row] * cache + mine * f_mine[row] + other * f_other[row]
        plane = d_before[row] * cache + pre_ref[part, :] + gain[row] * other
        t_first = jnp.where(side == 0, own_ref[part, :].astype(F32), recv_ref[part, :].astype(F32))
        second = d_first[row] * plane + t_first
        send_ref[part, :] = jnp.where(side == 0, second, plane).astype(BF16)
        stay_ref[part, :] = jnp.where(side == 0, plane, second).astype(BF16)


def chip_kernel(stay_ref, recv_ref, keep_ref, part_ref, after_ref, send_ref):
    enter_block(stay_ref, recv_ref, keep_ref, part_ref, send_ref, lax.axis_index(SEQ) % 2 == 1)


def block_kernel(stay_ref, recv_ref, keep_ref, part_ref, after_ref, own_ref):
    enter_block(stay_ref, recv_ref, keep_ref, part_ref, own_ref, lax.axis_index(SEQ) % 2 == 0)


def enter_block(stay_ref, recv_ref, keep_ref, part_ref, out_ref, first):
    device = lax.axis_index(SEQ)
    core, side = device % 2, (device // 2) % 2
    rows = stay_ref.shape[0]

    def fill(values):
        for y in range(PAIR):
            for mine, source in ((True, stay_ref), (False, recv_ref)):

                @pl.when((side == y) == mine)
                def _(y=y, source=source):
                    values(y, source)

    @pl.when(first)
    def _():
        def values(y, source):
            out_ref[y] = source[...]

        fill(values)

    for kept, local in ((0, keep_ref), (1, part_ref)):

        @pl.when(jnp.logical_not(first) & (core == kept))
        def _(local=local):
            def values(y, source):
                decay = unpack_decay(local[y, rows:, :])
                for i, part in blocks_of(rows):
                    entered = decay[i : i + 1] * source[part, :].astype(F32)
                    out_ref[y, part, :] = (entered + local[y, part, :].astype(F32)).astype(BF16)

            fill(values)


def diag_kernel(
    xc_ref,
    xfix_ref,
    b_ref,
    bfix_ref,
    c_ref,
    cfix_ref,
    cum_ref,
    row_ref,
    skip_ref,
    after_ref,
    out_ref,
    *,
    head_dim,
):
    rows, width = xc_ref.shape
    per_group = width // head_dim // PAIR
    below = lax.broadcasted_iota(jnp.int32, (rows, rows), 0)
    across = lax.broadcasted_iota(jnp.int32, (rows, rows), 1)
    mask = below >= across
    b_all = jnp.concatenate([bfix_ref[...], b_ref[TOP:, :]], axis=0)
    c_all = jnp.concatenate([cfix_ref[...], c_ref[TOP:, :]], axis=0)
    b_turned = b_all.T
    quad = 128 // head_dim
    lane = lax.broadcasted_iota(jnp.int32, (rows, 128), 1) // head_dim
    heads = cum_ref.shape[1]
    base = pl.program_id(0) * PAIR * per_group
    cum = pltpu.roll(cum_ref[...], heads - base, axis=1)
    for y in range(PAIR):
        part = slice(y * STATE, (y + 1) * STATE)
        c_dot_b = jnp.dot(c_all[:, part], b_turned[part, :], preferred_element_type=F32)
        for q in range(per_group // quad):
            cols = pl.ds((y * per_group + q * quad) * head_dim, 128)
            x_quad = jnp.concatenate([xfix_ref[:, cols], xc_ref[TOP:, cols]], axis=0)
            lhs, rhs = [], []
            for k in range(quad):
                head = y * per_group + q * quad + k
                gap = cum[:, head : head + 1] - row_ref[head : head + 1, :]
                decay = jnp.exp2(jnp.where(mask, gap, -1e30))
                lhs.append((c_dot_b * decay).astype(BF16))
                rhs.append(jnp.where(lane == k, x_quad, jnp.zeros_like(x_quad)))
            inner = jnp.dot(
                jnp.concatenate(lhs, axis=1),
                jnp.concatenate(rhs, axis=0),
                preferred_element_type=F32,
            )
            out_ref[:, cols] = inner + skip_ref[:, cols] * x_quad.astype(F32)


def gate_kernel(len_ref, z_ref, ecum_ref, final_ref, gate_ref, grow_ref, mine_ref, *, head_dim):
    device = lax.axis_index(SEQ)
    rows, width = z_ref.shape
    per_step = ecum_ref.shape[2] // 2
    token = device * rows + lax.broadcasted_iota(jnp.int32, (rows, 128), 0)
    live = token < len_ref[0]
    head = lax.broadcasted_iota(jnp.int32, (2 * per_step, width), 0) % per_step
    lane = lax.broadcasted_iota(jnp.int32, (2 * per_step, width), 1)
    spread = jnp.where(head == lane // head_dim, 1.0, 0.0).astype(BF16)
    grow_ref[...] = jnp.dot(ecum_ref[0], spread, preferred_element_type=F32)
    for j in range(width // 128):
        cols = pl.ds(128 * j, 128)
        gate_ref[:, cols] = jnp.where(live, silu(z_ref[:, cols].astype(F32)), 0.0)

    @pl.when(pl.program_id(0) == 0)
    def _():
        step = (device // (2 * PAIR)) % (final_ref.shape[0] // STATE)
        mine = final_ref[pl.ds(pl.multiple_of(step * STATE, STATE), STATE), :]
        mine_ref[...] = mine.T


def out_kernel(
    diag_ref, gate_ref, grow_ref, c_ref, cfix_ref, own_ref, recv_ref, gain_ref, out_ref, held, sems
):
    core = lax.axis_index(SEQ) % 2
    steps, _, width = held.shape
    unit = width // (2 * PAIR)
    side = PAIR * STATE
    copies = []
    for i in range(steps):
        c_all = jnp.concatenate(
            [cfix_ref[:, i * side : (i + 1) * side], c_ref[TOP:, i * side : (i + 1) * side]], axis=0
        )
        for y in range(PAIR):
            own = own_ref[y, i * STATE : (i + 1) * STATE, :]
            recv = recv_ref[y, i * STATE : (i + 1) * STATE, :]
            state = jnp.concatenate(
                [jnp.where(core == 0, own, recv), jnp.where(core == 0, recv, own)], axis=1
            )
            first = i * width + 2 * y * unit
            cols = slice(first, first + 2 * unit)
            entering = jnp.dot(
                c_all[:, y * STATE : (y + 1) * STATE], state, preferred_element_type=F32
            )
            y_all = (diag_ref[:, cols] + grow_ref[:, cols] * entering).astype(BF16).astype(F32)
            gated = y_all * gate_ref[:, cols]
            scale = lax.rsqrt(jnp.mean(gated * gated, axis=1, keepdims=True) + 1e-05)
            held[i, :, 2 * y * unit : 2 * (y + 1) * unit] = (
                gated * scale * gain_ref[:, cols]
            ).astype(BF16)
        copy = pltpu.make_async_copy(
            held.at[i], out_ref.at[:, pl.ds(i * width, width)], sems.at[i]
        )
        copy.start()
        copies.append(copy)
    for copy in copies:
        copy.wait()


def swap(value, mask):
    devices = range(lax.axis_size(SEQ))
    return lax.ppermute(value, SEQ, [(i, i ^ mask) for i in devices])


def whole(shape):
    return pl.BlockSpec(shape, lambda *_: (0,) * len(shape))


def near(shape, dtype):
    return pltpu.VMEM(shape, dtype)


def far(value):
    return pltpu.with_memory_space_constraint(value, pltpu.HBM)


VMEM_SPEC = pl.BlockSpec(memory_space=pltpu.VMEM)
ANY_SPEC = pl.BlockSpec(memory_space=pl.ANY)


def plain_call(body, out_shape, *args, after=(), nbytes=2**20, scratch=()):
    return pl.pallas_call(
        body,
        out_shape=out_shape,
        in_specs=[VMEM_SPEC] * len(args) + [ANY_SPEC] * len(after),
        out_specs=jax.tree.map(lambda _: VMEM_SPEC, out_shape),
        scratch_shapes=list(scratch),
        compiler_params=pltpu.CompilerParams(vmem_limit_bytes=12 * 2**20),
        cost_estimate=pl.CostEstimate(flops=0, bytes_accessed=nbytes, transcendentals=0),
    )(*args, *after)


def body(
    x_in,
    bc_in,
    z_in,
    dt_in,
    conv_weight,
    conv_bias,
    dt_bias,
    a_log,
    d_skip,
    norm_gain,
    conv_cache,
    cache_state,
    lengths,
):
    rows, inner = x_in.shape
    heads = dt_in.shape[1]
    head_dim = inner // heads
    devices = lax.axis_size(SEQ)
    index = lax.axis_index(SEQ)
    share = heads // devices
    steps = GROUPS // PAIR
    per_step = heads // steps
    width = inner // steps
    side = GROUPS * STATE
    bcw = PAIR * STATE
    b0, c0 = inner // bcw, inner // bcw + steps
    unit = width // (2 * PAIR)
    unit_heads = unit // head_dim
    state_rows = steps * STATE
    msg_rows = state_rows + 16
    smem = pl.BlockSpec(memory_space=pltpu.SMEM)

    def at(r, c, off):
        return pl.BlockSpec((r, c), lambda i: (0, i + off))

    def lead(*shape):
        return pl.BlockSpec(shape, lambda i: (i,) + (0,) * (len(shape) - 1))

    rim = pl.pallas_call(
        rim_kernel,
        out_shape=near((RIM, inner + 2 * side), BF16),
        in_specs=[ANY_SPEC, ANY_SPEC],
        out_specs=VMEM_SPEC,
        scratch_shapes=[
            pltpu.VMEM((TOP, inner), BF16),
            pltpu.VMEM((TOP, 2 * side), BF16),
            pltpu.SemaphoreType.DMA((2,)),
        ],
        compiler_params=pltpu.CompilerParams(vmem_limit_bytes=4 * 2**20),
    )(far(x_in), far(bc_in))
    rim_recv = lax.ppermute(rim, SEQ, [(i, (i + 1) % devices) for i in range(devices)])

    bias2 = far(conv_bias.reshape(1, -1))
    weight = far(conv_weight)
    weight_specs = [at(CONV_W, width, 0), at(CONV_W, bcw, b0), at(CONV_W, bcw, c0)]
    bias_specs = [at(1, width, 0), at(1, bcw, b0), at(1, bcw, c0)]
    xc, bc, cc, prex, preb, prec, cum, row, ecum, dec, top, local = grid_call(
        functools.partial(conv_kernel, heads=heads, head_dim=head_dim),
        (steps,),
        [smem, at(rows, width, 0), at(rows, bcw, 0), at(rows, bcw, steps), whole((rows, heads))]
        + weight_specs
        + bias_specs
        + [whole((1, heads))] * 2
        + [ANY_SPEC],
        [
            at(rows, width, 0),
            at(rows, bcw, 0),
            at(rows, bcw, 0),
            at(8, width, 0),
            at(8, bcw, 0),
            at(8, bcw, 0),
            whole((rows, heads)),
            whole((heads, rows)),
            whole((steps, rows, 2 * per_step)),
            whole((2 * PAIR, 16, unit)),
            at(8, width, 0),
            lead(PAIR, STATE, width // PAIR),
        ],
        [
            near((rows, inner), BF16),
            near((rows, side), BF16),
            near((rows, side), BF16),
            near((8, inner), F32),
            near((8, side), F32),
            near((8, side), F32),
            near((rows, heads), F32),
            near((heads, rows), F32),
            near((steps, rows, 2 * per_step), BF16),
            near((2 * PAIR, 16, unit), BF16),
            near((8, inner), F32),
            near((GROUPS, STATE, width // PAIR), F32),
        ],
        scratch=[
            pltpu.VMEM((8 + rows, 128), F32),
            pltpu.VMEM((steps, rows, 2 * per_step), BF16),
            pltpu.VMEM((rows, width), BF16),
        ],
        nbytes=4 * 2**20,
    )(
        lengths,
        far(x_in),
        far(bc_in),
        far(bc_in),
        far(dt_in),
        weight,
        weight,
        weight,
        bias2,
        bias2,
        bias2,
        far(dt_bias.reshape(1, -1)),
        far(a_log.reshape(1, -1)),
        rim,
    )

    pair_msg = near((PAIR, msg_rows, unit), BF16)
    send, keep, xfix, bfix, cfix = plain_call(
        fix_kernel,
        (pair_msg, pair_msg, near((TOP, inner), BF16), near((TOP, side), BF16), near((TOP, side), BF16)),
        rim_recv,
        conv_cache,
        conv_weight,
        prex,
        preb,
        prec,
        xc,
        bc,
        cc,
        top,
        local,
        dec,
        scratch=[pltpu.VMEM((16, inner + 2 * side), F32)],
    )

    message = near((msg_rows, unit), BF16)
    part = swap(send, 1)
    send_y, own = plain_call(core_kernel, (message, message), keep, part)
    recv = swap(send_y, 2)
    cache_steps = 4
    cache = grid_call(
        functools.partial(cache_kernel, unit_heads=unit_heads),
        (cache_steps,),
        [lead(head_dim // cache_steps, STATE, heads), ANY_SPEC],
        whole((state_rows, unit)),
        near((state_rows, unit), F32),
        scratch=[pltpu.VMEM((unit // 128, steps, STATE, 128), F32)],
        nbytes=2 * 2**20,
    )(far(cache_state.transpose(1, 2, 0)), own)
    total = plain_call(
        functools.partial(total_kernel, bit=2), message, own, recv, after=(cache,)
    )
    pre = None
    bit = 4
    pre_shape = (near((state_rows, unit), F32), near((8, unit), F32))
    while 2 * bit < devices:
        other = swap(total, 2 * bit - 4)
        if pre is None:
            total, *pre = plain_call(
                functools.partial(start_kernel, bit=bit), (message,) + pre_shape, total, other
            )
        else:
            total, *pre = plain_call(
                functools.partial(prefix_kernel, bit=bit), (message,) + pre_shape, total, other, *pre
            )
        bit *= 2
    if pre is None:
        pre = [jnp.zeros((state_rows, unit), F32), jnp.ones((8, unit), F32)]
    other = swap(total, 2 * bit - 4)
    diag = grid_call(
        functools.partial(diag_kernel, head_dim=head_dim),
        (steps,),
        [
            at(rows, width, 0),
            at(TOP, width, 0),
            at(rows, bcw, 0),
            at(TOP, bcw, 0),
            at(rows, bcw, 0),
            at(TOP, bcw, 0),
            whole((rows, heads)),
            pl.BlockSpec((per_step, rows), lambda i: (i, 0)),
            at(1, width, 0),
            ANY_SPEC,
        ],
        at(rows, width, 0),
        near((rows, inner), F32),
        nbytes=8 * 2**20,
    )(xc, xfix, bc, bfix, cc, cfix, cum, row, jnp.repeat(d_skip, head_dim).reshape(1, -1), total)
    state_out = near((state_rows, unit), BF16)
    send_y, stay, final = plain_call(
        functools.partial(enter_kernel, bit=bit),
        (state_out, state_out, near((state_rows, unit), F32)),
        total,
        other,
        *pre,
        cache,
        own,
        recv,
        after=(diag,),
    )
    recv_y = swap(send_y, 2)
    gate, grow, mine = grid_call(
        functools.partial(gate_kernel, head_dim=head_dim),
        (steps,),
        [smem, at(rows, width, 0), lead(1, rows, 2 * per_step), whole((state_rows, unit))],
        [at(rows, width, 0), at(rows, width, 0), whole((unit, STATE))],
        [
            near((rows, inner), F32),
            near((rows, inner), F32),
            jax.ShapeDtypeStruct((unit, STATE), F32),
        ],
        nbytes=5 * 2**20,
    )(lengths, far(z_in), ecum, final)
    half = near((PAIR, state_rows, unit), BF16)
    send_c = plain_call(chip_kernel, half, stay, recv_y, keep, part, after=(gate,))
    enter_recv = swap(send_c, 1)
    enter_own = plain_call(block_kernel, half, stay, recv_y, keep, part, after=(send_c,))

    mixed = pl.pallas_call(
        out_kernel,
        out_shape=jax.ShapeDtypeStruct((rows, inner), BF16),
        in_specs=[VMEM_SPEC] * 8,
        out_specs=ANY_SPEC,
        scratch_shapes=[
            pltpu.VMEM((steps, rows, width), BF16),
            pltpu.SemaphoreType.DMA((steps,)),
        ],
        compiler_params=pltpu.CompilerParams(vmem_limit_bytes=16 * 2**20),
        cost_estimate=pl.CostEstimate(flops=0, bytes_accessed=4 * 2**20, transcendentals=0),
    )(diag, gate, grow, cc, cfix, enter_own, enter_recv, norm_gain.reshape(1, -1))

    if share * head_dim == unit and devices == 2 * PAIR * steps:
        mine = mine.reshape(share, head_dim, STATE)
    else:
        around = [[4 * i + j for j in range(4)] for i in range(devices // 4)]
        every = final.reshape(steps, STATE, unit)
        every = lax.all_gather(every, SEQ, axis=1, axis_index_groups=around)
        every = every.reshape(steps * 2 * PAIR, STATE, unit).transpose(0, 2, 1)
        every = every.reshape(heads, head_dim, STATE)
        mine = lax.dynamic_slice_in_dim(every, index * share, share, 0)
    return (mixed, mine)


def solution(mesh):
    in_specs = (
        P(("groups", "seq"), None),
        P(("groups", "seq"), None),
        P(("groups", "seq"), None),
        P(("groups", "seq"), None),
        P(),
        P(),
        P(),
        P(),
        P(),
        P(),
        P("groups", None),
        P("groups", None, None),
        P("groups"),
    )
    out_specs = (P(("groups", "seq"), None), P(("groups", "seq"), None, None))
    return jax.shard_map(body, mesh=mesh, in_specs=in_specs, out_specs=out_specs, check_vma=False)
```

time: 68.3 us -> 40.6 us (0.59); the launches traced: 67.1 us -> 40.3 us
  local copies, waits for them, and re-layouts: 27.4 us -> 0.2 us
  Pallas kernels: 14 us -> 20 us
  waiting for transfers between devices: 13.8 us -> 8.96 us
    unnamed x53 -> x8, local copies, waits for them, and re-layouts: 20.9 us -> 0.02 us
    ppermute x6, waiting for transfers between devices: 13.8 us -> 7.95 us  [swap(): return lax.ppermute(value, SEQ, [(i, i ^ mask) for i in devices])]
    pallas_call x8 -> x12, Pallas kernels: 11.5 us -> 14.9 us  [the longest x1 4.15 us: body(): grid_call(functools.partial(diag_kernel, head_dim=head_dim), (steps,), [a...]
    dynamic_slice x2 -> x0, local copies, waits for them, and re-layouts: 3.1 us -> none  [body(): cache = lax.dynamic_index_in_dim(cache, quarter, 1, keepdims=False)]
    pallas_call x1, Pallas kernels: 2.48 us -> 5.02 us  [body(): grid_call(functools.partial(conv_kernel, heads=heads, head_dim=head_dim),...]
    slice x2 -> x0, local copies, waits for them, and re-layouts: 1.62 us -> none  [body(): rim = jnp.concatenate([x_in[rows - RIM:], bc_in[rows - RIM:]], axis=1)]
    transpose x2 -> x0, local copies, waits for them, and re-layouts: 1.61 us -> none  [body(): mine = mine.T.reshape(share, head_dim, STATE)]
    ppermute x1, waiting for transfers between devices: 0.01 us -> 1 us  [body(): lax.ppermute(rim, SEQ, [(i, (i + 1) % devices) for i in range(devices)])]
  transfers between devices with their start and end apart: 7 -> 7, of which waited for: 4 -> 6; matrix products, arithmetic and copies ran while one was open for 13% -> 0% of each run, Pallas kernels for 10% -> 40%
where the time goes in v2:
time: 40.6 us; the launch traced here: 40.3 us
  Pallas kernels  20 us (49%)
  starting transfers between devices  9.79 us (24%)
  waiting for transfers between devices  8.96 us (22%)
  between operations  1.41 us (3%)
    ppermute x6, starting transfers between devices, swap(): return lax.ppermute(value, SEQ, [(i, i ^ mask) for i in devices])  9.29 us
    ppermute x6, waiting for transfers between devices, swap(): return lax.ppermute(value, SEQ, [(i, i ^ mask) for i in devices])  7.95 us
    pallas_call x1, Pallas kernels, body(): grid_call(functools.partial(conv_kernel, heads=heads, head_dim=head_dim),...  5.02 us
    pallas_call x1, Pallas kernels, body(): grid_call(functools.partial(diag_kernel, head_dim=head_dim), (steps,), [a...  4.15 us
    pallas_call x1, Pallas kernels, body(): grid_call(functools.partial(gate_kernel, head_dim=head_dim), (steps,), [s...  3.83 us
    pallas_call x1, Pallas kernels, body(): grid_call(functools.partial(cache_kernel, unit_heads=unit_heads), (cache_...  3.26 us
    pallas_call x1, Pallas kernels, body(): pl.pallas_call(out_kernel, out_shape=jax.ShapeDtypeStruct((rows, inner),...  1.67 us
    pallas_call x7, Pallas kernels, plain_call(): pl.pallas_call(body, out_shape=out_shape, in_specs=[VMEM_SPEC] * len(args...  1.05 us
  transfers between devices with their start and end apart: 7, of which 6 were waited for; matrix products, arithmetic and copies ran while one was open for 0% of the time, Pallas kernels for 40%

profile of v2, /device:TPU:0, one launch (start us, length us, event | category | flops | bytes accessed | tf_op | source)
XLA Modules:
  0.0 40.3 jit_solution(18267207795563672944)
XLA Ops:
  0.6 0.0 copy-start
  0.6 0.0 copy-start.1
  0.7 1.0 %shard_map.140.after_ref = bf16[3,5120]{1,0:T(4,128)(2,1)S(1)} custom-call(bf16[128,4096]{1,0:T(8,128)(2,1)} %x_ref.3, bf16[128,1024]{1,0:T(8,128)(2,1)} %c_ref.1), custom_call_target="tpu_custom_call" | custom-call | tf_op jit(solution)/shard_map/pallas_call | solution.py:603
  1.6 0.5 %collective-permute-start = (bf16[3,5120]{1,0:T(4,128)(2,1)S(1)}, bf16[3,5120]{1,0:T(4,128)(2,1)S(1)}, u32[]{:S(2)}, u32[]{:S(2)}) collective-permute-start(bf16[3,5120]{1,0:T(4,128)(2,1)S(1)} %shard_map.140.after_ref), channel_id=1, source_target_pairs={{0,1},{1,2},{2,3},{3,4},{4,5},{5,6},{6,7},{7,8},{8,9},{9,10},{10,1... | collective-permute-start | bytes 92168 | tf_op jit(solution)/shard_map/ppermute | solution.py:615
  2.8 5.0 %shard_map.141 = (bf16[128,4096]{1,0:T(8,128)(2,1)S(1)}, bf16[128,512]{1,0:T(8,128)(2,1)S(1)}, bf16[128,512]{1,0:T(8,128)(2,1)S(1)}, f32[8,4096]{1,0:T(8,128)S(1...) custom-call(s32[1]{0:T(128)S(6)} %copy.15.len_ref, ...), custom_call_target="tpu_custom_call" | custom-call | bytes 4194304 | tf_op jit(solution)/shard_map/pallas_call | solution.py:621
  7.8 1.0 %collective-permute-done.rim_ref = bf16[3,5120]{1,0:T(4,128)(2,1)S(1)} collective-permute-done((bf16[3,5120]{1,0:T(4,128)(2,1)S(1)}, bf16[3,5120]{1,0:T(4,128)(2,1)S(1)}, u32[]{:S(2)}, u32[]{:S(2)}) %collective-permute-start) | collective-permute-done | bytes 30752 | tf_op jit(solution)/shard_map/ppermute | solution.py:615
  8.8 0.0 copy-done
  8.8 0.0 copy-done.1
  8.8 0.4 %shard_map.142 = (bf16[2,272,256]{2,1,0:T(8,128)(2,1)S(1)}, bf16[2,272,256]{2,1,0:T(8,128)(2,1)S(1)}, bf16[16,4096]{1,0:T(8,128)(2,1)S(1)}, bf16[16,512]{1,0:T(8,128)(2,1)S(1)}, bf16[16,512]{1,0:T(8,128)(2,1)S(1)}) custom-call(bf16[3,5120]{1,0:T(4,128)(2,1)S(1)} %collective-permute-done.rim_ref, bf16[3,5120]{1,0:T(4,128)(2,1)S(1)} %copy-done.1, ...), custom_call_target="tpu_custom_call" | custom-call | bytes 1048576 | tf_op jit(solution)/shard_map/pallas_call | solution.py:553
  9.3 0.0 copy-start.3
  9.3 1.7 %collective-permute-start.1 = (bf16[2,272,256]{2,1,0:T(8,128)(2,1)S(1)}, bf16[2,272,256]{2,1,0:T(8,128)(2,1)S(1)}, u32[]{:S(2)}, u32[]{:S(2)}) collective-permute-start(bf16[2,272,256]{2,1,0:T(8,128)(2,1)S(1)} %get-tuple-element.45), channel_id=1, source_target_pairs={{0,1},{1,0},{2,3},{3,2},{4,5},{5,4},{6,7},{7,6},{8,9},{9,8},{10,11... | collective-permute-start | bytes 835592 | tf_op jit(solution)/shard_map/ppermute | solution.py:533
  11.0 1.2 %collective-permute-done.1.recv_ref.part_ref = bf16[2,272,256]{2,1,0:T(8,128)(2,1)S(1)} collective-permute-done((bf16[2,272,256]{2,1,0:T(8,128)(2,1)S(1)}, bf16[2,272,256]{2,1,0:T(8,128)(2,1)S(1)}, u32[]{:S(2)}, u32[]{:S(2)}) %collective-permute-start.1) | collective-permute-done | bytes 278560 | tf_op jit(solution)/shard_map/ppermute | solution.py:533
  12.2 0.1 shard_map.143
  12.3 1.6 %collective-permute-start.2 = (bf16[272,256]{1,0:T(8,128)(2,1)S(1)}, bf16[272,256]{1,0:T(8,128)(2,1)S(1)}, u32[]{:S(2)}, u32[]{:S(2)}) collective-permute-start(bf16[272,256]{1,0:T(8,128)(2,1)S(1)} %get-tuple-element.47), channel_id=1, source_target_pairs={{0,2},{1,3},{2,0},{3,1},{4,6},{5,7},{6,4},{7,5},{8,10},{9,11},{10,... | collective-permute-start | bytes 417800 | tf_op jit(solution)/shard_map/ppermute | solution.py:533
  13.9 3.3 %shard_map.144.after_ref.cache_ref = f32[256,256]{1,0:T(8,128)S(1)} custom-call(f32[32,64,128]{2,1,0:T(8,128)} %bitcast.7, bf16[272,256]{1,0:T(8,128)(2,1)S(1)} %get-tuple-element.46.after_ref.mine_ref.own_ref), custom_call_target="tpu_custom_call" | custom-call | bytes 2097152 | tf_op jit(solution)/shard_map/pallas_call | solution.py:704
  17.2 1.1 %collective-permute-done.2.other_ref.recv_ref = bf16[272,256]{1,0:T(8,128)(2,1)S(1)} collective-permute-done((bf16[272,256]{1,0:T(8,128)(2,1)S(1)}, bf16[272,256]{1,0:T(8,128)(2,1)S(1)}, u32[]{:S(2)}, u32[]{:S(2)}) %collective-permute-start.2) | collective-permute-done | bytes 139296 | tf_op jit(solution)/shard_map/ppermute | solution.py:533
  18.3 0.1 shard_map.145.mine_ref
  18.4 1.6 %collective-permute-start.3 = (bf16[272,256]{1,0:T(8,128)(2,1)S(1)}, bf16[272,256]{1,0:T(8,128)(2,1)S(1)}, u32[]{:S(2)}, u32[]{:S(2)}) collective-permute-start(bf16[272,256]{1,0:T(8,128)(2,1)S(1)} %shard_map.145.mine_ref), channel_id=1, source_target_pairs={{0,4},{1,5},{2,6},{3,7},{4,0},{5,1},{6,2},{7,3},{8,12},{9,13},{10,... | collective-permute-start | bytes 417800 | tf_op jit(solution)/shard_map/ppermute | solution.py:533
  20.0 3.6 %collective-permute-done.3.other_ref = bf16[272,256]{1,0:T(8,128)(2,1)S(1)} collective-permute-done((bf16[272,256]{1,0:T(8,128)(2,1)S(1)}, bf16[272,256]{1,0:T(8,128)(2,1)S(1)}, u32[]{:S(2)}, u32[]{:S(2)}) %collective-permute-start.3) | collective-permute-done | bytes 139296 | tf_op jit(solution)/shard_map/ppermute | solution.py:533
  23.6 0.1 shard_map.146
  23.7 3.7 %collective-permute-start.4 = (bf16[272,256]{1,0:T(8,128)(2,1)S(1)}, bf16[272,256]{1,0:T(8,128)(2,1)S(1)}, u32[]{:S(2)}, u32[]{:S(2)}) collective-permute-start(bf16[272,256]{1,0:T(8,128)(2,1)S(1)} %get-tuple-element.48.after_ref.mine_ref), channel_id=1, source_target_pairs={{0,12},{1,13},{2,14},{3,15},{4,8},{5,9},{6,10},{7,11},{8,4},{9,5},... | collective-permute-start | bytes 417800 | tf_op jit(solution)/shard_map/ppermute | solution.py:533
  27.3 0.0 copy-done.3
  27.3 0.1 broadcast_in_dim.3
  27.4 0.1 reshape_reshape.3.skip_ref
  27.5 4.1 %shard_map.147.after_ref.diag_ref = f32[128,4096]{1,0:T(8,128)S(1)} custom-call(bf16[128,4096]{1,0:T(8,128)(2,1)S(1)} %get-tuple-element.30.xc_ref, bf16[16,4096]{1,0:T(8,128)(2,1)S(1)} %get-tuple-element.39.xfix_ref, bf16[128,512]{1,0:T(8,128)(2,1)S(1)} %get-tuple-element.34.bc_ref.b_ref, bf16[16,512]{1,0:T(8,128)(2,1)S(1)} %get-tuple-element.40.bfix_ref, ...), custom_call_target="tpu_custom_call" | custom-call | bytes 8388608 | tf_op jit(solution)/shard_map/pallas_call | solution.py:733
  31.7 0.0 collective-permute-done.4.other_ref
  31.7 0.2 shard_map.148
  31.9 0.6 %collective-permute-start.5 = (bf16[256,256]{1,0:T(8,128)(2,1)S(1)}, bf16[256,256]{1,0:T(8,128)(2,1)S(1)}, u32[]{:S(2)}, u32[]{:S(2)}) collective-permute-start(bf16[256,256]{1,0:T(8,128)(2,1)S(1)} %get-tuple-element.56), channel_id=1, source_target_pairs={{0,2},{1,3},{2,0},{3,1},{4,6},{5,7},{6,4},{7,5},{8,10},{9,11},{10,... | collective-permute-start | bytes 393224 | tf_op jit(solution)/shard_map/ppermute | solution.py:533
  32.5 3.8 %shard_map.149 = (f32[128,4096]{1,0:T(8,128)S(1)}, f32[128,4096]{1,0:T(8,128)S(1)}, f32[256,64]{1,0:T(8,128)}) custom-call(s32[1]{0:T(128)S(6)} %copy.15.len_ref, bf16[128,4096]{1,0:T(8,128)(2,1)} %z_ref.1, bf16[4,128,64]{2,1,0:T(8,128)(2,1)S(1)} %get-tuple-element.49.ecum_ref, f32[256,256]{1,0:T(8,128)S(1)} %get-tuple-element.52.final_ref), custom_call_target="tpu_custom_call" | custom-call | bytes 5242880 | tf_op jit(solution)/shard_map/pallas_call | solution.py:765
  36.3 0.6 %collective-permute-done.5.recv_ref = bf16[256,256]{1,0:T(8,128)(2,1)S(1)} collective-permute-done((bf16[256,256]{1,0:T(8,128)(2,1)S(1)}, bf16[256,256]{1,0:T(8,128)(2,1)S(1)}, u32[]{:S(2)}, u32[]{:S(2)}) %collective-permute-start.5) | collective-permute-done | bytes 131104 | tf_op jit(solution)/shard_map/ppermute | solution.py:533
  36.9 0.0 copy-start.2
  36.9 0.1 shard_map.150.after_ref
  37.0 0.1 collective-permute-start.6
  37.1 0.1 shard_map.151.own_ref
  37.2 1.5 %collective-permute-done.6.recv_ref = bf16[2,256,256]{2,1,0:T(8,128)(2,1)S(1)} collective-permute-done((bf16[2,256,256]{2,1,0:T(8,128)(2,1)S(1)}, bf16[2,256,256]{2,1,0:T(8,128)(2,1)S(1)}, u32[]{:S(2)}, u32[]{:S(2)}) %collective-permute-start.6) | collective-permute-done | bytes 262176 | tf_op jit(solution)/shard_map/ppermute | solution.py:533
  38.6 0.0 copy-done.2
  38.6 1.7 %shard_map.152 = bf16[128,4096]{1,0:T(8,128)(2,1)} custom-call(f32[128,4096]{1,0:T(8,128)S(1)} %shard_map.147.after_ref.diag_ref, f32[128,4096]{1,0:T(8,128)S(1)} %get-tuple-element.53.after_ref.gate_ref, f32[128,4096]{1,0:T(8,128)S(1)} %get-tuple-element.54.grow_ref, bf16[128,512]{1,0:T(8,128)(2,1)S(1)} %get-tuple-element.35.cc_ref.c_ref, ...), custom_call_target="tpu_custom_call" | custom-call | bytes 4194304 | tf_op jit(solution)/shard_map/pallas_call | solution.py:782
Async XLA Ops:
  0.6 8.2 %copy-start = (f32[4,5120]{1,0:T(4,128)S(1)}, f32[4,5120]{1,0:T(4,128)}, u32[]{:S(2)}) copy-start(f32[4,5120]{1,0:T(4,128)} %w_ref.1) | copy-start | bytes 245764
  0.6 8.2 %copy-start.1 = (bf16[3,5120]{1,0:T(4,128)(2,1)S(1)}, bf16[3,5120]{1,0:T(4,128)(2,1)}, u32[]{:S(2)}) copy-start(bf16[3,5120]{1,0:T(4,128)(2,1)} %cache_ref.1) | copy-start | bytes 92164
  1.6 7.2 %collective-permute-start = (bf16[3,5120]{1,0:T(4,128)(2,1)S(1)}, bf16[3,5120]{1,0:T(4,128)(2,1)S(1)}, u32[]{:S(2)}, u32[]{:S(2)}) collective-permute-start(bf16[3,5120]{1,0:T(4,128)(2,1)S(1)} %shard_map.140.after_ref), channel_id=1, source_target_pairs={{0,1},{1,2},{2,3},{3,4},{4,5},{5,6},{6,7},{7,8},{8,9},{9,10},{10,1... | collective-permute-start | bytes 92168 | tf_op jit(solution)/shard_map/ppermute | solution.py:615
  9.3 18.1 %copy-start.3 = (f32[128]{0:T(128)S(1)}, f32[128]{0:T(128)}, u32[]{:S(2)}) copy-start(f32[128]{0:T(128)} %param.21) | copy-start | bytes 1540
  9.3 2.9 %collective-permute-start.1 = (bf16[2,272,256]{2,1,0:T(8,128)(2,1)S(1)}, bf16[2,272,256]{2,1,0:T(8,128)(2,1)S(1)}, u32[]{:S(2)}, u32[]{:S(2)}) collective-permute-start(bf16[2,272,256]{2,1,0:T(8,128)(2,1)S(1)} %get-tuple-element.45), channel_id=1, source_target_pairs={{0,1},{1,0},{2,3},{3,2},{4,5},{5,4},{6,7},{7,6},{8,9},{9,8},{10,11... | collective-permute-start | bytes 835592 | tf_op jit(solution)/shard_map/ppermute | solution.py:533
  12.3 6.0 %collective-permute-start.2 = (bf16[272,256]{1,0:T(8,128)(2,1)S(1)}, bf16[272,256]{1,0:T(8,128)(2,1)S(1)}, u32[]{:S(2)}, u32[]{:S(2)}) collective-permute-start(bf16[272,256]{1,0:T(8,128)(2,1)S(1)} %get-tuple-element.47), channel_id=1, source_target_pairs={{0,2},{1,3},{2,0},{3,1},{4,6},{5,7},{6,4},{7,5},{8,10},{9,11},{10,... | collective-permute-start | bytes 417800 | tf_op jit(solution)/shard_map/ppermute | solution.py:533
  18.4 5.2 %collective-permute-start.3 = (bf16[272,256]{1,0:T(8,128)(2,1)S(1)}, bf16[272,256]{1,0:T(8,128)(2,1)S(1)}, u32[]{:S(2)}, u32[]{:S(2)}) collective-permute-start(bf16[272,256]{1,0:T(8,128)(2,1)S(1)} %shard_map.145.mine_ref), channel_id=1, source_target_pairs={{0,4},{1,5},{2,6},{3,7},{4,0},{5,1},{6,2},{7,3},{8,12},{9,13},{10,... | collective-permute-start | bytes 417800 | tf_op jit(solution)/shard_map/ppermute | solution.py:533
  23.7 8.0 %collective-permute-start.4 = (bf16[272,256]{1,0:T(8,128)(2,1)S(1)}, bf16[272,256]{1,0:T(8,128)(2,1)S(1)}, u32[]{:S(2)}, u32[]{:S(2)}) collective-permute-start(bf16[272,256]{1,0:T(8,128)(2,1)S(1)} %get-tuple-element.48.after_ref.mine_ref), channel_id=1, source_target_pairs={{0,12},{1,13},{2,14},{3,15},{4,8},{5,9},{6,10},{7,11},{8,4},{9,5},... | collective-permute-start | bytes 417800 | tf_op jit(solution)/shard_map/ppermute | solution.py:533
  31.9 5.0 %collective-permute-start.5 = (bf16[256,256]{1,0:T(8,128)(2,1)S(1)}, bf16[256,256]{1,0:T(8,128)(2,1)S(1)}, u32[]{:S(2)}, u32[]{:S(2)}) collective-permute-start(bf16[256,256]{1,0:T(8,128)(2,1)S(1)} %get-tuple-element.56), channel_id=1, source_target_pairs={{0,2},{1,3},{2,0},{3,1},{4,6},{5,7},{6,4},{7,5},{8,10},{9,11},{10,... | collective-permute-start | bytes 393224 | tf_op jit(solution)/shard_map/ppermute | solution.py:533
  36.9 1.7 %copy-start.2 = (f32[4096]{0:T(1024)S(1)}, f32[4096]{0:T(1024)}, u32[]{:S(2)}) copy-start(f32[4096]{0:T(1024)} %param.22) | copy-start | bytes 49156
  37.0 1.6 %collective-permute-start.6 = (bf16[2,256,256]{2,1,0:T(8,128)(2,1)S(1)}, bf16[2,256,256]{2,1,0:T(8,128)(2,1)S(1)}, u32[]{:S(2)}, u32[]{:S(2)}) collective-permute-start(bf16[2,256,256]{2,1,0:T(8,128)(2,1)S(1)} %shard_map.150.after_ref), channel_id=1, source_target_pairs={{0,1},{1,0},{2,3},{3,2},{4,5},{5,4},{6,7},{7,6},{8,9},{9,8},{10,11... | collective-permute-start | bytes 786440 | tf_op jit(solution)/shard_map/ppermute | solution.py:533

commit v3 on v2

v3 whole, which is shorter than its diff:
```python
import functools

import jax
import jax.numpy as jnp
from jax import lax
from jax.experimental import pallas as pl
from jax.experimental.pallas import tpu as pltpu
from jax.sharding import PartitionSpec as P

STATE = 64
GROUPS = 8
CONV_W = 4
RIM = CONV_W - 1
LOG2E = 1.4426950408889634
BF16 = jnp.bfloat16
F32 = jnp.float32
HI = lax.Precision.HIGHEST
SEQ = "seq"
PAIR = 2
TOP = 16


def silu(v):
    half = 0.5 * v
    return half + half * jnp.tanh(half)


def split2(v):
    hi = v.astype(BF16)
    return hi, (v - hi.astype(F32)).astype(BF16)


def rim_kernel(*refs, count):
    x_ref, bc_ref = refs[:2]
    sources, out_ref, refs = refs[2 : 2 + count], refs[2 + count], refs[3 + count :]
    targets, (x_rows, bc_rows, sems) = refs[: count + 1], refs[count + 1 :]
    rows, inner = x_ref.shape
    pairs = [
        (x_ref.at[pl.ds(rows - TOP, TOP), :], x_rows),
        (bc_ref.at[pl.ds(rows - TOP, TOP), :], bc_rows),
        (x_ref.at[:, pl.ds(0, targets[0].shape[1])], targets[0]),
    ] + list(zip(sources, targets[1:]))
    copies = [pltpu.make_async_copy(a, b, sems.at[k]) for k, (a, b) in enumerate(pairs)]
    for copy in copies:
        copy.start()
    for copy in copies[:2]:
        copy.wait()
    out_ref[:, :inner] = x_rows[...].astype(F32)[TOP - RIM :, :].astype(BF16)
    out_ref[:, inner:] = bc_rows[...].astype(F32)[TOP - RIM :, :].astype(BF16)
    for copy in copies[2:]:
        copy.wait()


def pack_decay(dec):
    hi, lo = split2(dec)
    return jnp.concatenate([hi.astype(F32), lo.astype(F32)], axis=0).astype(BF16)


def unpack_decay(rows):
    both = rows.astype(F32)
    return both[0:8] + both[8:16]


def convolve(values, w_ref, bias_ref, first, ext, rows):
    cols = pl.ds(first, 128)
    ext[8:, :] = values.astype(F32)
    total = jnp.broadcast_to(bias_ref[:, cols], (rows, 128))
    for k in range(CONV_W):
        total = total + ext[pl.ds(8 + k - RIM, rows), :] * w_ref[k : k + 1, cols]
    return total


def conv_kernel(
    len_ref,
    x_hbm,
    x0_ref,
    bc_ref,
    w_ref,
    bias_ref,
    dt_ref,
    dtb_ref,
    alog_ref,
    after_ref,
    xo_ref,
    bo_ref,
    prex_ref,
    preb_ref,
    cum_ref,
    step_ref,
    dec_ref,
    top_ref,
    local_ref,
    x_ref,
    ext,
    tails,
    scaled,
    sems,
    *,
    heads,
    head_dim,
):
    more, rows, width = x_ref.shape
    steps = more + 1
    per_step = heads // steps
    side = bo_ref.shape[1]
    inner = steps * width
    copies = [
        pltpu.make_async_copy(
            x_hbm.at[:, pl.ds((i + 1) * width, width)], x_ref.at[i], sems.at[i]
        )
        for i in range(more)
    ]
    for copy in copies:
        copy.start()
    spare = ext.shape[0]
    for k in range(spare):
        ext[k, 0:8, :] = jnp.zeros((8, 128), F32)

    raw = dt_ref[...].astype(F32) + dtb_ref[...]
    soft = jnp.maximum(raw, 0.0) + jnp.log1p(jnp.exp(-jnp.abs(raw)))
    token = lax.axis_index(SEQ) * rows + lax.broadcasted_iota(jnp.int32, (rows, heads), 0)
    dt = jnp.where(token < len_ref[0], soft, 0.0)
    step_ref[...] = dt
    rate = -jnp.exp(alog_ref[...]) * dt
    below = lax.broadcasted_iota(jnp.int32, (rows, rows), 0)
    across = lax.broadcasted_iota(jnp.int32, (rows, rows), 1)
    tri = jnp.where(below >= across, 1.0, 0.0).astype(BF16)
    hi, rest = split2(rate)
    mid, low = split2(rate - hi.astype(F32))
    sums = jnp.dot(tri, jnp.concatenate([hi, mid, low], axis=1), preferred_element_type=F32)
    cum = sums[:, :heads] + (sums[:, heads : 2 * heads] + sums[:, 2 * heads :])
    cum_ref[...] = cum

    for j in range(side // 128):
        cols = pl.ds(128 * j, 128)
        total = convolve(bc_ref[:, cols], w_ref, bias_ref, inner + 128 * j, ext.at[j % spare], rows)
        preb_ref[:, cols] = total[0:8]
        bo_ref[:, cols] = silu(total).astype(BF16)

    last = cum[rows - 1 : rows, :]
    tail_hi, tail_lo = split2(jnp.exp(last - cum) * dt)
    unit_heads = per_step // (2 * PAIR)
    unit_cols = unit_heads * head_dim
    owner = lax.broadcasted_iota(jnp.int32, (8, heads), 0)
    head = lax.broadcasted_iota(jnp.int32, (8, heads), 1)
    dec_hi, dec_lo = split2(jnp.exp(last))
    chosen = jnp.concatenate(
        [jnp.where(head // per_step == owner, v.astype(F32), 0.0) for v in (dec_hi, dec_lo)], axis=0
    ).astype(BF16)
    head = lax.broadcasted_iota(jnp.int32, (heads, unit_cols), 0)
    lane = lax.broadcasted_iota(jnp.int32, (heads, unit_cols), 1)
    same = head % unit_heads == lane // head_dim
    for q in range(2 * PAIR):
        spread = jnp.where(same & ((head % per_step) // unit_heads == q), 1.0, 0.0).astype(BF16)
        dec_ref[q] = jnp.dot(chosen, spread, preferred_element_type=F32).astype(BF16)

    head = lax.broadcasted_iota(jnp.int32, (2 * per_step, width), 0) % per_step
    lane = lax.broadcasted_iota(jnp.int32, (2 * per_step, width), 1) // head_dim
    spread = jnp.where(head == lane, 1.0, 0.0).astype(BF16)

    def widen(i):
        part = slice(i * per_step, (i + 1) * per_step)
        both = jnp.concatenate([tail_hi[:, part], tail_lo[:, part]], axis=1)
        tails[i % 2] = jnp.dot(both, spread, preferred_element_type=F32)

    early = lax.broadcasted_iota(jnp.int32, (8, 128), 0) < RIM
    group = width // PAIR
    widen(0)
    for i in range(steps):
        if i:
            copies[i - 1].wait()
        if i + 1 < steps:
            widen(i + 1)
        for j in range(width // 128):
            cols, lanes = pl.ds(i * width + 128 * j, 128), slice(128 * j, 128 * (j + 1))
            values = x_ref[i - 1, :, lanes] if i else x0_ref[:, lanes]
            total = convolve(
                values, w_ref, bias_ref, i * width + 128 * j, ext.at[j % spare], rows
            )
            prex_ref[:, cols] = total[0:8]
            xj = silu(total).astype(BF16)
            xo_ref[:, cols] = xj
            tail = tails[i % 2, :, lanes]
            top_ref[:, cols] = jnp.where(early, tail[0:8], 0.0)
            tail = jnp.concatenate([jnp.where(early, 0.0, tail[0:8]), tail[8:]], axis=0)
            scaled[i % 2, :, lanes] = (xj.astype(F32) * tail).astype(BF16)
        b_turned = bo_ref[:, i * PAIR * STATE : (i + 1) * PAIR * STATE].T
        for y in range(PAIR):
            local_ref[PAIR * i + y] = jnp.dot(
                b_turned[y * STATE : (y + 1) * STATE, :],
                scaled[i % 2, :, y * group : (y + 1) * group],
                preferred_element_type=F32,
            )


def before_block(near_rim, core_rim, cache):
    device = lax.axis_index(SEQ)
    rim = jnp.where(device % 2 == 1, core_rim.astype(F32), near_rim.astype(F32))
    return jnp.where(device == 0, cache.astype(F32), rim)


def side_kernel(
    bc_ref,
    w_ref,
    bias_ref,
    near_ref,
    core_ref,
    cache_ref,
    cum_ref,
    step_ref,
    after_ref,
    co_ref,
    log_ref,
    row_ref,
    ecum_ref,
    ext,
):
    rows, heads = cum_ref.shape
    side = co_ref.shape[1]
    first = w_ref.shape[1] - side
    spare = ext.shape[0]
    for j in range(side // 128):
        cols = pl.ds(first + 128 * j, 128)
        ext[j % spare, 8 - RIM : 8, :] = before_block(
            near_ref[:, cols], core_ref[:, cols], cache_ref[:, cols]
        )
        values = bc_ref[:, pl.ds(side + 128 * j, 128)]
        total = convolve(values, w_ref, bias_ref, first + 128 * j, ext.at[j % spare], rows)
        co_ref[:, pl.ds(128 * j, 128)] = silu(total).astype(BF16)
    cum, dt = cum_ref[...], step_ref[...]
    log_ref[...] = cum * LOG2E
    log_dt = jnp.where(dt > 0.0, jnp.log(jnp.maximum(dt, 1e-38)) * LOG2E, -1e30)
    row_ref[...] = (cum * LOG2E - log_dt).T
    ecum_hi, ecum_lo = split2(jnp.exp(cum))
    steps, _, twice = ecum_ref.shape
    for i in range(steps):
        part = slice(i * twice // 2, (i + 1) * twice // 2)
        ecum_ref[i] = jnp.concatenate([ecum_hi[:, part], ecum_lo[:, part]], axis=1)


def fix_kernel(
    near_ref,
    core_ref,
    cache_ref,
    w_ref,
    prex_ref,
    preb_ref,
    xc_ref,
    bc_ref,
    top_ref,
    local_ref,
    dec_ref,
    send_ref,
    keep_ref,
    xfix_ref,
    bfix_ref,
    ext,
):
    device = lax.axis_index(SEQ)
    core = device % 2
    inner = xc_ref.shape[1]
    side = bc_ref.shape[1]
    ext[8:, :] = jnp.zeros((8, ext.shape[1]), F32)
    cols = pl.ds(0, ext.shape[1])
    ext[8 - RIM : 8, :] = before_block(near_ref[:, cols], core_ref[:, cols], cache_ref[:, cols])

    def fix(pre, old, dst, first, count):
        cols = pl.ds(first, count)
        total = pre[...]
        for k in range(RIM):
            total = total + ext[pl.ds(8 - RIM + k, 8), cols] * w_ref[k : k + 1, cols]
        fixed = silu(total)
        dst[...] = jnp.concatenate([fixed, old[0:TOP, :].astype(F32)[8:, :]], axis=0).astype(BF16)
        return fixed.astype(BF16).astype(F32)

    x_top = fix(prex_ref, xc_ref, xfix_ref, 0, inner)
    b_top = fix(preb_ref, bc_ref, bfix_ref, inner, side)
    scaled = x_top * top_ref[...]
    scaled = jnp.concatenate([scaled, jnp.zeros_like(scaled)], axis=0).astype(BF16)
    b_top = jnp.concatenate([b_top, jnp.zeros_like(b_top)], axis=0)
    b_turned = b_top.T.astype(BF16)
    groups, _, width = local_ref.shape
    unit = width // 2
    for g in range(groups):
        extra = jnp.dot(
            b_turned[g * STATE : (g + 1) * STATE, :],
            scaled[:, g * width : (g + 1) * width],
            preferred_element_type=F32,
        )
        whole_state = local_ref[g] + extra
        low, high = whole_state[:, :unit], whole_state[:, unit:]
        where = pl.ds((g // PAIR) * STATE, STATE)
        send_ref[g % PAIR, where, :] = jnp.where(core == 0, high, low).astype(BF16)
        keep_ref[g % PAIR, where, :] = jnp.where(core == 0, low, high).astype(BF16)
    where = pl.ds(groups // PAIR * STATE, 16)
    for y in range(PAIR):
        send_ref[y, where, :] = dec_ref[2 * y + 1 - core]
        keep_ref[y, where, :] = dec_ref[2 * y + core]


def cache_kernel(state_hbm, after_ref, out_ref, state_ref, held, sems, *, unit_heads):
    channels, size, heads = state_hbm.shape
    chunks = sems.shape[0]
    count = channels // chunks
    copies = []
    for c in range(chunks):
        part = pl.ds(c * count, count)
        copies.append(pltpu.make_async_copy(state_hbm.at[part], state_ref.at[part], sems.at[c]))
        copies[c].start()
    per_tile = 128 // unit_heads
    quarters = 2 * PAIR
    steps = heads // (quarters * unit_heads)
    quarter = lax.axis_index(SEQ) % quarters
    lane = lax.broadcasted_iota(jnp.int32, (size, 128), 1) // unit_heads
    for channel in range(channels):
        if channel % count == 0:
            copies[channel // count].wait()
        tile, place = channel // per_tile, channel % per_tile
        value = state_ref[channel]
        for i in range(steps):
            start = (i * quarters + quarter) * unit_heads
            moved = pltpu.roll(value, (place * unit_heads - start + heads) % heads, axis=1)
            if place == 0:
                held[tile, i] = moved
            else:
                held[tile, i] = jnp.where(lane == place, moved, held[tile, i])
    unit = out_ref.shape[1]
    dim = unit // unit_heads
    source = lax.broadcasted_iota(jnp.int32, (unit, unit), 0)
    target = lax.broadcasted_iota(jnp.int32, (unit, unit), 1)
    chosen = source == (target % dim) * unit_heads + target // dim
    order = jnp.where(chosen, 1.0, 0.0).astype(BF16)
    for i in range(steps):
        value = jnp.concatenate([held[t, i] for t in range(unit // 128)], axis=1)
        hi = value.astype(BF16)
        rest = value - hi.astype(F32)
        mid = rest.astype(BF16)
        low = (rest - mid.astype(F32)).astype(BF16)
        parts = jnp.dot(
            jnp.concatenate([hi, mid, low], axis=0), order, preferred_element_type=F32
        )
        out_ref[i * size : (i + 1) * size, :] = (
            parts[:size] + parts[size : 2 * size] + parts[2 * size :]
        )


def blocks_of(rows):
    return [(i, slice(i * STATE, (i + 1) * STATE)) for i in range(rows // STATE)]


def core_kernel(keep_ref, recv_ref, send_ref, own_ref):
    device = lax.axis_index(SEQ)
    core, side = device % 2, (device // 2) % 2
    rows = keep_ref.shape[1] - 16
    for out, pick in ((send_ref, 1 - side), (own_ref, side)):
        mine, other = keep_ref.at[pick], recv_ref.at[pick]
        join_totals(mine, other, core == 0, out, rows)


def join_totals(mine, other, mine_first, out, rows):
    d_mine = unpack_decay(mine[rows:, :])
    d_other = unpack_decay(other[rows:, :])
    d_later = jnp.where(mine_first, d_other, d_mine)
    f_mine = jnp.where(mine_first, d_later, 1.0)
    f_other = jnp.where(mine_first, 1.0, d_later)
    for i, part in blocks_of(rows):
        total = mine[part, :].astype(F32) * f_mine[i : i + 1] + other[part, :].astype(F32) * f_other[
            i : i + 1
        ]
        out[part, :] = total.astype(BF16)
    out[rows:, :] = pack_decay(d_mine * d_other)


def total_kernel(mine_ref, other_ref, cache_ref, c_ref, out_ref, *, bit):
    device = lax.axis_index(SEQ)
    rows = mine_ref.shape[0] - 16
    join_totals(mine_ref, other_ref, (device // bit) % 2 == 0, out_ref, rows)


def prefix_kernel(mine_ref, other_ref, pre_ref, dpre_ref, out_ref, opre_ref, odpre_ref, *, bit):
    device = lax.axis_index(SEQ)
    rows = mine_ref.shape[0] - 16
    first = (device // bit) % 2 == 0
    join_totals(mine_ref, other_ref, first, out_ref, rows)
    d_other = unpack_decay(other_ref[rows:, :])
    d_pre = dpre_ref[...]
    gain = jnp.where(first, 0.0, d_pre)
    for i, part in blocks_of(rows):
        opre_ref[part, :] = pre_ref[part, :] + gain[i : i + 1] * other_ref[part, :].astype(F32)
    odpre_ref[...] = jnp.where(first, d_pre, d_pre * d_other)


def start_kernel(mine_ref, other_ref, after_ref, out_ref, opre_ref, odpre_ref, *, bit):
    device = lax.axis_index(SEQ)
    rows = mine_ref.shape[0] - 16
    first = (device // bit) % 2 == 0
    join_totals(mine_ref, other_ref, first, out_ref, rows)
    d_other = unpack_decay(other_ref[rows:, :])
    opre_ref[...] = jnp.where(first, 0.0, other_ref[:rows, :].astype(F32))
    odpre_ref[...] = jnp.where(first, 1.0, d_other)


def enter_kernel(
    mine_ref,
    other_ref,
    pre_ref,
    dpre_ref,
    cache_ref,
    own_ref,
    recv_ref,
    after_ref,
    send_ref,
    stay_ref,
    fin_ref,
    *,
    bit,
):
    device = lax.axis_index(SEQ)
    side = (device // 2) % 2
    rows = mine_ref.shape[0] - 16
    first = (device // bit) % 2 == 0
    d_mine = unpack_decay(mine_ref[rows:, :])
    d_other = unpack_decay(other_ref[rows:, :])
    d_later = jnp.where(first, d_other, d_mine)
    f_mine = jnp.where(first, d_later, 1.0)
    f_other = jnp.where(first, 1.0, d_later)
    d_all = d_mine * d_other
    d_pre = dpre_ref[...]
    gain = jnp.where(first, 0.0, d_pre)
    d_before = jnp.where(first, d_pre, d_pre * d_other)
    d_first = jnp.where(side == 0, unpack_decay(own_ref[rows:, :]), unpack_decay(recv_ref[rows:, :]))
    for i, part in blocks_of(rows):
        cache = cache_ref[part, :]
        other = other_ref[part, :].astype(F32)
        mine = mine_ref[part, :].astype(F32)
        row = slice(i, i + 1)
        fin_ref[part, :] = d_all[row] * cache + mine * f_mine[row] + other * f_other[row]
        plane = d_before[row] * cache + pre_ref[part, :] + gain[row] * other
        t_first = jnp.where(side == 0, own_ref[part, :].astype(F32), recv_ref[part, :].astype(F32))
        second = d_first[row] * plane + t_first
        send_ref[part, :] = jnp.where(side == 0, second, plane).astype(BF16)
        stay_ref[part, :] = jnp.where(side == 0, plane, second).astype(BF16)


def chip_kernel(stay_ref, recv_ref, keep_ref, part_ref, gate_ref, grow_ref, send_ref):
    enter_block(stay_ref, recv_ref, keep_ref, part_ref, send_ref, lax.axis_index(SEQ) % 2 == 1)


def block_kernel(stay_ref, recv_ref, keep_ref, part_ref, after_ref, own_ref):
    enter_block(stay_ref, recv_ref, keep_ref, part_ref, own_ref, lax.axis_index(SEQ) % 2 == 0)


def enter_block(stay_ref, recv_ref, keep_ref, part_ref, out_ref, first):
    device = lax.axis_index(SEQ)
    core, side = device % 2, (device // 2) % 2
    rows = stay_ref.shape[0]

    def fill(values):
        for y in range(PAIR):
            for mine, source in ((True, stay_ref), (False, recv_ref)):

                @pl.when((side == y) == mine)
                def _(y=y, source=source):
                    values(y, source)

    @pl.when(first)
    def _():
        def values(y, source):
            out_ref[y] = source[...]

        fill(values)

    for kept, local in ((0, keep_ref), (1, part_ref)):

        @pl.when(jnp.logical_not(first) & (core == kept))
        def _(local=local):
            def values(y, source):
                decay = unpack_decay(local[y, rows:, :])
                for i, part in blocks_of(rows):
                    entered = decay[i : i + 1] * source[part, :].astype(F32)
                    out_ref[y, part, :] = (entered + local[y, part, :].astype(F32)).astype(BF16)

            fill(values)


def diag_kernel(
    xc_ref,
    xfix_ref,
    b_ref,
    bfix_ref,
    c_ref,
    cum_ref,
    row_ref,
    skip_ref,
    after_ref,
    out_ref,
    *,
    head_dim,
    first,
):
    rows = xc_ref.shape[0]
    heads = cum_ref.shape[1]
    per_group = heads // GROUPS
    below = lax.broadcasted_iota(jnp.int32, (rows, rows), 0)
    across = lax.broadcasted_iota(jnp.int32, (rows, rows), 1)
    mask = below >= across
    quad = 128 // head_dim
    lane = lax.broadcasted_iota(jnp.int32, (rows, 128), 1) // head_dim
    for g in range(out_ref.shape[1] // (per_group * head_dim)):
        part = slice((first + g) * STATE, (first + g + 1) * STATE)
        b_all = jnp.concatenate([bfix_ref[:, part], b_ref[TOP:, part]], axis=0)
        c_dot_b = lax.dot_general(
            c_ref[:, part], b_all, (((1,), (1,)), ((), ())), preferred_element_type=F32
        )
        for q in range(per_group // quad):
            base = (first + g) * per_group + q * quad
            cols = pl.ds(base * head_dim, 128)
            x_quad = jnp.concatenate([xfix_ref[:, cols], xc_ref[TOP:, cols]], axis=0)
            lhs, rhs = [], []
            for k in range(quad):
                head = base + k
                gap = cum_ref[:, head : head + 1] - row_ref[head : head + 1, :]
                decay = jnp.exp2(jnp.where(mask, gap, -1e30))
                lhs.append((c_dot_b * decay).astype(BF16))
                rhs.append(jnp.where(lane == k, x_quad, jnp.zeros_like(x_quad)))
            skip = skip_ref[:, base : base + 1]
            for k in range(1, quad):
                skip = jnp.where(lane[0:1] == k, skip_ref[:, base + k : base + k + 1], skip)
            inner = jnp.dot(
                jnp.concatenate(lhs, axis=1),
                jnp.concatenate(rhs, axis=0),
                preferred_element_type=F32,
            )
            out = pl.ds((g * per_group + q * quad) * head_dim, 128)
            out_ref[:, out] = inner + skip * x_quad.astype(F32)


def gate_kernel(len_ref, z_ref, after_ref, gate_ref):
    rows, width = z_ref.shape
    first = lax.axis_index(SEQ) * rows
    live = first + lax.broadcasted_iota(jnp.int32, (rows, 128), 0) < len_ref[0]
    for j in range(width // 128):
        cols = pl.ds(128 * j, 128)
        gate_ref[:, cols] = jnp.where(live, silu(z_ref[:, cols].astype(F32)), 0.0)


def grow_kernel(ecum_ref, final_ref, grow_ref, mine_ref, *, head_dim):
    steps = ecum_ref.shape[0]
    per_step = ecum_ref.shape[2] // 2
    width = per_step * head_dim
    head = lax.broadcasted_iota(jnp.int32, (2 * per_step, width), 0) % per_step
    lane = lax.broadcasted_iota(jnp.int32, (2 * per_step, width), 1)
    spread = jnp.where(head == lane // head_dim, 1.0, 0.0).astype(BF16)
    for i in range(steps):
        grow_ref[:, i * width : (i + 1) * width] = jnp.dot(
            ecum_ref[i], spread, preferred_element_type=F32
        )
    step = (lax.axis_index(SEQ) // (2 * PAIR)) % (final_ref.shape[0] // STATE)
    mine = final_ref[pl.ds(pl.multiple_of(step * STATE, STATE), STATE), :]
    mine_ref[...] = mine.T


def out_kernel(
    *refs,
    parts,
):
    diag_refs, refs = refs[:parts], refs[parts:]
    gate_ref, grow_ref, c_ref, own_ref, recv_ref, gain_ref, out_ref, held, sems = refs
    core = lax.axis_index(SEQ) % 2
    steps, _, width = held.shape
    unit = width // (2 * PAIR)
    side = PAIR * STATE
    copies = []
    for i in range(steps):
        c_all = c_ref[:, i * side : (i + 1) * side]
        for y in range(PAIR):
            own = own_ref[y, i * STATE : (i + 1) * STATE, :]
            recv = recv_ref[y, i * STATE : (i + 1) * STATE, :]
            state = jnp.concatenate(
                [jnp.where(core == 0, own, recv), jnp.where(core == 0, recv, own)], axis=1
            )
            first = i * width + 2 * y * unit
            cols = slice(first, first + 2 * unit)
            entering = jnp.dot(
                c_all[:, y * STATE : (y + 1) * STATE], state, preferred_element_type=F32
            )
            held_cols = diag_refs[0].shape[1]
            diag = diag_refs[first // held_cols]
            first = first % held_cols
            y_all = diag[:, first : first + 2 * unit] + grow_ref[:, cols] * entering
            gated = y_all.astype(BF16).astype(F32) * gate_ref[:, cols]
            scale = lax.rsqrt(jnp.mean(gated * gated, axis=1, keepdims=True) + 1e-05)
            held[i, :, 2 * y * unit : 2 * (y + 1) * unit] = (
                gated * scale * gain_ref[:, cols]
            ).astype(BF16)
        copy = pltpu.make_async_copy(
            held.at[i], out_ref.at[:, pl.ds(i * width, width)], sems.at[i]
        )
        copy.start()
        copies.append(copy)
    for copy in copies:
        copy.wait()


def swap(value, mask):
    devices = range(lax.axis_size(SEQ))
    return lax.ppermute(value, SEQ, [(i, i ^ mask) for i in devices])


def chip_route(count):
    route = {i: i + 1 for i in range(1, count - 1, 2)}
    route.update({i: i - 1 for i in range(4, count - 2, 2)})
    route.update({2: 0, 0: 1, count - 2: count - 1, count - 1: count - 3})
    return sorted(route.items())


def near(shape, dtype):
    return pltpu.VMEM(shape, dtype)


VMEM_SPEC = pl.BlockSpec(memory_space=pltpu.VMEM)
ANY_SPEC = pl.BlockSpec(memory_space=pl.ANY)


def plain_call(
    body, out_shape, *args, smem=(), far=(), after=(), mib=12, nbytes=2**20, scratch=(), out_specs=None
):
    return pl.pallas_call(
        body,
        out_shape=out_shape,
        in_specs=[pl.BlockSpec(memory_space=pltpu.SMEM)] * len(smem)
        + [ANY_SPEC] * len(far)
        + [VMEM_SPEC] * len(args) + [ANY_SPEC] * len(after),
        out_specs=out_specs or jax.tree.map(lambda _: VMEM_SPEC, out_shape),
        scratch_shapes=list(scratch),
        compiler_params=pltpu.CompilerParams(vmem_limit_bytes=mib * 2**20),
        cost_estimate=pl.CostEstimate(flops=0, bytes_accessed=nbytes, transcendentals=0),
    )(*smem, *[pltpu.with_memory_space_constraint(a, pltpu.HBM) for a in far], *args, *after)


def body(
    x_in,
    bc_in,
    z_in,
    dt_in,
    conv_weight,
    conv_bias,
    dt_bias,
    a_log,
    d_skip,
    norm_gain,
    conv_cache,
    cache_state,
    lengths,
):
    rows, inner = x_in.shape
    heads = dt_in.shape[1]
    head_dim = inner // heads
    devices = lax.axis_size(SEQ)
    index = lax.axis_index(SEQ)
    share = heads // devices
    steps = GROUPS // PAIR
    per_step = heads // steps
    width = inner // steps
    side = GROUPS * STATE
    unit = width // (2 * PAIR)
    unit_heads = unit // head_dim
    state_rows = steps * STATE
    msg_rows = state_rows + 16
    dma = pltpu.SemaphoreType.DMA

    fetched = [
        bc_in,
        conv_weight,
        conv_bias.reshape(1, -1),
        dt_in,
        dt_bias.reshape(1, -1),
        a_log.reshape(1, -1),
    ]
    rim, *ready = plain_call(
        functools.partial(rim_kernel, count=len(fetched)),
        [near((RIM, inner + 2 * side), BF16), near((rows, width), BF16)]
        + [near(a.shape, a.dtype) for a in fetched],
        far=(x_in, bc_in, *fetched),
        mib=4,
        scratch=[
            pltpu.VMEM((TOP, inner), BF16),
            pltpu.VMEM((TOP, 2 * side), BF16),
            dma((3 + len(fetched),)),
        ],
    )
    near_rim = lax.ppermute(rim, SEQ, chip_route(devices))
    core_rim = swap(rim, 1)

    xc, bc, prex, preb, cum, step_size, dec, top, local = plain_call(
        functools.partial(conv_kernel, heads=heads, head_dim=head_dim),
        (
            near((rows, inner), BF16),
            near((rows, side), BF16),
            near((8, inner), F32),
            near((8, side), F32),
            near((rows, heads), F32),
            near((rows, heads), F32),
            near((2 * PAIR, 16, unit), BF16),
            near((8, inner), F32),
            near((GROUPS, STATE, width // PAIR), F32),
        ),
        *ready,
        smem=(lengths,),
        far=(x_in,),
        after=(rim,),
        scratch=[
            pltpu.VMEM((steps - 1, rows, width), BF16),
            pltpu.VMEM((4, 8 + rows, 128), F32),
            pltpu.VMEM((2, rows, width), F32),
            pltpu.VMEM((2, rows, width), BF16),
            dma((steps - 1,)),
        ],
        mib=16,
        nbytes=4 * 2**20,
    )

    pair_msg = near((PAIR, msg_rows, unit), BF16)
    send, keep, xfix, bfix = plain_call(
        fix_kernel,
        (pair_msg, pair_msg, near((TOP, inner), BF16), near((TOP, side), BF16)),
        near_rim,
        core_rim,
        conv_cache,
        ready[2],
        prex,
        preb,
        xc,
        bc,
        top,
        local,
        dec,
        scratch=[pltpu.VMEM((16, inner + side), F32)],
    )

    message = near((msg_rows, unit), BF16)
    part = swap(send, 1)
    send_y, own = plain_call(core_kernel, (message, message), keep, part)
    recv = swap(send_y, 2)
    chunks = 4
    cache = plain_call(
        functools.partial(cache_kernel, unit_heads=unit_heads),
        near((state_rows, unit), F32),
        far=(cache_state.transpose(1, 2, 0),),
        after=(own,),
        scratch=[
            pltpu.VMEM((head_dim, STATE, heads), F32),
            pltpu.VMEM((unit // 128, steps, STATE, 128), F32),
            dma((chunks,)),
        ],
        nbytes=2 * 2**20,
    )
    cc, log_cum, row, ecum = plain_call(
        side_kernel,
        (
            near((rows, side), BF16),
            near((rows, heads), F32),
            near((heads, rows), F32),
            near((steps, rows, 2 * per_step), BF16),
        ),
        ready[1],
        ready[2],
        ready[3],
        near_rim,
        core_rim,
        conv_cache,
        cum,
        step_size,
        after=(own,),
        scratch=[pltpu.VMEM((4, 8 + rows, 128), F32)],
    )
    total = plain_call(
        functools.partial(total_kernel, bit=2), message, own, recv, after=(cache, cc)
    )

    def diag_part(k, order):
        return plain_call(
            functools.partial(diag_kernel, head_dim=head_dim, first=k * GROUPS // 2),
            near((rows, inner // 2), F32),
            xc,
            xfix,
            bc,
            bfix,
            cc,
            log_cum,
            row,
            d_skip.reshape(1, -1),
            after=(order,),
            nbytes=4 * 2**20,
        )

    diags = [diag_part(0, total)]
    pre = None
    bit = 4
    pre_shape = (near((state_rows, unit), F32), near((8, unit), F32))
    while 2 * bit < devices:
        other = swap(total, 2 * bit - 4)
        if pre is None:
            total, *pre = plain_call(
                functools.partial(start_kernel, bit=bit),
                (message,) + pre_shape,
                total,
                other,
                after=(diags[0],),
            )
        else:
            total, *pre = plain_call(
                functools.partial(prefix_kernel, bit=bit), (message,) + pre_shape, total, other, *pre
            )
        bit *= 2
    if pre is None:
        pre = [jnp.zeros((state_rows, unit), F32), jnp.ones((8, unit), F32)]
    last = total
    other = swap(last, 2 * bit - 4)
    diags.append(diag_part(1, last))
    state_out = near((state_rows, unit), BF16)
    send_y, stay, final = plain_call(
        functools.partial(enter_kernel, bit=bit),
        (state_out, state_out, near((state_rows, unit), F32)),
        total,
        other,
        *pre,
        cache,
        own,
        recv,
        after=(diags[1],),
    )
    recv_y = swap(send_y, 2)
    grow, mine = plain_call(
        functools.partial(grow_kernel, head_dim=head_dim),
        (near((rows, inner), F32), jax.ShapeDtypeStruct((unit, STATE), F32)),
        ecum,
        final,
        nbytes=5 * 2**20,
    )
    gate = plain_call(
        gate_kernel, near((rows, inner), F32), z_in, smem=(lengths,), after=(final,)
    )
    half = near((PAIR, state_rows, unit), BF16)
    send_c = plain_call(chip_kernel, half, stay, recv_y, keep, part, after=(gate, grow))
    enter_recv = swap(send_c, 1)
    enter_own = plain_call(block_kernel, half, stay, recv_y, keep, part, after=(send_c,))

    mixed = plain_call(
        functools.partial(out_kernel, parts=len(diags)),
        jax.ShapeDtypeStruct((rows, inner), BF16),
        *diags,
        gate,
        grow,
        cc,
        enter_own,
        enter_recv,
        norm_gain.reshape(1, -1),
        out_specs=ANY_SPEC,
        scratch=[pltpu.VMEM((steps, rows, width), BF16), dma((steps,))],
        mib=16,
        nbytes=4 * 2**20,
    )

    if share * head_dim == unit and devices == 2 * PAIR * steps:
        mine = mine.reshape(share, head_dim, STATE)
    else:
        around = [[4 * i + j for j in range(4)] for i in range(devices // 4)]
        every = final.reshape(steps, STATE, unit)
        every = lax.all_gather(every, SEQ, axis=1, axis_index_groups=around)
        every = every.reshape(steps * 2 * PAIR, STATE, unit).transpose(0, 2, 1)
        every = every.reshape(heads, head_dim, STATE)
        mine = lax.dynamic_slice_in_dim(every, index * share, share, 0)
    return (mixed, mine)


def solution(mesh):
    in_specs = (
        P(("groups", "seq"), None),
        P(("groups", "seq"), None),
        P(("groups", "seq"), None),
        P(("groups", "seq"), None),
        P(),
        P(),
        P(),
        P(),
        P(),
        P(),
        P("groups", None),
        P("groups", None, None),
        P("groups"),
    )
    out_specs = (P(("groups", "seq"), None), P(("groups", "seq"), None, None))
    return jax.shard_map(body, mesh=mesh, in_specs=in_specs, out_specs=out_specs, check_vma=False)
```

time: 40.6 us -> 38.5 us (0.948)
  Pallas kernels: 20 us -> 15.3 us
  starting transfers between devices: 9.79 us -> 11.6 us
  waiting for transfers between devices: 8.96 us -> 9.94 us
    pallas_call x13 -> x16, Pallas kernels: 20 us -> 15.3 us  [plain_call(): pl.pallas_call(body, out_shape=out_shape, in_specs=[pl.BlockSpec(memory_s...]
    ppermute x6 -> x7, starting transfers between devices: 9.29 us -> 11.5 us  [swap(): return lax.ppermute(value, SEQ, [(i, i ^ mask) for i in devices])]
    ppermute x6 -> x7, waiting for transfers between devices: 7.95 us -> 9.75 us  [swap(): return lax.ppermute(value, SEQ, [(i, i ^ mask) for i in devices])]
    ppermute x1, waiting for transfers between devices: 1 us -> 0.19 us  [body(): near_rim = lax.ppermute(rim, SEQ, chip_route(devices))]
    ppermute x1, starting transfers between devices: 0.5 us -> 0.07 us  [body(): near_rim = lax.ppermute(rim, SEQ, chip_route(devices))]
  transfers between devices with their start and end apart: 7 -> 8, of which waited for: 6 -> 7; matrix products, arithmetic and copies ran while one was open for 0% -> 0% of each run, Pallas kernels for 40% -> 30%
where the time goes in v3:
time: 38.5 us; the launch traced here: 38.3 us
  Pallas kernels  15.3 us (40%)
  starting transfers between devices  11.6 us (30%)
  waiting for transfers between devices  9.94 us (26%)
  between operations  1.42 us (4%)
    pallas_call x16, Pallas kernels, plain_call(): pl.pallas_call(body, out_shape=out_shape, in_specs=[pl.BlockSpec(memory_s...  15.3 us
    ppermute x7, starting transfers between devices, swap(): return lax.ppermute(value, SEQ, [(i, i ^ mask) for i in devices])  11.5 us
    ppermute x7, waiting for transfers between devices, swap(): return lax.ppermute(value, SEQ, [(i, i ^ mask) for i in devices])  9.75 us
  transfers between devices with their start and end apart: 8, of which 7 were waited for; matrix products, arithmetic and copies ran while one was open for 0% of the time, Pallas kernels for 30%

profile of v3, /device:TPU:0, one launch (start us, length us, event | category | flops | bytes accessed | tf_op | source)
XLA Modules:
  0.0 38.3 jit_solution(5180304779496577422)
XLA Ops:
  0.6 0.0 copy-start.1
  0.6 1.2 %shard_map.140 = (bf16[3,5120]{1,0:T(4,128)(2,1)S(1)}, bf16[128,1024]{1,0:T(8,128)(2,1)S(1)}, bf16[128,1024]{1,0:T(8,128)(2,1)S(1)}, f32[4,5120]{1,0:T(4,128)S(1...) custom-call(bf16[128,4096]{1,0:T(8,128)(2,1)} %x_hbm.1, ...), custom_call_target="tpu_custom_call" | custom-call | bytes 1048576 | tf_op jit(solution)/shard_map/pallas_call | solution.py:628
  1.9 0.5 %collective-permute-start.1 = (bf16[3,5120]{1,0:T(4,128)(2,1)S(1)}, bf16[3,5120]{1,0:T(4,128)(2,1)S(1)}, u32[]{:S(2)}, u32[]{:S(2)}) collective-permute-start(bf16[3,5120]{1,0:T(4,128)(2,1)S(1)} %get-tuple-element.44.after_ref), channel_id=1, source_target_pairs={{0,1},{1,0},{2,3},{3,2},{4,5},{5,4},{6,7},{7,6},{8,9},{9,8},{10,11... | collective-permute-start | bytes 92168 | tf_op jit(solution)/shard_map/ppermute | solution.py:607
  2.4 0.1 collective-permute-start
  3.1 3.6 %shard_map.141 = (bf16[128,4096]{1,0:T(8,128)(2,1)S(1)}, bf16[128,512]{1,0:T(8,128)(2,1)S(1)}, f32[8,4096]{1,0:T(8,128)S(1)}, f32[8,512]{1,0:T(8,128)S(1)}, f32[...) custom-call(s32[1]{0:T(128)S(6)} %copy.15.len_ref, ...), custom_call_target="tpu_custom_call" | custom-call | bytes 4194304 | tf_op jit(solution)/shard_map/pallas_call | solution.py:628
  6.8 0.0 collective-permute-done.1.core_ref
  6.8 0.2 collective-permute-done.near_ref
  7.0 0.0 copy-done.1
  7.0 0.4 %shard_map.142 = (bf16[2,272,256]{2,1,0:T(8,128)(2,1)S(1)}, bf16[2,272,256]{2,1,0:T(8,128)(2,1)S(1)}, bf16[16,4096]{1,0:T(8,128)(2,1)S(1)}, bf16[16,512]{1,0:T(8,128)(2,1)S(1)}) custom-call(bf16[3,5120]{1,0:T(4,128)(2,1)S(1)} %collective-permute-done.near_ref, bf16[3,5120]{1,0:T(4,128)(2,1)S(1)} %collective-permute-done.1.core_ref, ...), custom_call_target="tpu_custom_call" | custom-call | bytes 1048576 | tf_op jit(solution)/shard_map/pallas_call | solution.py:628
  7.4 0.0 copy-start.3
  7.4 2.5 %collective-permute-start.2 = (bf16[2,272,256]{2,1,0:T(8,128)(2,1)S(1)}, bf16[2,272,256]{2,1,0:T(8,128)(2,1)S(1)}, u32[]{:S(2)}, u32[]{:S(2)}) collective-permute-start(bf16[2,272,256]{2,1,0:T(8,128)(2,1)S(1)} %get-tuple-element.57), channel_id=1, source_target_pairs={{0,1},{1,0},{2,3},{3,2},{4,5},{5,4},{6,7},{7,6},{8,9},{9,8},{10,11... | collective-permute-start | bytes 835592 | tf_op jit(solution)/shard_map/ppermute | solution.py:607
  9.9 1.2 %collective-permute-done.2.recv_ref.part_ref = bf16[2,272,256]{2,1,0:T(8,128)(2,1)S(1)} collective-permute-done((bf16[2,272,256]{2,1,0:T(8,128)(2,1)S(1)}, bf16[2,272,256]{2,1,0:T(8,128)(2,1)S(1)}, u32[]{:S(2)}, u32[]{:S(2)}) %collective-permute-start.2) | collective-permute-done | bytes 278560 | tf_op jit(solution)/shard_map/ppermute | solution.py:607
  11.1 0.1 shard_map.143
  11.2 1.6 %collective-permute-start.3 = (bf16[272,256]{1,0:T(8,128)(2,1)S(1)}, bf16[272,256]{1,0:T(8,128)(2,1)S(1)}, u32[]{:S(2)}, u32[]{:S(2)}) collective-permute-start(bf16[272,256]{1,0:T(8,128)(2,1)S(1)} %get-tuple-element.62), channel_id=1, source_target_pairs={{0,2},{1,3},{2,0},{3,1},{4,6},{5,7},{6,4},{7,5},{8,10},{9,11},{10,... | collective-permute-start | bytes 417800 | tf_op jit(solution)/shard_map/ppermute | solution.py:607
  12.8 2.5 %shard_map.145.cache_ref = f32[256,256]{1,0:T(8,128)S(1)} custom-call(f32[32,64,128]{2,1,0:T(8,128)} %bitcast.10, bf16[272,256]{1,0:T(8,128)(2,1)S(1)} %get-tuple-element.58.after_ref.mine_ref.own_ref), custom_call_target="tpu_custom_call" | custom-call | bytes 2097152 | tf_op jit(solution)/shard_map/pallas_call | solution.py:628
  15.4 0.2 shard_map.144
  15.6 1.6 %collective-permute-done.3.other_ref.recv_ref = bf16[272,256]{1,0:T(8,128)(2,1)S(1)} collective-permute-done((bf16[272,256]{1,0:T(8,128)(2,1)S(1)}, bf16[272,256]{1,0:T(8,128)(2,1)S(1)}, u32[]{:S(2)}, u32[]{:S(2)}) %collective-permute-start.3) | collective-permute-done | bytes 139296 | tf_op jit(solution)/shard_map/ppermute | solution.py:607
  17.2 0.1 shard_map.146.after_ref.mine_ref
  17.3 1.6 %collective-permute-start.4 = (bf16[272,256]{1,0:T(8,128)(2,1)S(1)}, bf16[272,256]{1,0:T(8,128)(2,1)S(1)}, u32[]{:S(2)}, u32[]{:S(2)}) collective-permute-start(bf16[272,256]{1,0:T(8,128)(2,1)S(1)} %shard_map.146.after_ref.mine_ref), channel_id=1, source_target_pairs={{0,4},{1,5},{2,6},{3,7},{4,0},{5,1},{6,2},{7,3},{8,12},{9,13},{10,... | collective-permute-start | bytes 417800 | tf_op jit(solution)/shard_map/ppermute | solution.py:607
  19.0 0.0 copy-done.3
  19.0 1.8 %shard_map.147.after_ref.refs_0_ = f32[128,2048]{1,0:T(8,128)S(1)} custom-call(bf16[128,4096]{1,0:T(8,128)(2,1)S(1)} %get-tuple-element.45.xc_ref, bf16[16,4096]{1,0:T(8,128)(2,1)S(1)} %get-tuple-element.52.xfix_ref, bf16[128,512]{1,0:T(8,128)(2,1)S(1)} %get-tuple-element.48.bc_ref.b_ref, bf16[16,512]{1,0:T(8,128)(2,1)S(1)} %get-tuple-element.53.bfix_ref, ...), custom_call_target="tpu_custom_call" | custom-call | bytes 4194304 | tf_op jit(solution)/shard_map/pallas_call | solution.py:628
  20.7 1.8 %collective-permute-done.4.other_ref = bf16[272,256]{1,0:T(8,128)(2,1)S(1)} collective-permute-done((bf16[272,256]{1,0:T(8,128)(2,1)S(1)}, bf16[272,256]{1,0:T(8,128)(2,1)S(1)}, u32[]{:S(2)}, u32[]{:S(2)}) %collective-permute-start.4) | collective-permute-done | bytes 139296 | tf_op jit(solution)/shard_map/ppermute | solution.py:607
  22.5 0.1 shard_map.148
  22.6 0.0 copy-start
  22.6 3.6 %collective-permute-start.5 = (bf16[272,256]{1,0:T(8,128)(2,1)S(1)}, bf16[272,256]{1,0:T(8,128)(2,1)S(1)}, u32[]{:S(2)}, u32[]{:S(2)}) collective-permute-start(bf16[272,256]{1,0:T(8,128)(2,1)S(1)} %get-tuple-element.63.after_ref.mine_ref), channel_id=1, source_target_pairs={{0,12},{1,13},{2,14},{3,15},{4,8},{5,9},{6,10},{7,11},{8,4},{9,5},... | collective-permute-start | bytes 417800 | tf_op jit(solution)/shard_map/ppermute | solution.py:607
  26.2 1.8 %shard_map.149.after_ref.refs_1_ = f32[128,2048]{1,0:T(8,128)S(1)} custom-call(bf16[128,4096]{1,0:T(8,128)(2,1)S(1)} %get-tuple-element.45.xc_ref, bf16[16,4096]{1,0:T(8,128)(2,1)S(1)} %get-tuple-element.52.xfix_ref, bf16[128,512]{1,0:T(8,128)(2,1)S(1)} %get-tuple-element.48.bc_ref.b_ref, bf16[16,512]{1,0:T(8,128)(2,1)S(1)} %get-tuple-element.53.bfix_ref, ...), custom_call_target="tpu_custom_call" | custom-call | bytes 4194304 | tf_op jit(solution)/shard_map/pallas_call | solution.py:628
  28.0 1.7 %collective-permute-done.5.other_ref = bf16[272,256]{1,0:T(8,128)(2,1)S(1)} collective-permute-done((bf16[272,256]{1,0:T(8,128)(2,1)S(1)}, bf16[272,256]{1,0:T(8,128)(2,1)S(1)}, u32[]{:S(2)}, u32[]{:S(2)}) %collective-permute-start.5) | collective-permute-done | bytes 139296 | tf_op jit(solution)/shard_map/ppermute | solution.py:607
  29.7 0.2 shard_map.150
  29.9 1.6 %collective-permute-start.6 = (bf16[256,256]{1,0:T(8,128)(2,1)S(1)}, bf16[256,256]{1,0:T(8,128)(2,1)S(1)}, u32[]{:S(2)}, u32[]{:S(2)}) collective-permute-start(bf16[256,256]{1,0:T(8,128)(2,1)S(1)} %get-tuple-element.70), channel_id=1, source_target_pairs={{0,2},{1,3},{2,0},{3,1},{4,6},{5,7},{6,4},{7,5},{8,10},{9,11},{10,... | collective-permute-start | bytes 393224 | tf_op jit(solution)/shard_map/ppermute | solution.py:607
  31.5 0.0 copy-done
  31.5 0.4 %shard_map.151.gate_ref.refs_2_ = f32[128,4096]{1,0:T(8,128)S(1)} custom-call(s32[1]{0:T(128)S(6)} %copy.15.len_ref, bf16[128,4096]{1,0:T(8,128)(2,1)S(1)} %copy-done, f32[256,256]{1,0:T(8,128)S(1)} %get-tuple-element.66.after_ref.final_ref), custom_call_target="tpu_custom_call" | custom-call | bytes 1048576 | tf_op jit(solution)/shard_map/pallas_call | solution.py:628
  31.9 1.0 %shard_map.152 = (f32[128,4096]{1,0:T(8,128)S(1)}, f32[256,64]{1,0:T(8,128)}) custom-call(bf16[4,128,64]{2,1,0:T(8,128)(2,1)S(1)} %get-tuple-element.67.ecum_ref, f32[256,256]{1,0:T(8,128)S(1)} %get-tuple-element.66.after_ref.final_ref), custom_call_target="tpu_custom_call" | custom-call | bytes 5242880 | tf_op jit(solution)/shard_map/pallas_call | solution.py:628
  32.9 2.0 %collective-permute-done.6.recv_ref = bf16[256,256]{1,0:T(8,128)(2,1)S(1)} collective-permute-done((bf16[256,256]{1,0:T(8,128)(2,1)S(1)}, bf16[256,256]{1,0:T(8,128)(2,1)S(1)}, u32[]{:S(2)}, u32[]{:S(2)}) %collective-permute-start.6) | collective-permute-done | bytes 131104 | tf_op jit(solution)/shard_map/ppermute | solution.py:607
  34.9 0.0 copy-start.2
  34.9 0.1 shard_map.153.after_ref
  35.0 0.1 collective-permute-start.7
  35.1 0.1 shard_map.154.refs_5_
  35.2 1.5 %collective-permute-done.7.refs_6_ = bf16[2,256,256]{2,1,0:T(8,128)(2,1)S(1)} collective-permute-done((bf16[2,256,256]{2,1,0:T(8,128)(2,1)S(1)}, bf16[2,256,256]{2,1,0:T(8,128)(2,1)S(1)}, u32[]{:S(2)}, u32[]{:S(2)}) %collective-permute-start.7) | collective-permute-done | bytes 262176 | tf_op jit(solution)/shard_map/ppermute | solution.py:607
  36.6 0.0 copy-done.2
  36.6 1.7 %shard_map.155 = bf16[128,4096]{1,0:T(8,128)(2,1)} custom-call(f32[128,2048]{1,0:T(8,128)S(1)} %shard_map.147.after_ref.refs_0_, f32[128,2048]{1,0:T(8,128)S(1)} %shard_map.149.after_ref.refs_1_, f32[128,4096]{1,0:T(8,128)S(1)} %shard_map.151.gate_ref.refs_2_, f32[128,4096]{1,0:T(8,128)S(1)} %get-tuple-element.68.grow_ref.refs_3_, ...), custom_call_target="tpu_custom_call" | custom-call | bytes 4194304 | tf_op jit(solution)/shard_map/pallas_call | solution.py:628
Async XLA Ops:
  0.6 6.3 %copy-start.1 = (bf16[3,5120]{1,0:T(4,128)(2,1)S(1)}, bf16[3,5120]{1,0:T(4,128)(2,1)}, u32[]{:S(2)}) copy-start(bf16[3,5120]{1,0:T(4,128)(2,1)} %cache_ref.3) | copy-start | bytes 92164
  1.9 4.9 %collective-permute-start.1 = (bf16[3,5120]{1,0:T(4,128)(2,1)S(1)}, bf16[3,5120]{1,0:T(4,128)(2,1)S(1)}, u32[]{:S(2)}, u32[]{:S(2)}) collective-permute-start(bf16[3,5120]{1,0:T(4,128)(2,1)S(1)} %get-tuple-element.44.after_ref), channel_id=1, source_target_pairs={{0,1},{1,0},{2,3},{3,2},{4,5},{5,4},{6,7},{7,6},{8,9},{9,8},{10,11... | collective-permute-start | bytes 92168 | tf_op jit(solution)/shard_map/ppermute | solution.py:607
  2.4 4.6 %collective-permute-start = (bf16[3,5120]{1,0:T(4,128)(2,1)S(1)}, bf16[3,5120]{1,0:T(4,128)(2,1)S(1)}, u32[]{:S(2)}, u32[]{:S(2)}) collective-permute-start(bf16[3,5120]{1,0:T(4,128)(2,1)S(1)} %get-tuple-element.44.after_ref), channel_id=1, source_target_pairs={{0,1},{1,2},{2,0},{3,4},{4,3},{5,6},{6,5},{7,8},{8,7},{9,10},{10,9... | collective-permute-start | bytes 92168 | tf_op jit(solution)/shard_map/ppermute | solution.py:692
  7.4 11.6 %copy-start.3 = (f32[128]{0:T(128)S(1)}, f32[128]{0:T(128)}, u32[]{:S(2)}) copy-start(f32[128]{0:T(128)} %param.21) | copy-start | bytes 1540
  7.4 3.7 %collective-permute-start.2 = (bf16[2,272,256]{2,1,0:T(8,128)(2,1)S(1)}, bf16[2,272,256]{2,1,0:T(8,128)(2,1)S(1)}, u32[]{:S(2)}, u32[]{:S(2)}) collective-permute-start(bf16[2,272,256]{2,1,0:T(8,128)(2,1)S(1)} %get-tuple-element.57), channel_id=1, source_target_pairs={{0,1},{1,0},{2,3},{3,2},{4,5},{5,4},{6,7},{7,6},{8,9},{9,8},{10,11... | collective-permute-start | bytes 835592 | tf_op jit(solution)/shard_map/ppermute | solution.py:607
  11.2 6.0 %collective-permute-start.3 = (bf16[272,256]{1,0:T(8,128)(2,1)S(1)}, bf16[272,256]{1,0:T(8,128)(2,1)S(1)}, u32[]{:S(2)}, u32[]{:S(2)}) collective-permute-start(bf16[272,256]{1,0:T(8,128)(2,1)S(1)} %get-tuple-element.62), channel_id=1, source_target_pairs={{0,2},{1,3},{2,0},{3,1},{4,6},{5,7},{6,4},{7,5},{8,10},{9,11},{10,... | collective-permute-start | bytes 417800 | tf_op jit(solution)/shard_map/ppermute | solution.py:607
  17.3 5.2 %collective-permute-start.4 = (bf16[272,256]{1,0:T(8,128)(2,1)S(1)}, bf16[272,256]{1,0:T(8,128)(2,1)S(1)}, u32[]{:S(2)}, u32[]{:S(2)}) collective-permute-start(bf16[272,256]{1,0:T(8,128)(2,1)S(1)} %shard_map.146.after_ref.mine_ref), channel_id=1, source_target_pairs={{0,4},{1,5},{2,6},{3,7},{4,0},{5,1},{6,2},{7,3},{8,12},{9,13},{10,... | collective-permute-start | bytes 417800 | tf_op jit(solution)/shard_map/ppermute | solution.py:607
  22.6 8.8 %copy-start = (bf16[128,4096]{1,0:T(8,128)(2,1)S(1)}, bf16[128,4096]{1,0:T(8,128)(2,1)}, u32[]{:S(2)}) copy-start(bf16[128,4096]{1,0:T(8,128)(2,1)} %z_ref.1) | copy-start | bytes 3145732
  22.6 7.0 %collective-permute-start.5 = (bf16[272,256]{1,0:T(8,128)(2,1)S(1)}, bf16[272,256]{1,0:T(8,128)(2,1)S(1)}, u32[]{:S(2)}, u32[]{:S(2)}) collective-permute-start(bf16[272,256]{1,0:T(8,128)(2,1)S(1)} %get-tuple-element.63.after_ref.mine_ref), channel_id=1, source_target_pairs={{0,12},{1,13},{2,14},{3,15},{4,8},{5,9},{6,10},{7,11},{8,4},{9,5},... | collective-permute-start | bytes 417800 | tf_op jit(solution)/shard_map/ppermute | solution.py:607
  29.9 5.0 %collective-permute-start.6 = (bf16[256,256]{1,0:T(8,128)(2,1)S(1)}, bf16[256,256]{1,0:T(8,128)(2,1)S(1)}, u32[]{:S(2)}, u32[]{:S(2)}) collective-permute-start(bf16[256,256]{1,0:T(8,128)(2,1)S(1)} %get-tuple-element.70), channel_id=1, source_target_pairs={{0,2},{1,3},{2,0},{3,1},{4,6},{5,7},{6,4},{7,5},{8,10},{9,11},{10,... | collective-permute-start | bytes 393224 | tf_op jit(solution)/shard_map/ppermute | solution.py:607
  34.9 1.7 %copy-start.2 = (f32[4096]{0:T(1024)S(1)}, f32[4096]{0:T(1024)}, u32[]{:S(2)}) copy-start(f32[4096]{0:T(1024)} %param.22) | copy-start | bytes 49156
  35.0 1.6 %collective-permute-start.7 = (bf16[2,256,256]{2,1,0:T(8,128)(2,1)S(1)}, bf16[2,256,256]{2,1,0:T(8,128)(2,1)S(1)}, u32[]{:S(2)}, u32[]{:S(2)}) collective-permute-start(bf16[2,256,256]{2,1,0:T(8,128)(2,1)S(1)} %shard_map.153.after_ref), channel_id=1, source_target_pairs={{0,1},{1,0},{2,3},{3,2},{4,5},{5,4},{6,7},{7,6},{8,9},{9,8},{10,11... | collective-permute-start | bytes 786440 | tf_op jit(solution)/shard_map/ppermute | solution.py:607

commit v4 on v3

--- a/solution.py
+++ b/solution.py
@@ -32,14 +32,13 @@
 
 def rim_kernel(*refs, count):
     x_ref, bc_ref = refs[:2]
-    sources, out_ref, refs = refs[2 : 2 + count], refs[2 + count], refs[3 + count :]
-    targets, (x_rows, bc_rows, sems) = refs[: count + 1], refs[count + 1 :]
+    sources, out_ref, refs = refs[:count], refs[count], refs[count + 1 :]
+    targets, (x_rows, bc_rows, sems) = refs[:count], refs[count:]
     rows, inner = x_ref.shape
     pairs = [
         (x_ref.at[pl.ds(rows - TOP, TOP), :], x_rows),
         (bc_ref.at[pl.ds(rows - TOP, TOP), :], bc_rows),
-        (x_ref.at[:, pl.ds(0, targets[0].shape[1])], targets[0]),
-    ] + list(zip(sources, targets[1:]))
+    ] + list(zip(sources, targets))
     copies = [pltpu.make_async_copy(a, b, sems.at[k]) for k, (a, b) in enumerate(pairs)]
     for copy in copies:
         copy.start()
@@ -72,8 +71,7 @@
 
 def conv_kernel(
     len_ref,
-    x_hbm,
-    x0_ref,
+    x_ref,
     bc_ref,
     w_ref,
     bias_ref,
@@ -90,28 +88,18 @@
     dec_ref,
     top_ref,
     local_ref,
-    x_ref,
     ext,
     tails,
     scaled,
-    sems,
     *,
     heads,
     head_dim,
 ):
-    more, rows, width = x_ref.shape
-    steps = more + 1
+    _, rows, width = tails.shape
+    side = bo_ref.shape[1]
+    inner = x_ref.shape[1]
+    steps = inner // width
     per_step = heads // steps
-    side = bo_ref.shape[1]
-    inner = steps * width
-    copies = [
-        pltpu.make_async_copy(
-            x_hbm.at[:, pl.ds((i + 1) * width, width)], x_ref.at[i], sems.at[i]
-        )
-        for i in range(more)
-    ]
-    for copy in copies:
-        copy.start()
     spare = ext.shape[0]
     for k in range(spare):
         ext[k, 0:8, :] = jnp.zeros((8, 128), F32)
@@ -167,15 +155,12 @@
     group = width // PAIR
     widen(0)
     for i in range(steps):
-        if i:
-            copies[i - 1].wait()
         if i + 1 < steps:
             widen(i + 1)
         for j in range(width // 128):
             cols, lanes = pl.ds(i * width + 128 * j, 128), slice(128 * j, 128 * (j + 1))
-            values = x_ref[i - 1, :, lanes] if i else x0_ref[:, lanes]
             total = convolve(
-                values, w_ref, bias_ref, i * width + 128 * j, ext.at[j % spare], rows
+                x_ref[:, cols], w_ref, bias_ref, i * width + 128 * j, ext.at[j % spare], rows
             )
             prex_ref[:, cols] = total[0:8]
             xj = silu(total).astype(BF16)
@@ -444,10 +429,6 @@
 
 def chip_kernel(stay_ref, recv_ref, keep_ref, part_ref, gate_ref, grow_ref, send_ref):
     enter_block(stay_ref, recv_ref, keep_ref, part_ref, send_ref, lax.axis_index(SEQ) % 2 == 1)
-
-
-def block_kernel(stay_ref, recv_ref, keep_ref, part_ref, after_ref, own_ref):
-    enter_block(stay_ref, recv_ref, keep_ref, part_ref, own_ref, lax.axis_index(SEQ) % 2 == 0)
 
 
 def enter_block(stay_ref, recv_ref, keep_ref, part_ref, out_ref, first):
@@ -560,41 +541,50 @@
     mine_ref[...] = mine.T
 
 
-def out_kernel(
-    *refs,
-    parts,
-):
+def gated_part(parts, gate_ref, grow_ref, c_ref, state, group, half):
+    width = gate_ref.shape[1] // GROUPS
+    unit = width // 2
+    per_part = GROUPS // len(parts)
+    inside = pl.ds(pl.multiple_of((group % per_part) * width + half * unit, 128), unit)
+    cols = pl.ds(pl.multiple_of(group * width + half * unit, 128), unit)
+    entering = jnp.dot(
+        c_ref[:, group * STATE : (group + 1) * STATE], state, preferred_element_type=F32
+    )
+    y_all = parts[group // per_part][:, inside] + grow_ref[:, cols] * entering
+    return y_all.astype(BF16).astype(F32) * gate_ref[:, cols], cols
+
+
+def own_kernel(*refs, parts):
+    diag_refs, refs = refs[:parts], refs[parts:]
+    gate_ref, grow_ref, c_ref, stay_ref, recv_ref, keep_ref, part_ref, after_ref, out_ref, own_ref = refs
+    core = lax.axis_index(SEQ) % 2
+    enter_block(stay_ref, recv_ref, keep_ref, part_ref, own_ref, core == 0)
+    for g in range(GROUPS):
+        i, y = g // PAIR, g % PAIR
+        state = own_ref[y, i * STATE : (i + 1) * STATE, :]
+        out_ref[g], _ = gated_part(diag_refs, gate_ref, grow_ref, c_ref, state, g, core)
+
+
+def out_kernel(*refs, parts):
     diag_refs, refs = refs[:parts], refs[parts:]
     gate_ref, grow_ref, c_ref, own_ref, recv_ref, gain_ref, out_ref, held, sems = refs
     core = lax.axis_index(SEQ) % 2
-    steps, _, width = held.shape
-    unit = width // (2 * PAIR)
-    side = PAIR * STATE
+    unit = own_ref.shape[2]
+    width = 2 * unit
     copies = []
-    for i in range(steps):
-        c_all = c_ref[:, i * side : (i + 1) * side]
-        for y in range(PAIR):
-            own = own_ref[y, i * STATE : (i + 1) * STATE, :]
-            recv = recv_ref[y, i * STATE : (i + 1) * STATE, :]
-            state = jnp.concatenate(
-                [jnp.where(core == 0, own, recv), jnp.where(core == 0, recv, own)], axis=1
-            )
-            first = i * width + 2 * y * unit
-            cols = slice(first, first + 2 * unit)
-            entering = jnp.dot(
-                c_all[:, y * STATE : (y + 1) * STATE], state, preferred_element_type=F32
-            )
-            held_cols = diag_refs[0].shape[1]
-            diag = diag_refs[first // held_cols]
-            first = first % held_cols
-            y_all = diag[:, first : first + 2 * unit] + grow_ref[:, cols] * entering
-            gated = y_all.astype(BF16).astype(F32) * gate_ref[:, cols]
-            scale = lax.rsqrt(jnp.mean(gated * gated, axis=1, keepdims=True) + 1e-05)
-            held[i, :, 2 * y * unit : 2 * (y + 1) * unit] = (
-                gated * scale * gain_ref[:, cols]
-            ).astype(BF16)
+    for g in range(GROUPS):
+        i, y = g // PAIR, g % PAIR
+        state = recv_ref[y, i * STATE : (i + 1) * STATE, :]
+        other, cols = gated_part(diag_refs, gate_ref, grow_ref, c_ref, state, g, 1 - core)
+        own = own_ref[g]
+        squares = jnp.sum(own * own + other * other, axis=1, keepdims=True)
+        scale = lax.rsqrt(squares * (1.0 / width) + 1e-05)
+        for half, value in ((core, own), (1 - core, other)):
+            cols = pl.ds(pl.multiple_of(g * width + half * unit, 128), unit)
+            lanes = pl.ds(pl.multiple_of(half * unit, 128), unit)
+            held[g, :, lanes] = (value * scale * gain_ref[:, cols]).astype(BF16)
         copy = pltpu.make_async_copy(
-            held.at[i], out_ref.at[:, pl.ds(i * width, width)], sems.at[i]
+            held.at[g], out_ref.at[:, pl.ds(g * width, width)], sems.at[g]
         )
         copy.start()
         copies.append(copy)
@@ -670,6 +660,7 @@
     dma = pltpu.SemaphoreType.DMA
 
     fetched = [
+        x_in,
         bc_in,
         conv_weight,
         conv_bias.reshape(1, -1),
@@ -679,14 +670,13 @@
     ]
     rim, *ready = plain_call(
         functools.partial(rim_kernel, count=len(fetched)),
-        [near((RIM, inner + 2 * side), BF16), near((rows, width), BF16)]
-        + [near(a.shape, a.dtype) for a in fetched],
-        far=(x_in, bc_in, *fetched),
+        [near((RIM, inner + 2 * side), BF16)] + [near(a.shape, a.dtype) for a in fetched],
+        far=fetched,
         mib=4,
         scratch=[
             pltpu.VMEM((TOP, inner), BF16),
             pltpu.VMEM((TOP, 2 * side), BF16),
-            dma((3 + len(fetched),)),
+            dma((2 + len(fetched),)),
         ],
     )
     near_rim = lax.ppermute(rim, SEQ, chip_route(devices))
@@ -707,14 +697,11 @@
         ),
         *ready,
         smem=(lengths,),
-        far=(x_in,),
         after=(rim,),
         scratch=[
-            pltpu.VMEM((steps - 1, rows, width), BF16),
             pltpu.VMEM((4, 8 + rows, 128), F32),
             pltpu.VMEM((2, rows, width), F32),
             pltpu.VMEM((2, rows, width), BF16),
-            dma((steps - 1,)),
         ],
         mib=16,
         nbytes=4 * 2**20,
@@ -844,7 +831,20 @@
     half = near((PAIR, state_rows, unit), BF16)
     send_c = plain_call(chip_kernel, half, stay, recv_y, keep, part, after=(gate, grow))
     enter_recv = swap(send_c, 1)
-    enter_own = plain_call(block_kernel, half, stay, recv_y, keep, part, after=(send_c,))
+    gated_own = plain_call(
+        functools.partial(own_kernel, parts=len(diags)),
+        near((GROUPS, rows, unit), F32),
+        *diags,
+        gate,
+        grow,
+        cc,
+        stay,
+        recv_y,
+        keep,
+        part,
+        after=(send_c,),
+        scratch=[pltpu.VMEM((PAIR, state_rows, unit), BF16)],
+    )
 
     mixed = plain_call(
         functools.partial(out_kernel, parts=len(diags)),
@@ -853,11 +853,11 @@
         gate,
         grow,
         cc,
-        enter_own,
+        gated_own,
         enter_recv,
         norm_gain.reshape(1, -1),
         out_specs=ANY_SPEC,
-        scratch=[pltpu.VMEM((steps, rows, width), BF16), dma((steps,))],
+        scratch=[pltpu.VMEM((GROUPS, rows, 2 * unit), BF16), dma((GROUPS,))],
         mib=16,
         nbytes=4 * 2**20,
     )

time: 38.5 us -> 37.2 us (0.966)
  starting transfers between devices: 11.6 us -> 10.6 us
  Pallas kernels: 15.3 us -> 14.4 us
  waiting for transfers between devices: 9.94 us -> 10.6 us
    ppermute x1, waiting for transfers between devices: 0.19 us -> 1.54 us  [body(): near_rim = lax.ppermute(rim, SEQ, chip_route(devices))]
    ppermute x7, starting transfers between devices: 11.5 us -> 10.5 us  [swap(): return lax.ppermute(value, SEQ, [(i, i ^ mask) for i in devices])]
    pallas_call x16, Pallas kernels: 15.3 us -> 14.4 us  [plain_call(): pl.pallas_call(body, out_shape=out_shape, in_specs=[pl.BlockSpec(memory_s...]
    ppermute x7, waiting for transfers between devices: 9.75 us -> 9.08 us  [swap(): return lax.ppermute(value, SEQ, [(i, i ^ mask) for i in devices])]
  transfers between devices with their start and end apart: 8 -> 8, of which waited for: 7 -> 7; matrix products, arithmetic and copies ran while one was open for 0% -> 0% of each run, Pallas kernels for 30% -> 28%
where the time goes in v4:
time: 37.2 us; the launch traced here: 37 us
  Pallas kernels  14.4 us (39%)
  starting transfers between devices  10.6 us (28%)
  waiting for transfers between devices  10.6 us (28%)
  between operations  1.43 us (4%)
    pallas_call x16, Pallas kernels, plain_call(): pl.pallas_call(body, out_shape=out_shape, in_specs=[pl.BlockSpec(memory_s...  14.4 us
    ppermute x7, starting transfers between devices, swap(): return lax.ppermute(value, SEQ, [(i, i ^ mask) for i in devices])  10.5 us
    ppermute x7, waiting for transfers between devices, swap(): return lax.ppermute(value, SEQ, [(i, i ^ mask) for i in devices])  9.08 us
    ppermute x1, waiting for transfers between devices, body(): near_rim = lax.ppermute(rim, SEQ, chip_route(devices))  1.54 us
  transfers between devices with their start and end apart: 8, of which 7 were waited for; matrix products, arithmetic and copies ran while one was open for 0% of the time, Pallas kernels for 28%

profile of v4, /device:TPU:0, one launch (start us, length us, event | category | flops | bytes accessed | tf_op | source)
XLA Modules:
  0.0 37.0 jit_solution(10553636621106109585)
XLA Ops:
  0.6 0.0 copy-start.1
  0.6 1.5 %shard_map.140 = (bf16[3,5120]{1,0:T(4,128)(2,1)S(1)}, bf16[128,4096]{1,0:T(8,128)(2,1)S(1)}, bf16[128,1024]{1,0:T(8,128)(2,1)S(1)}, f32[4,5120]{1,0:T(4,128)S(1...) custom-call(bf16[128,4096]{1,0:T(8,128)(2,1)} %refs_0_.1, ...), custom_call_target="tpu_custom_call" | custom-call | bytes 1048576 | tf_op jit(solution)/shard_map/pallas_call | solution.py:618
  2.1 0.5 %collective-permute-start.1 = (bf16[3,5120]{1,0:T(4,128)(2,1)S(1)}, bf16[3,5120]{1,0:T(4,128)(2,1)S(1)}, u32[]{:S(2)}, u32[]{:S(2)}) collective-permute-start(bf16[3,5120]{1,0:T(4,128)(2,1)S(1)} %get-tuple-element.44.after_ref), channel_id=1, source_target_pairs={{0,1},{1,0},{2,3},{3,2},{4,5},{5,4},{6,7},{7,6},{8,9},{9,8},{10,11... | collective-permute-start | bytes 92168 | tf_op jit(solution)/shard_map/ppermute | solution.py:597
  2.6 0.1 collective-permute-start
  3.3 2.3 %shard_map.141 = (bf16[128,4096]{1,0:T(8,128)(2,1)S(1)}, bf16[128,512]{1,0:T(8,128)(2,1)S(1)}, f32[8,4096]{1,0:T(8,128)S(1)}, f32[8,512]{1,0:T(8,128)S(1)}, f32[...) custom-call(s32[1]{0:T(128)S(6)} %copy.15.len_ref, ...), custom_call_target="tpu_custom_call" | custom-call | bytes 4194304 | tf_op jit(solution)/shard_map/pallas_call | solution.py:618
  5.6 0.0 collective-permute-done.1.core_ref
  5.7 1.5 %collective-permute-done.near_ref = bf16[3,5120]{1,0:T(4,128)(2,1)S(1)} collective-permute-done((bf16[3,5120]{1,0:T(4,128)(2,1)S(1)}, bf16[3,5120]{1,0:T(4,128)(2,1)S(1)}, u32[]{:S(2)}, u32[]{:S(2)}) %collective-permute-start) | collective-permute-done | bytes 30752 | tf_op jit(solution)/shard_map/ppermute | solution.py:682
  7.2 0.0 copy-done.1
  7.2 0.4 %shard_map.142 = (bf16[2,272,256]{2,1,0:T(8,128)(2,1)S(1)}, bf16[2,272,256]{2,1,0:T(8,128)(2,1)S(1)}, bf16[16,4096]{1,0:T(8,128)(2,1)S(1)}, bf16[16,512]{1,0:T(8,128)(2,1)S(1)}) custom-call(bf16[3,5120]{1,0:T(4,128)(2,1)S(1)} %collective-permute-done.near_ref, bf16[3,5120]{1,0:T(4,128)(2,1)S(1)} %collective-permute-done.1.core_ref, ...), custom_call_target="tpu_custom_call" | custom-call | bytes 1048576 | tf_op jit(solution)/shard_map/pallas_call | solution.py:618
  7.6 0.0 copy-start.3
  7.6 1.2 %collective-permute-start.2 = (bf16[2,272,256]{2,1,0:T(8,128)(2,1)S(1)}, bf16[2,272,256]{2,1,0:T(8,128)(2,1)S(1)}, u32[]{:S(2)}, u32[]{:S(2)}) collective-permute-start(bf16[2,272,256]{2,1,0:T(8,128)(2,1)S(1)} %get-tuple-element.57), channel_id=1, source_target_pairs={{0,1},{1,0},{2,3},{3,2},{4,5},{5,4},{6,7},{7,6},{8,9},{9,8},{10,11... | collective-permute-start | bytes 835592 | tf_op jit(solution)/shard_map/ppermute | solution.py:597
  8.8 1.2 %collective-permute-done.2.recv_ref.part_ref.refs_8_ = bf16[2,272,256]{2,1,0:T(8,128)(2,1)S(1)} collective-permute-done((bf16[2,272,256]{2,1,0:T(8,128)(2,1)S(1)}, bf16[2,272,256]{2,1,0:T(8,128)(2,1)S(1)}, u32[]{:S(2)}, u32[]{:S(2)}) %collective-permute-start.2) | collective-permute-done | bytes 278560 | tf_op jit(solution)/shard_map/ppermute | solution.py:597
  10.0 0.1 shard_map.143
  10.1 1.8 %collective-permute-start.3 = (bf16[272,256]{1,0:T(8,128)(2,1)S(1)}, bf16[272,256]{1,0:T(8,128)(2,1)S(1)}, u32[]{:S(2)}, u32[]{:S(2)}) collective-permute-start(bf16[272,256]{1,0:T(8,128)(2,1)S(1)} %get-tuple-element.62), channel_id=1, source_target_pairs={{0,2},{1,3},{2,0},{3,1},{4,6},{5,7},{6,4},{7,5},{8,10},{9,11},{10,... | collective-permute-start | bytes 417800 | tf_op jit(solution)/shard_map/ppermute | solution.py:597
  11.9 2.5 %shard_map.145.cache_ref = f32[256,256]{1,0:T(8,128)S(1)} custom-call(f32[32,64,128]{2,1,0:T(8,128)} %bitcast.10, bf16[272,256]{1,0:T(8,128)(2,1)S(1)} %get-tuple-element.58.after_ref.mine_ref.own_ref), custom_call_target="tpu_custom_call" | custom-call | bytes 2097152 | tf_op jit(solution)/shard_map/pallas_call | solution.py:618
  14.4 0.2 shard_map.144
  14.7 1.5 %collective-permute-done.3.other_ref.recv_ref = bf16[272,256]{1,0:T(8,128)(2,1)S(1)} collective-permute-done((bf16[272,256]{1,0:T(8,128)(2,1)S(1)}, bf16[272,256]{1,0:T(8,128)(2,1)S(1)}, u32[]{:S(2)}, u32[]{:S(2)}) %collective-permute-start.3) | collective-permute-done | bytes 139296 | tf_op jit(solution)/shard_map/ppermute | solution.py:597
  16.1 0.1 shard_map.146.after_ref.mine_ref
  16.2 1.6 %collective-permute-start.4 = (bf16[272,256]{1,0:T(8,128)(2,1)S(1)}, bf16[272,256]{1,0:T(8,128)(2,1)S(1)}, u32[]{:S(2)}, u32[]{:S(2)}) collective-permute-start(bf16[272,256]{1,0:T(8,128)(2,1)S(1)} %shard_map.146.after_ref.mine_ref), channel_id=1, source_target_pairs={{0,4},{1,5},{2,6},{3,7},{4,0},{5,1},{6,2},{7,3},{8,12},{9,13},{10,... | collective-permute-start | bytes 417800 | tf_op jit(solution)/shard_map/ppermute | solution.py:597
  17.8 0.0 copy-done.3
  17.8 1.8 %shard_map.147.after_ref.refs_0_ = f32[128,2048]{1,0:T(8,128)S(1)} custom-call(bf16[128,4096]{1,0:T(8,128)(2,1)S(1)} %get-tuple-element.45.xc_ref, bf16[16,4096]{1,0:T(8,128)(2,1)S(1)} %get-tuple-element.52.xfix_ref, bf16[128,512]{1,0:T(8,128)(2,1)S(1)} %get-tuple-element.48.bc_ref.b_ref, bf16[16,512]{1,0:T(8,128)(2,1)S(1)} %get-tuple-element.53.bfix_ref, ...), custom_call_target="tpu_custom_call" | custom-call | bytes 4194304 | tf_op jit(solution)/shard_map/pallas_call | solution.py:618
  19.6 1.8 %collective-permute-done.4.other_ref = bf16[272,256]{1,0:T(8,128)(2,1)S(1)} collective-permute-done((bf16[272,256]{1,0:T(8,128)(2,1)S(1)}, bf16[272,256]{1,0:T(8,128)(2,1)S(1)}, u32[]{:S(2)}, u32[]{:S(2)}) %collective-permute-start.4) | collective-permute-done | bytes 139296 | tf_op jit(solution)/shard_map/ppermute | solution.py:597
  21.4 0.1 shard_map.148
  21.5 0.0 copy-start
  21.5 3.6 %collective-permute-start.5 = (bf16[272,256]{1,0:T(8,128)(2,1)S(1)}, bf16[272,256]{1,0:T(8,128)(2,1)S(1)}, u32[]{:S(2)}, u32[]{:S(2)}) collective-permute-start(bf16[272,256]{1,0:T(8,128)(2,1)S(1)} %get-tuple-element.63.after_ref.mine_ref), channel_id=1, source_target_pairs={{0,12},{1,13},{2,14},{3,15},{4,8},{5,9},{6,10},{7,11},{8,4},{9,5},... | collective-permute-start | bytes 417800 | tf_op jit(solution)/shard_map/ppermute | solution.py:597
  25.1 1.8 %shard_map.149.after_ref.refs_1_ = f32[128,2048]{1,0:T(8,128)S(1)} custom-call(bf16[128,4096]{1,0:T(8,128)(2,1)S(1)} %get-tuple-element.45.xc_ref, bf16[16,4096]{1,0:T(8,128)(2,1)S(1)} %get-tuple-element.52.xfix_ref, bf16[128,512]{1,0:T(8,128)(2,1)S(1)} %get-tuple-element.48.bc_ref.b_ref, bf16[16,512]{1,0:T(8,128)(2,1)S(1)} %get-tuple-element.53.bfix_ref, ...), custom_call_target="tpu_custom_call" | custom-call | bytes 4194304 | tf_op jit(solution)/shard_map/pallas_call | solution.py:618
  26.9 1.7 %collective-permute-done.5.other_ref = bf16[272,256]{1,0:T(8,128)(2,1)S(1)} collective-permute-done((bf16[272,256]{1,0:T(8,128)(2,1)S(1)}, bf16[272,256]{1,0:T(8,128)(2,1)S(1)}, u32[]{:S(2)}, u32[]{:S(2)}) %collective-permute-start.5) | collective-permute-done | bytes 139296 | tf_op jit(solution)/shard_map/ppermute | solution.py:597
  28.5 0.2 shard_map.150
  28.7 1.7 %collective-permute-start.6 = (bf16[256,256]{1,0:T(8,128)(2,1)S(1)}, bf16[256,256]{1,0:T(8,128)(2,1)S(1)}, u32[]{:S(2)}, u32[]{:S(2)}) collective-permute-start(bf16[256,256]{1,0:T(8,128)(2,1)S(1)} %get-tuple-element.70), channel_id=1, source_target_pairs={{0,2},{1,3},{2,0},{3,1},{4,6},{5,7},{6,4},{7,5},{8,10},{9,11},{10,... | collective-permute-start | bytes 393224 | tf_op jit(solution)/shard_map/ppermute | solution.py:597
  30.5 0.0 copy-done
  30.5 0.4 %shard_map.151.gate_ref.refs_2_ = f32[128,4096]{1,0:T(8,128)S(1)} custom-call(s32[1]{0:T(128)S(6)} %copy.15.len_ref, bf16[128,4096]{1,0:T(8,128)(2,1)S(1)} %copy-done, f32[256,256]{1,0:T(8,128)S(1)} %get-tuple-element.66.after_ref.final_ref), custom_call_target="tpu_custom_call" | custom-call | bytes 1048576 | tf_op jit(solution)/shard_map/pallas_call | solution.py:618
  30.9 1.0 %shard_map.152 = (f32[128,4096]{1,0:T(8,128)S(1)}, f32[256,64]{1,0:T(8,128)}) custom-call(bf16[4,128,64]{2,1,0:T(8,128)(2,1)S(1)} %get-tuple-element.67.ecum_ref, f32[256,256]{1,0:T(8,128)S(1)} %get-tuple-element.66.after_ref.final_ref), custom_call_target="tpu_custom_call" | custom-call | bytes 5242880 | tf_op jit(solution)/shard_map/pallas_call | solution.py:618
  31.9 1.9 %collective-permute-done.6.recv_ref.refs_6_ = bf16[256,256]{1,0:T(8,128)(2,1)S(1)} collective-permute-done((bf16[256,256]{1,0:T(8,128)(2,1)S(1)}, bf16[256,256]{1,0:T(8,128)(2,1)S(1)}, u32[]{:S(2)}, u32[]{:S(2)}) %collective-permute-start.6) | collective-permute-done | bytes 131104 | tf_op jit(solution)/shard_map/ppermute | solution.py:597
  33.8 0.1 shard_map.153.refs_9_
  33.9 0.0 copy-start.2
  33.9 0.1 collective-permute-start.7
  34.0 0.4 %shard_map.154.refs_5_ = f32[8,128,256]{2,1,0:T(8,128)S(1)} custom-call(f32[128,2048]{1,0:T(8,128)S(1)} %shard_map.147.after_ref.refs_0_, f32[128,2048]{1,0:T(8,128)S(1)} %shard_map.149.after_ref.refs_1_, f32[128,4096]{1,0:T(8,128)S(1)} %shard_map.151.gate_ref.refs_2_, f32[128,4096]{1,0:T(8,128)S(1)} %get-tuple-element.68.grow_ref.refs_3_, ...), custom_call_target="tpu_custom_call" | custom-call | bytes 1048576 | tf_op jit(solution)/shard_map/pallas_call | solution.py:618
  34.4 1.1 %collective-permute-done.7.refs_6_ = bf16[2,256,256]{2,1,0:T(8,128)(2,1)S(1)} collective-permute-done((bf16[2,256,256]{2,1,0:T(8,128)(2,1)S(1)}, bf16[2,256,256]{2,1,0:T(8,128)(2,1)S(1)}, u32[]{:S(2)}, u32[]{:S(2)}) %collective-permute-start.7) | collective-permute-done | bytes 262176 | tf_op jit(solution)/shard_map/ppermute | solution.py:597
  35.5 0.0 copy-done.2
  35.5 1.5 %shard_map.155 = bf16[128,4096]{1,0:T(8,128)(2,1)} custom-call(f32[128,2048]{1,0:T(8,128)S(1)} %shard_map.147.after_ref.refs_0_, f32[128,2048]{1,0:T(8,128)S(1)} %shard_map.149.after_ref.refs_1_, f32[128,4096]{1,0:T(8,128)S(1)} %shard_map.151.gate_ref.refs_2_, f32[128,4096]{1,0:T(8,128)S(1)} %get-tuple-element.68.grow_ref.refs_3_, ...), custom_call_target="tpu_custom_call" | custom-call | bytes 4194304 | tf_op jit(solution)/shard_map/pallas_call | solution.py:618
Async XLA Ops:
  0.6 6.6 %copy-start.1 = (bf16[3,5120]{1,0:T(4,128)(2,1)S(1)}, bf16[3,5120]{1,0:T(4,128)(2,1)}, u32[]{:S(2)}) copy-start(bf16[3,5120]{1,0:T(4,128)(2,1)} %cache_ref.3) | copy-start | bytes 92164
  2.1 3.5 %collective-permute-start.1 = (bf16[3,5120]{1,0:T(4,128)(2,1)S(1)}, bf16[3,5120]{1,0:T(4,128)(2,1)S(1)}, u32[]{:S(2)}, u32[]{:S(2)}) collective-permute-start(bf16[3,5120]{1,0:T(4,128)(2,1)S(1)} %get-tuple-element.44.after_ref), channel_id=1, source_target_pairs={{0,1},{1,0},{2,3},{3,2},{4,5},{5,4},{6,7},{7,6},{8,9},{9,8},{10,11... | collective-permute-start | bytes 92168 | tf_op jit(solution)/shard_map/ppermute | solution.py:597
  2.6 4.6 %collective-permute-start = (bf16[3,5120]{1,0:T(4,128)(2,1)S(1)}, bf16[3,5120]{1,0:T(4,128)(2,1)S(1)}, u32[]{:S(2)}, u32[]{:S(2)}) collective-permute-start(bf16[3,5120]{1,0:T(4,128)(2,1)S(1)} %get-tuple-element.44.after_ref), channel_id=1, source_target_pairs={{0,1},{1,2},{2,0},{3,4},{4,3},{5,6},{6,5},{7,8},{8,7},{9,10},{10,9... | collective-permute-start | bytes 92168 | tf_op jit(solution)/shard_map/ppermute | solution.py:682
  7.6 10.2 %copy-start.3 = (f32[128]{0:T(128)S(1)}, f32[128]{0:T(128)}, u32[]{:S(2)}) copy-start(f32[128]{0:T(128)} %param.21) | copy-start | bytes 1540
  7.6 2.4 %collective-permute-start.2 = (bf16[2,272,256]{2,1,0:T(8,128)(2,1)S(1)}, bf16[2,272,256]{2,1,0:T(8,128)(2,1)S(1)}, u32[]{:S(2)}, u32[]{:S(2)}) collective-permute-start(bf16[2,272,256]{2,1,0:T(8,128)(2,1)S(1)} %get-tuple-element.57), channel_id=1, source_target_pairs={{0,1},{1,0},{2,3},{3,2},{4,5},{5,4},{6,7},{7,6},{8,9},{9,8},{10,11... | collective-permute-start | bytes 835592 | tf_op jit(solution)/shard_map/ppermute | solution.py:597
  10.1 6.0 %collective-permute-start.3 = (bf16[272,256]{1,0:T(8,128)(2,1)S(1)}, bf16[272,256]{1,0:T(8,128)(2,1)S(1)}, u32[]{:S(2)}, u32[]{:S(2)}) collective-permute-start(bf16[272,256]{1,0:T(8,128)(2,1)S(1)} %get-tuple-element.62), channel_id=1, source_target_pairs={{0,2},{1,3},{2,0},{3,1},{4,6},{5,7},{6,4},{7,5},{8,10},{9,11},{10,... | collective-permute-start | bytes 417800 | tf_op jit(solution)/shard_map/ppermute | solution.py:597
  16.2 5.2 %collective-permute-start.4 = (bf16[272,256]{1,0:T(8,128)(2,1)S(1)}, bf16[272,256]{1,0:T(8,128)(2,1)S(1)}, u32[]{:S(2)}, u32[]{:S(2)}) collective-permute-start(bf16[272,256]{1,0:T(8,128)(2,1)S(1)} %shard_map.146.after_ref.mine_ref), channel_id=1, source_target_pairs={{0,4},{1,5},{2,6},{3,7},{4,0},{5,1},{6,2},{7,3},{8,12},{9,13},{10,... | collective-permute-start | bytes 417800 | tf_op jit(solution)/shard_map/ppermute | solution.py:597
  21.5 9.0 %copy-start = (bf16[128,4096]{1,0:T(8,128)(2,1)S(1)}, bf16[128,4096]{1,0:T(8,128)(2,1)}, u32[]{:S(2)}) copy-start(bf16[128,4096]{1,0:T(8,128)(2,1)} %z_ref.1) | copy-start | bytes 3145732
  21.5 7.0 %collective-permute-start.5 = (bf16[272,256]{1,0:T(8,128)(2,1)S(1)}, bf16[272,256]{1,0:T(8,128)(2,1)S(1)}, u32[]{:S(2)}, u32[]{:S(2)}) collective-permute-start(bf16[272,256]{1,0:T(8,128)(2,1)S(1)} %get-tuple-element.63.after_ref.mine_ref), channel_id=1, source_target_pairs={{0,12},{1,13},{2,14},{3,15},{4,8},{5,9},{6,10},{7,11},{8,4},{9,5},... | collective-permute-start | bytes 417800 | tf_op jit(solution)/shard_map/ppermute | solution.py:597
  28.7 5.0 %collective-permute-start.6 = (bf16[256,256]{1,0:T(8,128)(2,1)S(1)}, bf16[256,256]{1,0:T(8,128)(2,1)S(1)}, u32[]{:S(2)}, u32[]{:S(2)}) collective-permute-start(bf16[256,256]{1,0:T(8,128)(2,1)S(1)} %get-tuple-element.70), channel_id=1, source_target_pairs={{0,2},{1,3},{2,0},{3,1},{4,6},{5,7},{6,4},{7,5},{8,10},{9,11},{10,... | collective-permute-start | bytes 393224 | tf_op jit(solution)/shard_map/ppermute | solution.py:597
  33.9 1.6 %copy-start.2 = (f32[4096]{0:T(1024)S(1)}, f32[4096]{0:T(1024)}, u32[]{:S(2)}) copy-start(f32[4096]{0:T(1024)} %param.22) | copy-start | bytes 49156
  33.9 1.6 %collective-permute-start.7 = (bf16[2,256,256]{2,1,0:T(8,128)(2,1)S(1)}, bf16[2,256,256]{2,1,0:T(8,128)(2,1)S(1)}, u32[]{:S(2)}, u32[]{:S(2)}) collective-permute-start(bf16[2,256,256]{2,1,0:T(8,128)(2,1)S(1)} %shard_map.153.refs_9_), channel_id=1, source_target_pairs={{0,1},{1,0},{2,3},{3,2},{4,5},{5,4},{6,7},{7,6},{8,9},{9,8},{10,11... | collective-permute-start | bytes 786440 | tf_op jit(solution)/shard_map/ppermute | solution.py:597

commit v5 on v4

--- a/solution.py
+++ b/solution.py
@@ -21,7 +21,10 @@
 
 
 def silu(v):
-    half = 0.5 * v
+    return silu_of_twice(0.5 * v)
+
+
+def silu_of_twice(half):
     return half + half * jnp.tanh(half)
 
 
@@ -63,9 +66,9 @@
 def convolve(values, w_ref, bias_ref, first, ext, rows):
     cols = pl.ds(first, 128)
     ext[8:, :] = values.astype(F32)
-    total = jnp.broadcast_to(bias_ref[:, cols], (rows, 128))
+    total = jnp.broadcast_to(0.5 * bias_ref[:, cols], (rows, 128))
     for k in range(CONV_W):
-        total = total + ext[pl.ds(8 + k - RIM, rows), :] * w_ref[k : k + 1, cols]
+        total = total + ext[pl.ds(8 + k - RIM, rows), :] * (0.5 * w_ref[k : k + 1, cols])
     return total
 
 
@@ -123,7 +126,7 @@
         cols = pl.ds(128 * j, 128)
         total = convolve(bc_ref[:, cols], w_ref, bias_ref, inner + 128 * j, ext.at[j % spare], rows)
         preb_ref[:, cols] = total[0:8]
-        bo_ref[:, cols] = silu(total).astype(BF16)
+        bo_ref[:, cols] = silu_of_twice(total).astype(BF16)
 
     last = cum[rows - 1 : rows, :]
     tail_hi, tail_lo = split2(jnp.exp(last - cum) * dt)
@@ -163,7 +166,7 @@
                 x_ref[:, cols], w_ref, bias_ref, i * width + 128 * j, ext.at[j % spare], rows
             )
             prex_ref[:, cols] = total[0:8]
-            xj = silu(total).astype(BF16)
+            xj = silu_of_twice(total).astype(BF16)
             xo_ref[:, cols] = xj
             tail = tails[i % 2, :, lanes]
             top_ref[:, cols] = jnp.where(early, tail[0:8], 0.0)
@@ -211,7 +214,7 @@
         )
         values = bc_ref[:, pl.ds(side + 128 * j, 128)]
         total = convolve(values, w_ref, bias_ref, first + 128 * j, ext.at[j % spare], rows)
-        co_ref[:, pl.ds(128 * j, 128)] = silu(total).astype(BF16)
+        co_ref[:, pl.ds(128 * j, 128)] = silu_of_twice(total).astype(BF16)
     cum, dt = cum_ref[...], step_ref[...]
     log_ref[...] = cum * LOG2E
     log_dt = jnp.where(dt > 0.0, jnp.log(jnp.maximum(dt, 1e-38)) * LOG2E, -1e30)
@@ -253,8 +256,8 @@
         cols = pl.ds(first, count)
         total = pre[...]
         for k in range(RIM):
-            total = total + ext[pl.ds(8 - RIM + k, 8), cols] * w_ref[k : k + 1, cols]
-        fixed = silu(total)
+            total = total + ext[pl.ds(8 - RIM + k, 8), cols] * (0.5 * w_ref[k : k + 1, cols])
+        fixed = silu_of_twice(total)
         dst[...] = jnp.concatenate([fixed, old[0:TOP, :].astype(F32)[8:, :]], axis=0).astype(BF16)
         return fixed.astype(BF16).astype(F32)
 
@@ -554,20 +557,27 @@
     return y_all.astype(BF16).astype(F32) * gate_ref[:, cols], cols
 
 
+def sum_lanes(value):
+    return sum(value[:, j : j + 128] for j in range(0, value.shape[1], 128))
+
+
 def own_kernel(*refs, parts):
     diag_refs, refs = refs[:parts], refs[parts:]
-    gate_ref, grow_ref, c_ref, stay_ref, recv_ref, keep_ref, part_ref, after_ref, out_ref, own_ref = refs
+    gate_ref, grow_ref, c_ref, gain_ref, stay_ref, recv_ref, keep_ref, part_ref = refs[:8]
+    out_ref, sums_ref, own_ref = refs[9:]
     core = lax.axis_index(SEQ) % 2
     enter_block(stay_ref, recv_ref, keep_ref, part_ref, own_ref, core == 0)
     for g in range(GROUPS):
         i, y = g // PAIR, g % PAIR
         state = own_ref[y, i * STATE : (i + 1) * STATE, :]
-        out_ref[g], _ = gated_part(diag_refs, gate_ref, grow_ref, c_ref, state, g, core)
+        gated, cols = gated_part(diag_refs, gate_ref, grow_ref, c_ref, state, g, core)
+        sums_ref[g] = sum_lanes(gated * gated)
+        out_ref[g] = gated * gain_ref[:, cols]
 
 
 def out_kernel(*refs, parts):
     diag_refs, refs = refs[:parts], refs[parts:]
-    gate_ref, grow_ref, c_ref, own_ref, recv_ref, gain_ref, out_ref, held, sems = refs
+    gate_ref, grow_ref, c_ref, own_ref, sums_ref, recv_ref, gain_ref, out_ref, held, sems = refs
     core = lax.axis_index(SEQ) % 2
     unit = own_ref.shape[2]
     width = 2 * unit
@@ -576,13 +586,11 @@
         i, y = g // PAIR, g % PAIR
         state = recv_ref[y, i * STATE : (i + 1) * STATE, :]
         other, cols = gated_part(diag_refs, gate_ref, grow_ref, c_ref, state, g, 1 - core)
-        own = own_ref[g]
-        squares = jnp.sum(own * own + other * other, axis=1, keepdims=True)
+        squares = jnp.sum(sums_ref[g] + sum_lanes(other * other), axis=1, keepdims=True)
         scale = lax.rsqrt(squares * (1.0 / width) + 1e-05)
-        for half, value in ((core, own), (1 - core, other)):
-            cols = pl.ds(pl.multiple_of(g * width + half * unit, 128), unit)
+        for half, value in ((core, own_ref[g]), (1 - core, other * gain_ref[:, cols])):
             lanes = pl.ds(pl.multiple_of(half * unit, 128), unit)
-            held[g, :, lanes] = (value * scale * gain_ref[:, cols]).astype(BF16)
+            held[g, :, lanes] = (value * scale).astype(BF16)
         copy = pltpu.make_async_copy(
             held.at[g], out_ref.at[:, pl.ds(g * width, width)], sems.at[g]
         )
@@ -667,6 +675,7 @@
         dt_in,
         dt_bias.reshape(1, -1),
         a_log.reshape(1, -1),
+        norm_gain.reshape(1, -1),
     ]
     rim, *ready = plain_call(
         functools.partial(rim_kernel, count=len(fetched)),
@@ -695,7 +704,7 @@
             near((8, inner), F32),
             near((GROUPS, STATE, width // PAIR), F32),
         ),
-        *ready,
+        *ready[:-1],
         smem=(lengths,),
         after=(rim,),
         scratch=[
@@ -831,13 +840,15 @@
     half = near((PAIR, state_rows, unit), BF16)
     send_c = plain_call(chip_kernel, half, stay, recv_y, keep, part, after=(gate, grow))
     enter_recv = swap(send_c, 1)
-    gated_own = plain_call(
+    gain = ready[-1]
+    gated_own, own_sums = plain_call(
         functools.partial(own_kernel, parts=len(diags)),
-        near((GROUPS, rows, unit), F32),
+        (near((GROUPS, rows, unit), F32), near((GROUPS, rows, 128), F32)),
         *diags,
         gate,
         grow,
         cc,
+        gain,
         stay,
         recv_y,
         keep,
@@ -854,8 +865,9 @@
         grow,
         cc,
         gated_own,
+        own_sums,
         enter_recv,
-        norm_gain.reshape(1, -1),
+        gain,
         out_specs=ANY_SPEC,
         scratch=[pltpu.VMEM((GROUPS, rows, 2 * unit), BF16), dma((GROUPS,))],
         mib=16,

time: 37.2 us -> 37 us (level)
  waiting for transfers between devices: 10.6 us -> 9.33 us
  starting transfers between devices: 10.6 us -> 11.7 us
    ppermute x1, waiting for transfers between devices: 1.54 us -> 0.01 us  [body(): near_rim = lax.ppermute(rim, SEQ, chip_route(devices))]
    ppermute x7, starting transfers between devices: 10.5 us -> 11.2 us  [swap(): return lax.ppermute(value, SEQ, [(i, i ^ mask) for i in devices])]
    ppermute x1, starting transfers between devices: 0.07 us -> 0.51 us  [body(): near_rim = lax.ppermute(rim, SEQ, chip_route(devices))]
  transfers between devices with their start and end apart: 8 -> 8, of which waited for: 7 -> 6; matrix products, arithmetic and copies ran while one was open for 0% -> 0% of each run, Pallas kernels for 28% -> 28%
where the time goes in v5:
time: 37 us; the launch traced here: 36.8 us
  Pallas kernels  14.3 us (39%)
  starting transfers between devices  11.7 us (32%)
  waiting for transfers between devices  9.33 us (25%)
  between operations  1.44 us (4%)
    pallas_call x16, Pallas kernels, plain_call(): pl.pallas_call(body, out_shape=out_shape, in_specs=[pl.BlockSpec(memory_s...  14.3 us
    ppermute x7, starting transfers between devices, swap(): return lax.ppermute(value, SEQ, [(i, i ^ mask) for i in devices])  11.2 us
    ppermute x7, waiting for transfers between devices, swap(): return lax.ppermute(value, SEQ, [(i, i ^ mask) for i in devices])  9.33 us
  transfers between devices with their start and end apart: 8, of which 6 were waited for; matrix products, arithmetic and copies ran while one was open for 0% of the time, Pallas kernels for 28%

profile of v5, /device:TPU:0, one launch (start us, length us, event | category | flops | bytes accessed | tf_op | source)
XLA Modules:
  0.0 36.8 jit_solution(306590056512919129)
XLA Ops:
  0.6 0.0 copy-start.1
  0.6 1.5 %shard_map.140 = (bf16[3,5120]{1,0:T(4,128)(2,1)S(1)}, bf16[128,4096]{1,0:T(8,128)(2,1)S(1)}, bf16[128,1024]{1,0:T(8,128)(2,1)S(1)}, f32[4,5120]{1,0:T(4,128)S(1...) custom-call(bf16[128,4096]{1,0:T(8,128)(2,1)} %refs_0_.1, ...), custom_call_target="tpu_custom_call" | custom-call | bytes 1048576 | tf_op jit(solution)/shard_map/pallas_call | solution.py:626
  2.1 0.5 %collective-permute-start = (bf16[3,5120]{1,0:T(4,128)(2,1)S(1)}, bf16[3,5120]{1,0:T(4,128)(2,1)S(1)}, u32[]{:S(2)}, u32[]{:S(2)}) collective-permute-start(bf16[3,5120]{1,0:T(4,128)(2,1)S(1)} %get-tuple-element.47.after_ref), channel_id=1, source_target_pairs={{0,1},{1,2},{2,0},{3,4},{4,3},{5,6},{6,5},{7,8},{8,7},{9,10},{10,9... | collective-permute-start | bytes 92168 | tf_op jit(solution)/shard_map/ppermute | solution.py:691
  2.6 2.6 %collective-permute-start.1 = (bf16[3,5120]{1,0:T(4,128)(2,1)S(1)}, bf16[3,5120]{1,0:T(4,128)(2,1)S(1)}, u32[]{:S(2)}, u32[]{:S(2)}) collective-permute-start(bf16[3,5120]{1,0:T(4,128)(2,1)S(1)} %get-tuple-element.47.after_ref), channel_id=1, source_target_pairs={{0,1},{1,0},{2,3},{3,2},{4,5},{5,4},{6,7},{7,6},{8,9},{9,8},{10,11... | collective-permute-start | bytes 92168 | tf_op jit(solution)/shard_map/ppermute | solution.py:605
  5.9 2.2 %shard_map.141 = (bf16[128,4096]{1,0:T(8,128)(2,1)S(1)}, bf16[128,512]{1,0:T(8,128)(2,1)S(1)}, f32[8,4096]{1,0:T(8,128)S(1)}, f32[8,512]{1,0:T(8,128)S(1)}, f32[...) custom-call(s32[1]{0:T(128)S(6)} %copy.15.len_ref, ...), custom_call_target="tpu_custom_call" | custom-call | bytes 4194304 | tf_op jit(solution)/shard_map/pallas_call | solution.py:626
  8.1 0.0 collective-permute-done.near_ref
  8.1 0.0 collective-permute-done.1.core_ref
  8.1 0.0 copy-done.1
  8.1 0.4 %shard_map.142 = (bf16[2,272,256]{2,1,0:T(8,128)(2,1)S(1)}, bf16[2,272,256]{2,1,0:T(8,128)(2,1)S(1)}, bf16[16,4096]{1,0:T(8,128)(2,1)S(1)}, bf16[16,512]{1,0:T(8,128)(2,1)S(1)}) custom-call(bf16[3,5120]{1,0:T(4,128)(2,1)S(1)} %collective-permute-done.near_ref, bf16[3,5120]{1,0:T(4,128)(2,1)S(1)} %collective-permute-done.1.core_ref, ...), custom_call_target="tpu_custom_call" | custom-call | bytes 1048576 | tf_op jit(solution)/shard_map/pallas_call | solution.py:626
  8.6 0.0 copy-start.2
  8.6 0.1 collective-permute-start.2
  8.6 1.5 %collective-permute-done.2.recv_ref.part_ref.refs_9_ = bf16[2,272,256]{2,1,0:T(8,128)(2,1)S(1)} collective-permute-done((bf16[2,272,256]{2,1,0:T(8,128)(2,1)S(1)}, bf16[2,272,256]{2,1,0:T(8,128)(2,1)S(1)}, u32[]{:S(2)}, u32[]{:S(2)}) %collective-permute-start.2) | collective-permute-done | bytes 278560 | tf_op jit(solution)/shard_map/ppermute | solution.py:605
  10.2 0.1 shard_map.143
  10.3 1.6 %collective-permute-start.3 = (bf16[272,256]{1,0:T(8,128)(2,1)S(1)}, bf16[272,256]{1,0:T(8,128)(2,1)S(1)}, u32[]{:S(2)}, u32[]{:S(2)}) collective-permute-start(bf16[272,256]{1,0:T(8,128)(2,1)S(1)} %get-tuple-element.65), channel_id=1, source_target_pairs={{0,2},{1,3},{2,0},{3,1},{4,6},{5,7},{6,4},{7,5},{8,10},{9,11},{10,... | collective-permute-start | bytes 417800 | tf_op jit(solution)/shard_map/ppermute | solution.py:605
  11.9 2.5 %shard_map.145.cache_ref = f32[256,256]{1,0:T(8,128)S(1)} custom-call(f32[32,64,128]{2,1,0:T(8,128)} %bitcast.9, bf16[272,256]{1,0:T(8,128)(2,1)S(1)} %get-tuple-element.61.after_ref.mine_ref.own_ref), custom_call_target="tpu_custom_call" | custom-call | bytes 2097152 | tf_op jit(solution)/shard_map/pallas_call | solution.py:626
  14.4 0.2 shard_map.144
  14.7 1.4 %collective-permute-done.3.other_ref.recv_ref = bf16[272,256]{1,0:T(8,128)(2,1)S(1)} collective-permute-done((bf16[272,256]{1,0:T(8,128)(2,1)S(1)}, bf16[272,256]{1,0:T(8,128)(2,1)S(1)}, u32[]{:S(2)}, u32[]{:S(2)}) %collective-permute-start.3) | collective-permute-done | bytes 139296 | tf_op jit(solution)/shard_map/ppermute | solution.py:605
  16.1 0.1 shard_map.146.after_ref.mine_ref
  16.2 1.6 %collective-permute-start.4 = (bf16[272,256]{1,0:T(8,128)(2,1)S(1)}, bf16[272,256]{1,0:T(8,128)(2,1)S(1)}, u32[]{:S(2)}, u32[]{:S(2)}) collective-permute-start(bf16[272,256]{1,0:T(8,128)(2,1)S(1)} %shard_map.146.after_ref.mine_ref), channel_id=1, source_target_pairs={{0,4},{1,5},{2,6},{3,7},{4,0},{5,1},{6,2},{7,3},{8,12},{9,13},{10,... | collective-permute-start | bytes 417800 | tf_op jit(solution)/shard_map/ppermute | solution.py:605
  17.8 0.0 copy-done.2
  17.8 1.8 %shard_map.147.after_ref.refs_0_ = f32[128,2048]{1,0:T(8,128)S(1)} custom-call(bf16[128,4096]{1,0:T(8,128)(2,1)S(1)} %get-tuple-element.48.xc_ref, bf16[16,4096]{1,0:T(8,128)(2,1)S(1)} %get-tuple-element.55.xfix_ref, bf16[128,512]{1,0:T(8,128)(2,1)S(1)} %get-tuple-element.51.bc_ref.b_ref, bf16[16,512]{1,0:T(8,128)(2,1)S(1)} %get-tuple-element.56.bfix_ref, ...), custom_call_target="tpu_custom_call" | custom-call | bytes 4194304 | tf_op jit(solution)/shard_map/pallas_call | solution.py:626
  19.6 1.7 %collective-permute-done.4.other_ref = bf16[272,256]{1,0:T(8,128)(2,1)S(1)} collective-permute-done((bf16[272,256]{1,0:T(8,128)(2,1)S(1)}, bf16[272,256]{1,0:T(8,128)(2,1)S(1)}, u32[]{:S(2)}, u32[]{:S(2)}) %collective-permute-start.4) | collective-permute-done | bytes 139296 | tf_op jit(solution)/shard_map/ppermute | solution.py:605
  21.3 0.1 shard_map.148
  21.4 0.0 copy-start
  21.4 3.7 %collective-permute-start.5 = (bf16[272,256]{1,0:T(8,128)(2,1)S(1)}, bf16[272,256]{1,0:T(8,128)(2,1)S(1)}, u32[]{:S(2)}, u32[]{:S(2)}) collective-permute-start(bf16[272,256]{1,0:T(8,128)(2,1)S(1)} %get-tuple-element.66.after_ref.mine_ref), channel_id=1, source_target_pairs={{0,12},{1,13},{2,14},{3,15},{4,8},{5,9},{6,10},{7,11},{8,4},{9,5},... | collective-permute-start | bytes 417800 | tf_op jit(solution)/shard_map/ppermute | solution.py:605
  25.0 1.8 %shard_map.149.after_ref.refs_1_ = f32[128,2048]{1,0:T(8,128)S(1)} custom-call(bf16[128,4096]{1,0:T(8,128)(2,1)S(1)} %get-tuple-element.48.xc_ref, bf16[16,4096]{1,0:T(8,128)(2,1)S(1)} %get-tuple-element.55.xfix_ref, bf16[128,512]{1,0:T(8,128)(2,1)S(1)} %get-tuple-element.51.bc_ref.b_ref, bf16[16,512]{1,0:T(8,128)(2,1)S(1)} %get-tuple-element.56.bfix_ref, ...), custom_call_target="tpu_custom_call" | custom-call | bytes 4194304 | tf_op jit(solution)/shard_map/pallas_call | solution.py:626
  26.8 1.6 %collective-permute-done.5.other_ref = bf16[272,256]{1,0:T(8,128)(2,1)S(1)} collective-permute-done((bf16[272,256]{1,0:T(8,128)(2,1)S(1)}, bf16[272,256]{1,0:T(8,128)(2,1)S(1)}, u32[]{:S(2)}, u32[]{:S(2)}) %collective-permute-start.5) | collective-permute-done | bytes 139296 | tf_op jit(solution)/shard_map/ppermute | solution.py:605
  28.4 0.2 shard_map.150
  28.6 1.6 %collective-permute-start.6 = (bf16[256,256]{1,0:T(8,128)(2,1)S(1)}, bf16[256,256]{1,0:T(8,128)(2,1)S(1)}, u32[]{:S(2)}, u32[]{:S(2)}) collective-permute-start(bf16[256,256]{1,0:T(8,128)(2,1)S(1)} %get-tuple-element.74), channel_id=1, source_target_pairs={{0,2},{1,3},{2,0},{3,1},{4,6},{5,7},{6,4},{7,5},{8,10},{9,11},{10,... | collective-permute-start | bytes 393224 | tf_op jit(solution)/shard_map/ppermute | solution.py:605
  30.2 1.0 %shard_map.152 = (f32[128,4096]{1,0:T(8,128)S(1)}, f32[256,64]{1,0:T(8,128)}) custom-call(bf16[4,128,64]{2,1,0:T(8,128)(2,1)S(1)} %get-tuple-element.70.ecum_ref, f32[256,256]{1,0:T(8,128)S(1)} %get-tuple-element.69.after_ref.final_ref), custom_call_target="tpu_custom_call" | custom-call | bytes 5242880 | tf_op jit(solution)/shard_map/pallas_call | solution.py:626
  31.2 0.0 copy-done
  31.2 0.4 %shard_map.151.gate_ref.refs_2_ = f32[128,4096]{1,0:T(8,128)S(1)} custom-call(s32[1]{0:T(128)S(6)} %copy.15.len_ref, bf16[128,4096]{1,0:T(8,128)(2,1)S(1)} %copy-done, f32[256,256]{1,0:T(8,128)S(1)} %get-tuple-element.69.after_ref.final_ref), custom_call_target="tpu_custom_call" | custom-call | bytes 1048576 | tf_op jit(solution)/shard_map/pallas_call | solution.py:626
  31.6 2.0 %collective-permute-done.6.recv_ref.refs_7_ = bf16[256,256]{1,0:T(8,128)(2,1)S(1)} collective-permute-done((bf16[256,256]{1,0:T(8,128)(2,1)S(1)}, bf16[256,256]{1,0:T(8,128)(2,1)S(1)}, u32[]{:S(2)}, u32[]{:S(2)}) %collective-permute-start.6) | collective-permute-done | bytes 131104 | tf_op jit(solution)/shard_map/ppermute | solution.py:605
  33.6 0.1 shard_map.153.refs_10_
  33.8 0.1 collective-permute-start.7
  33.8 0.5 %shard_map.154 = (f32[8,128,256]{2,1,0:T(8,128)S(1)}, f32[8,128,128]{2,1,0:T(8,128)S(1)}) custom-call(f32[128,2048]{1,0:T(8,128)S(1)} %shard_map.147.after_ref.refs_0_, f32[128,2048]{1,0:T(8,128)S(1)} %shard_map.149.after_ref.refs_1_, f32[128,4096]{1,0:T(8,128)S(1)} %shard_map.151.gate_ref.refs_2_, f32[128,4096]{1,0:T(8,128)S(1)} %get-tuple-element.71.grow_ref.refs_3_, ...), custom_call_target="tpu_custom_call" | custom-call | bytes 1048576 | tf_op jit(solution)/shard_map/pallas_call | solution.py:626
  34.3 1.1 %collective-permute-done.7.refs_7_ = bf16[2,256,256]{2,1,0:T(8,128)(2,1)S(1)} collective-permute-done((bf16[2,256,256]{2,1,0:T(8,128)(2,1)S(1)}, bf16[2,256,256]{2,1,0:T(8,128)(2,1)S(1)}, u32[]{:S(2)}, u32[]{:S(2)}) %collective-permute-start.7) | collective-permute-done | bytes 262176 | tf_op jit(solution)/shard_map/ppermute | solution.py:605
  35.4 1.5 %shard_map.155 = bf16[128,4096]{1,0:T(8,128)(2,1)} custom-call(f32[128,2048]{1,0:T(8,128)S(1)} %shard_map.147.after_ref.refs_0_, f32[128,2048]{1,0:T(8,128)S(1)} %shard_map.149.after_ref.refs_1_, f32[128,4096]{1,0:T(8,128)S(1)} %shard_map.151.gate_ref.refs_2_, f32[128,4096]{1,0:T(8,128)S(1)} %get-tuple-element.71.grow_ref.refs_3_, ...), custom_call_target="tpu_custom_call" | custom-call | bytes 4194304 | tf_op jit(solution)/shard_map/pallas_call | solution.py:626
Async XLA Ops:
  0.6 7.5 %copy-start.1 = (bf16[3,5120]{1,0:T(4,128)(2,1)S(1)}, bf16[3,5120]{1,0:T(4,128)(2,1)}, u32[]{:S(2)}) copy-start(bf16[3,5120]{1,0:T(4,128)(2,1)} %cache_ref.3) | copy-start | bytes 92164
  2.1 6.0 %collective-permute-start = (bf16[3,5120]{1,0:T(4,128)(2,1)S(1)}, bf16[3,5120]{1,0:T(4,128)(2,1)S(1)}, u32[]{:S(2)}, u32[]{:S(2)}) collective-permute-start(bf16[3,5120]{1,0:T(4,128)(2,1)S(1)} %get-tuple-element.47.after_ref), channel_id=1, source_target_pairs={{0,1},{1,2},{2,0},{3,4},{4,3},{5,6},{6,5},{7,8},{8,7},{9,10},{10,9... | collective-permute-start | bytes 92168 | tf_op jit(solution)/shard_map/ppermute | solution.py:691
  2.6 5.5 %collective-permute-start.1 = (bf16[3,5120]{1,0:T(4,128)(2,1)S(1)}, bf16[3,5120]{1,0:T(4,128)(2,1)S(1)}, u32[]{:S(2)}, u32[]{:S(2)}) collective-permute-start(bf16[3,5120]{1,0:T(4,128)(2,1)S(1)} %get-tuple-element.47.after_ref), channel_id=1, source_target_pairs={{0,1},{1,0},{2,3},{3,2},{4,5},{5,4},{6,7},{7,6},{8,9},{9,8},{10,11... | collective-permute-start | bytes 92168 | tf_op jit(solution)/shard_map/ppermute | solution.py:605
  8.6 9.2 %copy-start.2 = (f32[128]{0:T(128)S(1)}, f32[128]{0:T(128)}, u32[]{:S(2)}) copy-start(f32[128]{0:T(128)} %param.21) | copy-start | bytes 1540
  8.6 1.6 %collective-permute-start.2 = (bf16[2,272,256]{2,1,0:T(8,128)(2,1)S(1)}, bf16[2,272,256]{2,1,0:T(8,128)(2,1)S(1)}, u32[]{:S(2)}, u32[]{:S(2)}) collective-permute-start(bf16[2,272,256]{2,1,0:T(8,128)(2,1)S(1)} %get-tuple-element.60), channel_id=1, source_target_pairs={{0,1},{1,0},{2,3},{3,2},{4,5},{5,4},{6,7},{7,6},{8,9},{9,8},{10,11... | collective-permute-start | bytes 835592 | tf_op jit(solution)/shard_map/ppermute | solution.py:605
  10.3 5.8 %collective-permute-start.3 = (bf16[272,256]{1,0:T(8,128)(2,1)S(1)}, bf16[272,256]{1,0:T(8,128)(2,1)S(1)}, u32[]{:S(2)}, u32[]{:S(2)}) collective-permute-start(bf16[272,256]{1,0:T(8,128)(2,1)S(1)} %get-tuple-element.65), channel_id=1, source_target_pairs={{0,2},{1,3},{2,0},{3,1},{4,6},{5,7},{6,4},{7,5},{8,10},{9,11},{10,... | collective-permute-start | bytes 417800 | tf_op jit(solution)/shard_map/ppermute | solution.py:605
  16.2 5.1 %collective-permute-start.4 = (bf16[272,256]{1,0:T(8,128)(2,1)S(1)}, bf16[272,256]{1,0:T(8,128)(2,1)S(1)}, u32[]{:S(2)}, u32[]{:S(2)}) collective-permute-start(bf16[272,256]{1,0:T(8,128)(2,1)S(1)} %shard_map.146.after_ref.mine_ref), channel_id=1, source_target_pairs={{0,4},{1,5},{2,6},{3,7},{4,0},{5,1},{6,2},{7,3},{8,12},{9,13},{10,... | collective-permute-start | bytes 417800 | tf_op jit(solution)/shard_map/ppermute | solution.py:605
  21.4 9.8 %copy-start = (bf16[128,4096]{1,0:T(8,128)(2,1)S(1)}, bf16[128,4096]{1,0:T(8,128)(2,1)}, u32[]{:S(2)}) copy-start(bf16[128,4096]{1,0:T(8,128)(2,1)} %z_ref.1) | copy-start | bytes 3145732
  21.4 7.0 %collective-permute-start.5 = (bf16[272,256]{1,0:T(8,128)(2,1)S(1)}, bf16[272,256]{1,0:T(8,128)(2,1)S(1)}, u32[]{:S(2)}, u32[]{:S(2)}) collective-permute-start(bf16[272,256]{1,0:T(8,128)(2,1)S(1)} %get-tuple-element.66.after_ref.mine_ref), channel_id=1, source_target_pairs={{0,12},{1,13},{2,14},{3,15},{4,8},{5,9},{6,10},{7,11},{8,4},{9,5},... | collective-permute-start | bytes 417800 | tf_op jit(solution)/shard_map/ppermute | solution.py:605
  28.6 5.0 %collective-permute-start.6 = (bf16[256,256]{1,0:T(8,128)(2,1)S(1)}, bf16[256,256]{1,0:T(8,128)(2,1)S(1)}, u32[]{:S(2)}, u32[]{:S(2)}) collective-permute-start(bf16[256,256]{1,0:T(8,128)(2,1)S(1)} %get-tuple-element.74), channel_id=1, source_target_pairs={{0,2},{1,3},{2,0},{3,1},{4,6},{5,7},{6,4},{7,5},{8,10},{9,11},{10,... | collective-permute-start | bytes 393224 | tf_op jit(solution)/shard_map/ppermute | solution.py:605
  33.8 1.6 %collective-permute-start.7 = (bf16[2,256,256]{2,1,0:T(8,128)(2,1)S(1)}, bf16[2,256,256]{2,1,0:T(8,128)(2,1)S(1)}, u32[]{:S(2)}, u32[]{:S(2)}) collective-permute-start(bf16[2,256,256]{2,1,0:T(8,128)(2,1)S(1)} %shard_map.153.refs_10_), channel_id=1, source_target_pairs={{0,1},{1,0},{2,3},{3,2},{4,5},{5,4},{6,7},{7,6},{8,9},{9,8},{10,11... | collective-permute-start | bytes 786440 | tf_op jit(solution)/shard_map/ppermute | solution.py:605

commit v6 on v5

--- a/solution.py
+++ b/solution.py
@@ -238,7 +238,8 @@
     top_ref,
     local_ref,
     dec_ref,
-    send_ref,
+    far_ref,
+    near_out_ref,
     keep_ref,
     xfix_ref,
     bfix_ref,
@@ -269,20 +270,27 @@
     b_turned = b_top.T.astype(BF16)
     groups, _, width = local_ref.shape
     unit = width // 2
-    for g in range(groups):
-        extra = jnp.dot(
-            b_turned[g * STATE : (g + 1) * STATE, :],
-            scaled[:, g * width : (g + 1) * width],
-            preferred_element_type=F32,
-        )
-        whole_state = local_ref[g] + extra
-        low, high = whole_state[:, :unit], whole_state[:, unit:]
-        where = pl.ds((g // PAIR) * STATE, STATE)
-        send_ref[g % PAIR, where, :] = jnp.where(core == 0, high, low).astype(BF16)
-        keep_ref[g % PAIR, where, :] = jnp.where(core == 0, low, high).astype(BF16)
+    side_bit = (device // 2) % 2
+    for i in range(groups // PAIR):
+        where = pl.ds(i * STATE, STATE)
+        sends = []
+        for y in range(PAIR):
+            g = PAIR * i + y
+            extra = jnp.dot(
+                b_turned[g * STATE : (g + 1) * STATE, :],
+                scaled[:, g * width : (g + 1) * width],
+                preferred_element_type=F32,
+            )
+            whole_state = local_ref[g] + extra
+            low, high = whole_state[:, :unit], whole_state[:, unit:]
+            sends.append(jnp.where(core == 0, high, low))
+            keep_ref[y, where, :] = jnp.where(core == 0, low, high).astype(BF16)
+        far_ref[where, :] = jnp.where(side_bit == 0, sends[1], sends[0]).astype(BF16)
+        near_out_ref[where, :] = jnp.where(side_bit == 0, sends[0], sends[1]).astype(BF16)
     where = pl.ds(groups // PAIR * STATE, 16)
+    far_ref[where, :] = dec_ref[2 * (1 - side_bit) + 1 - core]
+    near_out_ref[where, :] = dec_ref[2 * side_bit + 1 - core]
     for y in range(PAIR):
-        send_ref[y, where, :] = dec_ref[2 * y + 1 - core]
         keep_ref[y, where, :] = dec_ref[2 * y + core]
 
 
@@ -336,13 +344,12 @@
     return [(i, slice(i * STATE, (i + 1) * STATE)) for i in range(rows // STATE)]
 
 
-def core_kernel(keep_ref, recv_ref, send_ref, own_ref):
+def core_kernel(keep_ref, recv_ref, *rest, own):
     device = lax.axis_index(SEQ)
     core, side = device % 2, (device // 2) % 2
-    rows = keep_ref.shape[1] - 16
-    for out, pick in ((send_ref, 1 - side), (own_ref, side)):
-        mine, other = keep_ref.at[pick], recv_ref.at[pick]
-        join_totals(mine, other, core == 0, out, rows)
+    out_ref = rest[-1]
+    pick = side if own else 1 - side
+    join_totals(keep_ref.at[pick], recv_ref, core == 0, out_ref, recv_ref.shape[0] - 16)
 
 
 def join_totals(mine, other, mine_first, out, rows):
@@ -430,11 +437,12 @@
         stay_ref[part, :] = jnp.where(side == 0, plane, second).astype(BF16)
 
 
-def chip_kernel(stay_ref, recv_ref, keep_ref, part_ref, gate_ref, grow_ref, send_ref):
-    enter_block(stay_ref, recv_ref, keep_ref, part_ref, send_ref, lax.axis_index(SEQ) % 2 == 1)
-
-
-def enter_block(stay_ref, recv_ref, keep_ref, part_ref, out_ref, first):
+def chip_kernel(stay_ref, recv_ref, keep_ref, far_ref, near_ref, gate_ref, grow_ref, send_ref):
+    parts = (far_ref, near_ref)
+    enter_block(stay_ref, recv_ref, keep_ref, parts, send_ref, lax.axis_index(SEQ) % 2 == 1)
+
+
+def enter_block(stay_ref, recv_ref, keep_ref, parts, out_ref, first):
     device = lax.axis_index(SEQ)
     core, side = device % 2, (device // 2) % 2
     rows = stay_ref.shape[0]
@@ -444,25 +452,26 @@
             for mine, source in ((True, stay_ref), (False, recv_ref)):
 
                 @pl.when((side == y) == mine)
-                def _(y=y, source=source):
-                    values(y, source)
+                def _(y=y, source=source, mine=mine):
+                    values(y, source, mine)
 
     @pl.when(first)
     def _():
-        def values(y, source):
+        def values(y, source, mine):
             out_ref[y] = source[...]
 
         fill(values)
 
-    for kept, local in ((0, keep_ref), (1, part_ref)):
+    for kept in range(2):
 
         @pl.when(jnp.logical_not(first) & (core == kept))
-        def _(local=local):
-            def values(y, source):
-                decay = unpack_decay(local[y, rows:, :])
+        def _(kept=kept):
+            def values(y, source, mine):
+                local = parts[mine] if kept else keep_ref.at[y]
+                decay = unpack_decay(local[rows:, :])
                 for i, part in blocks_of(rows):
                     entered = decay[i : i + 1] * source[part, :].astype(F32)
-                    out_ref[y, part, :] = (entered + local[y, part, :].astype(F32)).astype(BF16)
+                    out_ref[y, part, :] = (entered + local[part, :].astype(F32)).astype(BF16)
 
             fill(values)
 
@@ -563,10 +572,10 @@
 
 def own_kernel(*refs, parts):
     diag_refs, refs = refs[:parts], refs[parts:]
-    gate_ref, grow_ref, c_ref, gain_ref, stay_ref, recv_ref, keep_ref, part_ref = refs[:8]
-    out_ref, sums_ref, own_ref = refs[9:]
+    gate_ref, grow_ref, c_ref, gain_ref, stay_ref, recv_ref, keep_ref, *parts_in = refs[:9]
+    out_ref, sums_ref, own_ref = refs[10:]
     core = lax.axis_index(SEQ) % 2
-    enter_block(stay_ref, recv_ref, keep_ref, part_ref, own_ref, core == 0)
+    enter_block(stay_ref, recv_ref, keep_ref, parts_in, own_ref, core == 0)
     for g in range(GROUPS):
         i, y = g // PAIR, g % PAIR
         state = own_ref[y, i * STATE : (i + 1) * STATE, :]
@@ -717,9 +726,10 @@
     )
 
     pair_msg = near((PAIR, msg_rows, unit), BF16)
-    send, keep, xfix, bfix = plain_call(
+    message = near((msg_rows, unit), BF16)
+    send_far, send_near, keep, xfix, bfix = plain_call(
         fix_kernel,
-        (pair_msg, pair_msg, near((TOP, inner), BF16), near((TOP, side), BF16)),
+        (message, message, pair_msg, near((TOP, inner), BF16), near((TOP, side), BF16)),
         near_rim,
         core_rim,
         conv_cache,
@@ -734,10 +744,13 @@
         scratch=[pltpu.VMEM((16, inner + side), F32)],
     )
 
-    message = near((msg_rows, unit), BF16)
-    part = swap(send, 1)
-    send_y, own = plain_call(core_kernel, (message, message), keep, part)
+    part_far = swap(send_far, 1)
+    part_near = swap(send_near, 1)
+    send_y = plain_call(functools.partial(core_kernel, own=False), message, keep, part_far)
     recv = swap(send_y, 2)
+    own = plain_call(
+        functools.partial(core_kernel, own=True), message, keep, part_near, after=(send_y,)
+    )
     chunks = 4
     cache = plain_call(
         functools.partial(cache_kernel, unit_heads=unit_heads),
@@ -838,7 +851,7 @@
         gate_kernel, near((rows, inner), F32), z_in, smem=(lengths,), after=(final,)
     )
     half = near((PAIR, state_rows, unit), BF16)
-    send_c = plain_call(chip_kernel, half, stay, recv_y, keep, part, after=(gate, grow))
+    send_c = plain_call(chip_kernel, half, stay, recv_y, keep, part_far, part_near, after=(gate, grow))
     enter_recv = swap(send_c, 1)
     gain = ready[-1]
     gated_own, own_sums = plain_call(
@@ -852,7 +865,8 @@
         stay,
         recv_y,
         keep,
-        part,
+        part_far,
+        part_near,
         after=(send_c,),
         scratch=[pltpu.VMEM((PAIR, state_rows, unit), BF16)],
     )

time: 37 us -> 36.8 us (level)
  waiting for transfers between devices: 9.33 us -> 8.64 us
  starting transfers between devices: 11.7 us -> 12.3 us
    ppermute x7 -> x8, waiting for transfers between devices: 9.33 us -> 8.63 us  [swap(): return lax.ppermute(value, SEQ, [(i, i ^ mask) for i in devices])]
    ppermute x7 -> x8, starting transfers between devices: 11.2 us -> 11.8 us  [swap(): return lax.ppermute(value, SEQ, [(i, i ^ mask) for i in devices])]
    pallas_call x16 -> x17, Pallas kernels: 14.3 us -> 14.2 us  [plain_call(): pl.pallas_call(body, out_shape=out_shape, in_specs=[pl.BlockSpec(memory_s...]
  transfers between devices with their start and end apart: 8 -> 9, of which waited for: 6 -> 6; matrix products, arithmetic and copies ran while one was open for 0% -> 0% of each run, Pallas kernels for 28% -> 28%
where the time goes in v6:
time: 36.8 us; the launch traced here: 36.6 us
  Pallas kernels  14.2 us (39%)
  starting transfers between devices  12.3 us (33%)
  waiting for transfers between devices  8.64 us (23%)
  between operations  1.45 us (4%)
    pallas_call x17, Pallas kernels, plain_call(): pl.pallas_call(body, out_shape=out_shape, in_specs=[pl.BlockSpec(memory_s...  14.2 us
    ppermute x8, starting transfers between devices, swap(): return lax.ppermute(value, SEQ, [(i, i ^ mask) for i in devices])  11.8 us
    ppermute x8, waiting for transfers between devices, swap(): return lax.ppermute(value, SEQ, [(i, i ^ mask) for i in devices])  8.63 us
  transfers between devices with their start and end apart: 9, of which 6 were waited for; matrix products, arithmetic and copies ran while one was open for 0% of the time, Pallas kernels for 28%

profile of v6, /device:TPU:0, one launch (start us, length us, event | category | flops | bytes accessed | tf_op | source)
XLA Modules:
  0.0 36.6 jit_solution(5760074892288016963)
XLA Ops:
  0.6 0.0 copy-start.1
  0.6 1.5 %shard_map.140 = (bf16[3,5120]{1,0:T(4,128)(2,1)S(1)}, bf16[128,4096]{1,0:T(8,128)(2,1)S(1)}, bf16[128,1024]{1,0:T(8,128)(2,1)S(1)}, f32[4,5120]{1,0:T(4,128)S(1...) custom-call(bf16[128,4096]{1,0:T(8,128)(2,1)} %refs_0_.1, ...), custom_call_target="tpu_custom_call" | custom-call | bytes 1048576 | tf_op jit(solution)/shard_map/pallas_call | solution.py:635
  2.1 0.5 %collective-permute-start = (bf16[3,5120]{1,0:T(4,128)(2,1)S(1)}, bf16[3,5120]{1,0:T(4,128)(2,1)S(1)}, u32[]{:S(2)}, u32[]{:S(2)}) collective-permute-start(bf16[3,5120]{1,0:T(4,128)(2,1)S(1)} %get-tuple-element.46.after_ref), channel_id=1, source_target_pairs={{0,1},{1,2},{2,0},{3,4},{4,3},{5,6},{6,5},{7,8},{8,7},{9,10},{10,9... | collective-permute-start | bytes 92168 | tf_op jit(solution)/shard_map/ppermute | solution.py:700
  2.6 2.6 %collective-permute-start.1 = (bf16[3,5120]{1,0:T(4,128)(2,1)S(1)}, bf16[3,5120]{1,0:T(4,128)(2,1)S(1)}, u32[]{:S(2)}, u32[]{:S(2)}) collective-permute-start(bf16[3,5120]{1,0:T(4,128)(2,1)S(1)} %get-tuple-element.46.after_ref), channel_id=1, source_target_pairs={{0,1},{1,0},{2,3},{3,2},{4,5},{5,4},{6,7},{7,6},{8,9},{9,8},{10,11... | collective-permute-start | bytes 92168 | tf_op jit(solution)/shard_map/ppermute | solution.py:614
  5.9 2.2 %shard_map.141 = (bf16[128,4096]{1,0:T(8,128)(2,1)S(1)}, bf16[128,512]{1,0:T(8,128)(2,1)S(1)}, f32[8,4096]{1,0:T(8,128)S(1)}, f32[8,512]{1,0:T(8,128)S(1)}, f32[...) custom-call(s32[1]{0:T(128)S(6)} %copy.15.len_ref, ...), custom_call_target="tpu_custom_call" | custom-call | bytes 4194304 | tf_op jit(solution)/shard_map/pallas_call | solution.py:635
  8.1 0.0 collective-permute-done.near_ref
  8.1 0.0 collective-permute-done.1.core_ref
  8.1 0.0 copy-done.1
  8.1 0.4 %shard_map.142 = (bf16[272,256]{1,0:T(8,128)(2,1)S(1)}, bf16[272,256]{1,0:T(8,128)(2,1)S(1)}, bf16[2,272,256]{2,1,0:T(8,128)(2,1)S(1)}, bf16[16,4096]{1,0:T(8,128)(2,1)S(1)}, bf16[16,512]{1,0:T(8,128)(2,1)S(1)}) custom-call(bf16[3,5120]{1,0:T(4,128)(2,1)S(1)} %collective-permute-done.near_ref, bf16[3,5120]{1,0:T(4,128)(2,1)S(1)} %collective-permute-done.1.core_ref, ...), custom_call_target="tpu_custom_call" | custom-call | bytes 1048576 | tf_op jit(solution)/shard_map/pallas_call | solution.py:635
  8.5 0.1 collective-permute-start.3
  8.6 0.5 %collective-permute-start.2 = (bf16[272,256]{1,0:T(8,128)(2,1)S(1)}, bf16[272,256]{1,0:T(8,128)(2,1)S(1)}, u32[]{:S(2)}, u32[]{:S(2)}) collective-permute-start(bf16[272,256]{1,0:T(8,128)(2,1)S(1)} %get-tuple-element.59), channel_id=1, source_target_pairs={{0,1},{1,0},{2,3},{3,2},{4,5},{5,4},{6,7},{7,6},{8,9},{9,8},{10,11... | collective-permute-start | bytes 417800 | tf_op jit(solution)/shard_map/ppermute | solution.py:614
  9.1 0.8 %collective-permute-done.3.recv_ref.far_ref.refs_9_ = bf16[272,256]{1,0:T(8,128)(2,1)S(1)} collective-permute-done((bf16[272,256]{1,0:T(8,128)(2,1)S(1)}, bf16[272,256]{1,0:T(8,128)(2,1)S(1)}, u32[]{:S(2)}, u32[]{:S(2)}) %collective-permute-start.3) | collective-permute-done | bytes 139296 | tf_op jit(solution)/shard_map/ppermute | solution.py:614
  10.0 0.0 copy-start.2
  10.0 0.1 shard_map.143.rest_0_
  10.0 1.6 %collective-permute-start.4 = (bf16[272,256]{1,0:T(8,128)(2,1)S(1)}, bf16[272,256]{1,0:T(8,128)(2,1)S(1)}, u32[]{:S(2)}, u32[]{:S(2)}) collective-permute-start(bf16[272,256]{1,0:T(8,128)(2,1)S(1)} %shard_map.143.rest_0_), channel_id=1, source_target_pairs={{0,2},{1,3},{2,0},{3,1},{4,6},{5,7},{6,4},{7,5},{8,10},{9,11},{10,... | collective-permute-start | bytes 417800 | tf_op jit(solution)/shard_map/ppermute | solution.py:614
  11.6 0.0 collective-permute-done.2.recv_ref.near_ref.refs_10_
  11.6 0.1 shard_map.144.after_ref.mine_ref.own_ref
  11.7 2.5 %shard_map.146.cache_ref = f32[256,256]{1,0:T(8,128)S(1)} custom-call(f32[32,64,128]{2,1,0:T(8,128)} %bitcast.9, bf16[272,256]{1,0:T(8,128)(2,1)S(1)} %shard_map.144.after_ref.mine_ref.own_ref), custom_call_target="tpu_custom_call" | custom-call | bytes 2097152 | tf_op jit(solution)/shard_map/pallas_call | solution.py:635
  14.2 0.2 shard_map.145
  14.5 1.3 %collective-permute-done.4.other_ref.recv_ref = bf16[272,256]{1,0:T(8,128)(2,1)S(1)} collective-permute-done((bf16[272,256]{1,0:T(8,128)(2,1)S(1)}, bf16[272,256]{1,0:T(8,128)(2,1)S(1)}, u32[]{:S(2)}, u32[]{:S(2)}) %collective-permute-start.4) | collective-permute-done | bytes 139296 | tf_op jit(solution)/shard_map/ppermute | solution.py:614
  15.8 0.1 shard_map.147.after_ref.mine_ref
  15.9 1.6 %collective-permute-start.5 = (bf16[272,256]{1,0:T(8,128)(2,1)S(1)}, bf16[272,256]{1,0:T(8,128)(2,1)S(1)}, u32[]{:S(2)}, u32[]{:S(2)}) collective-permute-start(bf16[272,256]{1,0:T(8,128)(2,1)S(1)} %shard_map.147.after_ref.mine_ref), channel_id=1, source_target_pairs={{0,4},{1,5},{2,6},{3,7},{4,0},{5,1},{6,2},{7,3},{8,12},{9,13},{10,... | collective-permute-start | bytes 417800 | tf_op jit(solution)/shard_map/ppermute | solution.py:614
  17.6 0.0 copy-done.2
  17.6 1.7 %shard_map.148.after_ref.refs_0_ = f32[128,2048]{1,0:T(8,128)S(1)} custom-call(bf16[128,4096]{1,0:T(8,128)(2,1)S(1)} %get-tuple-element.47.xc_ref, bf16[16,4096]{1,0:T(8,128)(2,1)S(1)} %get-tuple-element.54.xfix_ref, bf16[128,512]{1,0:T(8,128)(2,1)S(1)} %get-tuple-element.50.bc_ref.b_ref, bf16[16,512]{1,0:T(8,128)(2,1)S(1)} %get-tuple-element.55.bfix_ref, ...), custom_call_target="tpu_custom_call" | custom-call | bytes 4194304 | tf_op jit(solution)/shard_map/pallas_call | solution.py:635
  19.3 1.7 %collective-permute-done.5.other_ref = bf16[272,256]{1,0:T(8,128)(2,1)S(1)} collective-permute-done((bf16[272,256]{1,0:T(8,128)(2,1)S(1)}, bf16[272,256]{1,0:T(8,128)(2,1)S(1)}, u32[]{:S(2)}, u32[]{:S(2)}) %collective-permute-start.5) | collective-permute-done | bytes 139296 | tf_op jit(solution)/shard_map/ppermute | solution.py:614
  21.0 0.1 shard_map.149
  21.1 0.0 copy-start
  21.1 3.7 %collective-permute-start.6 = (bf16[272,256]{1,0:T(8,128)(2,1)S(1)}, bf16[272,256]{1,0:T(8,128)(2,1)S(1)}, u32[]{:S(2)}, u32[]{:S(2)}) collective-permute-start(bf16[272,256]{1,0:T(8,128)(2,1)S(1)} %get-tuple-element.64.after_ref.mine_ref), channel_id=1, source_target_pairs={{0,12},{1,13},{2,14},{3,15},{4,8},{5,9},{6,10},{7,11},{8,4},{9,5},... | collective-permute-start | bytes 417800 | tf_op jit(solution)/shard_map/ppermute | solution.py:614
  24.8 1.7 %shard_map.150.after_ref.refs_1_ = f32[128,2048]{1,0:T(8,128)S(1)} custom-call(bf16[128,4096]{1,0:T(8,128)(2,1)S(1)} %get-tuple-element.47.xc_ref, bf16[16,4096]{1,0:T(8,128)(2,1)S(1)} %get-tuple-element.54.xfix_ref, bf16[128,512]{1,0:T(8,128)(2,1)S(1)} %get-tuple-element.50.bc_ref.b_ref, bf16[16,512]{1,0:T(8,128)(2,1)S(1)} %get-tuple-element.55.bfix_ref, ...), custom_call_target="tpu_custom_call" | custom-call | bytes 4194304 | tf_op jit(solution)/shard_map/pallas_call | solution.py:635
  26.5 1.6 %collective-permute-done.6.other_ref = bf16[272,256]{1,0:T(8,128)(2,1)S(1)} collective-permute-done((bf16[272,256]{1,0:T(8,128)(2,1)S(1)}, bf16[272,256]{1,0:T(8,128)(2,1)S(1)}, u32[]{:S(2)}, u32[]{:S(2)}) %collective-permute-start.6) | collective-permute-done | bytes 139296 | tf_op jit(solution)/shard_map/ppermute | solution.py:614
  28.2 0.2 shard_map.151
  28.4 1.6 %collective-permute-start.7 = (bf16[256,256]{1,0:T(8,128)(2,1)S(1)}, bf16[256,256]{1,0:T(8,128)(2,1)S(1)}, u32[]{:S(2)}, u32[]{:S(2)}) collective-permute-start(bf16[256,256]{1,0:T(8,128)(2,1)S(1)} %get-tuple-element.72), channel_id=1, source_target_pairs={{0,2},{1,3},{2,0},{3,1},{4,6},{5,7},{6,4},{7,5},{8,10},{9,11},{10,... | collective-permute-start | bytes 393224 | tf_op jit(solution)/shard_map/ppermute | solution.py:614
  30.0 1.0 %shard_map.153 = (f32[128,4096]{1,0:T(8,128)S(1)}, f32[256,64]{1,0:T(8,128)}) custom-call(bf16[4,128,64]{2,1,0:T(8,128)(2,1)S(1)} %get-tuple-element.68.ecum_ref, f32[256,256]{1,0:T(8,128)S(1)} %get-tuple-element.67.after_ref.final_ref), custom_call_target="tpu_custom_call" | custom-call | bytes 5242880 | tf_op jit(solution)/shard_map/pallas_call | solution.py:635
  30.9 0.0 copy-done
  30.9 0.4 %shard_map.152.gate_ref.refs_2_ = f32[128,4096]{1,0:T(8,128)S(1)} custom-call(s32[1]{0:T(128)S(6)} %copy.15.len_ref, bf16[128,4096]{1,0:T(8,128)(2,1)S(1)} %copy-done, f32[256,256]{1,0:T(8,128)S(1)} %get-tuple-element.67.after_ref.final_ref), custom_call_target="tpu_custom_call" | custom-call | bytes 1048576 | tf_op jit(solution)/shard_map/pallas_call | solution.py:635
  31.4 2.0 %collective-permute-done.7.recv_ref.refs_7_ = bf16[256,256]{1,0:T(8,128)(2,1)S(1)} collective-permute-done((bf16[256,256]{1,0:T(8,128)(2,1)S(1)}, bf16[256,256]{1,0:T(8,128)(2,1)S(1)}, u32[]{:S(2)}, u32[]{:S(2)}) %collective-permute-start.7) | collective-permute-done | bytes 131104 | tf_op jit(solution)/shard_map/ppermute | solution.py:614
  33.4 0.1 shard_map.154.refs_11_
  33.5 0.1 collective-permute-start.8
  33.6 0.5 %shard_map.155 = (f32[8,128,256]{2,1,0:T(8,128)S(1)}, f32[8,128,128]{2,1,0:T(8,128)S(1)}) custom-call(f32[128,2048]{1,0:T(8,128)S(1)} %shard_map.148.after_ref.refs_0_, f32[128,2048]{1,0:T(8,128)S(1)} %shard_map.150.after_ref.refs_1_, f32[128,4096]{1,0:T(8,128)S(1)} %shard_map.152.gate_ref.refs_2_, f32[128,4096]{1,0:T(8,128)S(1)} %get-tuple-element.69.grow_ref.refs_3_, ...), custom_call_target="tpu_custom_call" | custom-call | bytes 1048576 | tf_op jit(solution)/shard_map/pallas_call | solution.py:635
  34.0 1.1 %collective-permute-done.8.refs_7_ = bf16[2,256,256]{2,1,0:T(8,128)(2,1)S(1)} collective-permute-done((bf16[2,256,256]{2,1,0:T(8,128)(2,1)S(1)}, bf16[2,256,256]{2,1,0:T(8,128)(2,1)S(1)}, u32[]{:S(2)}, u32[]{:S(2)}) %collective-permute-start.8) | collective-permute-done | bytes 262176 | tf_op jit(solution)/shard_map/ppermute | solution.py:614
  35.1 1.5 %shard_map.156 = bf16[128,4096]{1,0:T(8,128)(2,1)} custom-call(f32[128,2048]{1,0:T(8,128)S(1)} %shard_map.148.after_ref.refs_0_, f32[128,2048]{1,0:T(8,128)S(1)} %shard_map.150.after_ref.refs_1_, f32[128,4096]{1,0:T(8,128)S(1)} %shard_map.152.gate_ref.refs_2_, f32[128,4096]{1,0:T(8,128)S(1)} %get-tuple-element.69.grow_ref.refs_3_, ...), custom_call_target="tpu_custom_call" | custom-call | bytes 4194304 | tf_op jit(solution)/shard_map/pallas_call | solution.py:635
Async XLA Ops:
  0.6 7.5 %copy-start.1 = (bf16[3,5120]{1,0:T(4,128)(2,1)S(1)}, bf16[3,5120]{1,0:T(4,128)(2,1)}, u32[]{:S(2)}) copy-start(bf16[3,5120]{1,0:T(4,128)(2,1)} %cache_ref.3) | copy-start | bytes 92164
  2.1 6.0 %collective-permute-start = (bf16[3,5120]{1,0:T(4,128)(2,1)S(1)}, bf16[3,5120]{1,0:T(4,128)(2,1)S(1)}, u32[]{:S(2)}, u32[]{:S(2)}) collective-permute-start(bf16[3,5120]{1,0:T(4,128)(2,1)S(1)} %get-tuple-element.46.after_ref), channel_id=1, source_target_pairs={{0,1},{1,2},{2,0},{3,4},{4,3},{5,6},{6,5},{7,8},{8,7},{9,10},{10,9... | collective-permute-start | bytes 92168 | tf_op jit(solution)/shard_map/ppermute | solution.py:700
  2.6 5.5 %collective-permute-start.1 = (bf16[3,5120]{1,0:T(4,128)(2,1)S(1)}, bf16[3,5120]{1,0:T(4,128)(2,1)S(1)}, u32[]{:S(2)}, u32[]{:S(2)}) collective-permute-start(bf16[3,5120]{1,0:T(4,128)(2,1)S(1)} %get-tuple-element.46.after_ref), channel_id=1, source_target_pairs={{0,1},{1,0},{2,3},{3,2},{4,5},{5,4},{6,7},{7,6},{8,9},{9,8},{10,11... | collective-permute-start | bytes 92168 | tf_op jit(solution)/shard_map/ppermute | solution.py:614
  8.5 1.4 %collective-permute-start.3 = (bf16[272,256]{1,0:T(8,128)(2,1)S(1)}, bf16[272,256]{1,0:T(8,128)(2,1)S(1)}, u32[]{:S(2)}, u32[]{:S(2)}) collective-permute-start(bf16[272,256]{1,0:T(8,128)(2,1)S(1)} %get-tuple-element.60), channel_id=1, source_target_pairs={{0,1},{1,0},{2,3},{3,2},{4,5},{5,4},{6,7},{7,6},{8,9},{9,8},{10,11... | collective-permute-start | bytes 417800 | tf_op jit(solution)/shard_map/ppermute | solution.py:614
  8.6 3.0 %collective-permute-start.2 = (bf16[272,256]{1,0:T(8,128)(2,1)S(1)}, bf16[272,256]{1,0:T(8,128)(2,1)S(1)}, u32[]{:S(2)}, u32[]{:S(2)}) collective-permute-start(bf16[272,256]{1,0:T(8,128)(2,1)S(1)} %get-tuple-element.59), channel_id=1, source_target_pairs={{0,1},{1,0},{2,3},{3,2},{4,5},{5,4},{6,7},{7,6},{8,9},{9,8},{10,11... | collective-permute-start | bytes 417800 | tf_op jit(solution)/shard_map/ppermute | solution.py:614
  10.0 7.6 %copy-start.2 = (f32[128]{0:T(128)S(1)}, f32[128]{0:T(128)}, u32[]{:S(2)}) copy-start(f32[128]{0:T(128)} %param.21) | copy-start | bytes 1540
  10.0 5.8 %collective-permute-start.4 = (bf16[272,256]{1,0:T(8,128)(2,1)S(1)}, bf16[272,256]{1,0:T(8,128)(2,1)S(1)}, u32[]{:S(2)}, u32[]{:S(2)}) collective-permute-start(bf16[272,256]{1,0:T(8,128)(2,1)S(1)} %shard_map.143.rest_0_), channel_id=1, source_target_pairs={{0,2},{1,3},{2,0},{3,1},{4,6},{5,7},{6,4},{7,5},{8,10},{9,11},{10,... | collective-permute-start | bytes 417800 | tf_op jit(solution)/shard_map/ppermute | solution.py:614
  15.9 5.1 %collective-permute-start.5 = (bf16[272,256]{1,0:T(8,128)(2,1)S(1)}, bf16[272,256]{1,0:T(8,128)(2,1)S(1)}, u32[]{:S(2)}, u32[]{:S(2)}) collective-permute-start(bf16[272,256]{1,0:T(8,128)(2,1)S(1)} %shard_map.147.after_ref.mine_ref), channel_id=1, source_target_pairs={{0,4},{1,5},{2,6},{3,7},{4,0},{5,1},{6,2},{7,3},{8,12},{9,13},{10,... | collective-permute-start | bytes 417800 | tf_op jit(solution)/shard_map/ppermute | solution.py:614
  21.1 9.8 %copy-start = (bf16[128,4096]{1,0:T(8,128)(2,1)S(1)}, bf16[128,4096]{1,0:T(8,128)(2,1)}, u32[]{:S(2)}) copy-start(bf16[128,4096]{1,0:T(8,128)(2,1)} %z_ref.1) | copy-start | bytes 3145732
  21.1 7.0 %collective-permute-start.6 = (bf16[272,256]{1,0:T(8,128)(2,1)S(1)}, bf16[272,256]{1,0:T(8,128)(2,1)S(1)}, u32[]{:S(2)}, u32[]{:S(2)}) collective-permute-start(bf16[272,256]{1,0:T(8,128)(2,1)S(1)} %get-tuple-element.64.after_ref.mine_ref), channel_id=1, source_target_pairs={{0,12},{1,13},{2,14},{3,15},{4,8},{5,9},{6,10},{7,11},{8,4},{9,5},... | collective-permute-start | bytes 417800 | tf_op jit(solution)/shard_map/ppermute | solution.py:614
  28.4 5.0 %collective-permute-start.7 = (bf16[256,256]{1,0:T(8,128)(2,1)S(1)}, bf16[256,256]{1,0:T(8,128)(2,1)S(1)}, u32[]{:S(2)}, u32[]{:S(2)}) collective-permute-start(bf16[256,256]{1,0:T(8,128)(2,1)S(1)} %get-tuple-element.72), channel_id=1, source_target_pairs={{0,2},{1,3},{2,0},{3,1},{4,6},{5,7},{6,4},{7,5},{8,10},{9,11},{10,... | collective-permute-start | bytes 393224 | tf_op jit(solution)/shard_map/ppermute | solution.py:614
  33.5 1.6 %collective-permute-start.8 = (bf16[2,256,256]{2,1,0:T(8,128)(2,1)S(1)}, bf16[2,256,256]{2,1,0:T(8,128)(2,1)S(1)}, u32[]{:S(2)}, u32[]{:S(2)}) collective-permute-start(bf16[2,256,256]{2,1,0:T(8,128)(2,1)S(1)} %shard_map.154.refs_11_), channel_id=1, source_target_pairs={{0,1},{1,0},{2,3},{3,2},{4,5},{5,4},{6,7},{7,6},{8,9},{9,8},{10,11... | collective-permute-start | bytes 786440 | tf_op jit(solution)/shard_map/ppermute | solution.py:614

commit v7 on v6

--- a/solution.py
+++ b/solution.py
@@ -437,43 +437,27 @@
         stay_ref[part, :] = jnp.where(side == 0, plane, second).astype(BF16)
 
 
-def chip_kernel(stay_ref, recv_ref, keep_ref, far_ref, near_ref, gate_ref, grow_ref, send_ref):
-    parts = (far_ref, near_ref)
-    enter_block(stay_ref, recv_ref, keep_ref, parts, send_ref, lax.axis_index(SEQ) % 2 == 1)
-
-
-def enter_block(stay_ref, recv_ref, keep_ref, parts, out_ref, first):
-    device = lax.axis_index(SEQ)
-    core, side = device % 2, (device // 2) % 2
-    rows = stay_ref.shape[0]
-
-    def fill(values):
-        for y in range(PAIR):
-            for mine, source in ((True, stay_ref), (False, recv_ref)):
-
-                @pl.when((side == y) == mine)
-                def _(y=y, source=source, mine=mine):
-                    values(y, source, mine)
+def chip_kernel(source_ref, keep_ref, part_ref, *rest, own):
+    core, side = lax.axis_index(SEQ) % 2, (lax.axis_index(SEQ) // 2) % 2
+    enter_block(source_ref, keep_ref, part_ref, rest[-1], core == 1, side if own else 1 - side)
+
+
+def enter_block(source_ref, keep_ref, part_ref, out_ref, first, slot):
+    core = lax.axis_index(SEQ) % 2
+    rows = source_ref.shape[0]
 
     @pl.when(first)
     def _():
-        def values(y, source, mine):
-            out_ref[y] = source[...]
-
-        fill(values)
-
-    for kept in range(2):
+        out_ref[...] = source_ref[...]
+
+    for kept, local in ((0, keep_ref.at[slot]), (1, part_ref)):
 
         @pl.when(jnp.logical_not(first) & (core == kept))
-        def _(kept=kept):
-            def values(y, source, mine):
-                local = parts[mine] if kept else keep_ref.at[y]
-                decay = unpack_decay(local[rows:, :])
-                for i, part in blocks_of(rows):
-                    entered = decay[i : i + 1] * source[part, :].astype(F32)
-                    out_ref[y, part, :] = (entered + local[part, :].astype(F32)).astype(BF16)
-
-            fill(values)
+        def _(local=local):
+            decay = unpack_decay(local[rows:, :])
+            for i, part in blocks_of(rows):
+                entered = decay[i : i + 1] * source_ref[part, :].astype(F32)
+                out_ref[part, :] = (entered + local[part, :].astype(F32)).astype(BF16)
 
 
 def diag_kernel(
@@ -553,16 +537,17 @@
     mine_ref[...] = mine.T
 
 
-def gated_part(parts, gate_ref, grow_ref, c_ref, state, group, half):
+def gated_part(parts, gate_ref, grow_ref, c_ref, state, i, y, half):
     width = gate_ref.shape[1] // GROUPS
     unit = width // 2
     per_part = GROUPS // len(parts)
-    inside = pl.ds(pl.multiple_of((group % per_part) * width + half * unit, 128), unit)
-    cols = pl.ds(pl.multiple_of(group * width + half * unit, 128), unit)
-    entering = jnp.dot(
-        c_ref[:, group * STATE : (group + 1) * STATE], state, preferred_element_type=F32
-    )
-    y_all = parts[group // per_part][:, inside] + grow_ref[:, cols] * entering
+    offset = y * width + half * unit
+    inside = pl.ds(pl.multiple_of(PAIR * i % per_part * width + offset, 128), unit)
+    cols = pl.ds(pl.multiple_of(PAIR * i * width + offset, 128), unit)
+    both = c_ref[:, PAIR * i * STATE : PAIR * (i + 1) * STATE]
+    c_group = jnp.where(y == 0, both[:, :STATE], both[:, STATE:])
+    entering = jnp.dot(c_group, state, preferred_element_type=F32)
+    y_all = parts[PAIR * i // per_part][:, inside] + grow_ref[:, cols] * entering
     return y_all.astype(BF16).astype(F32) * gate_ref[:, cols], cols
 
 
@@ -570,41 +555,56 @@
     return sum(value[:, j : j + 128] for j in range(0, value.shape[1], 128))
 
 
+def finish_group(held, i, y, halves, squares, out_ref, sems):
+    unit = halves[0][1].shape[1]
+    scale = lax.rsqrt(jnp.sum(squares, axis=1, keepdims=True) * (0.5 / unit) + 1e-05)
+    for half, value in halves:
+        held[i, :, pl.ds(pl.multiple_of(half * unit, 128), unit)] = (value * scale).astype(BF16)
+    first = pl.multiple_of((PAIR * i + y) * 2 * unit, 128)
+    copy = pltpu.make_async_copy(held.at[i], out_ref.at[:, pl.ds(first, 2 * unit)], sems.at[i])
+    copy.start()
+    return copy
+
+
 def own_kernel(*refs, parts):
     diag_refs, refs = refs[:parts], refs[parts:]
-    gate_ref, grow_ref, c_ref, gain_ref, stay_ref, recv_ref, keep_ref, *parts_in = refs[:9]
-    out_ref, sums_ref, own_ref = refs[10:]
-    core = lax.axis_index(SEQ) % 2
-    enter_block(stay_ref, recv_ref, keep_ref, parts_in, own_ref, core == 0)
-    for g in range(GROUPS):
-        i, y = g // PAIR, g % PAIR
-        state = own_ref[y, i * STATE : (i + 1) * STATE, :]
-        gated, cols = gated_part(diag_refs, gate_ref, grow_ref, c_ref, state, g, core)
-        sums_ref[g] = sum_lanes(gated * gated)
-        out_ref[g] = gated * gain_ref[:, cols]
+    gate_ref, grow_ref, c_ref, gain_ref, stay_ref, recv_ref, keep_ref, far_ref, near_ref, enter_ref = refs[:10]
+    out_ref, gated_ref, sums_ref, own_ref, held, sems = refs[11:]
+    core, side = lax.axis_index(SEQ) % 2, (lax.axis_index(SEQ) // 2) % 2
+    steps = held.shape[0]
+    given = (diag_refs, gate_ref, grow_ref, c_ref)
+    enter_block(stay_ref, keep_ref, near_ref, own_ref.at[0], core == 0, side)
+    copies = []
+    for i in range(steps):
+        part = slice(i * STATE, (i + 1) * STATE)
+        own, own_cols = gated_part(*given, own_ref[0, part, :], i, side, core)
+        other, cols = gated_part(*given, enter_ref[part, :], i, side, 1 - core)
+        squares = sum_lanes(own * own) + sum_lanes(other * other)
+        halves = ((core, own * gain_ref[:, own_cols]), (1 - core, other * gain_ref[:, cols]))
+        copies.append(finish_group(held, i, side, halves, squares, out_ref, sems))
+    enter_block(recv_ref, keep_ref, far_ref, own_ref.at[1], core == 0, 1 - side)
+    for i in range(steps):
+        part = slice(i * STATE, (i + 1) * STATE)
+        own, own_cols = gated_part(*given, own_ref[1, part, :], i, 1 - side, core)
+        sums_ref[i] = sum_lanes(own * own)
+        gated_ref[i] = own * gain_ref[:, own_cols]
+    for copy in copies:
+        copy.wait()
 
 
 def out_kernel(*refs, parts):
     diag_refs, refs = refs[:parts], refs[parts:]
-    gate_ref, grow_ref, c_ref, own_ref, sums_ref, recv_ref, gain_ref, out_ref, held, sems = refs
-    core = lax.axis_index(SEQ) % 2
-    unit = own_ref.shape[2]
-    width = 2 * unit
+    gate_ref, grow_ref, c_ref, gated_ref, sums_ref, enter_ref, gain_ref = refs[:7]
+    out_ref, held, sems = refs[8:]
+    core, side = lax.axis_index(SEQ) % 2, (lax.axis_index(SEQ) // 2) % 2
+    given = (diag_refs, gate_ref, grow_ref, c_ref)
     copies = []
-    for g in range(GROUPS):
-        i, y = g // PAIR, g % PAIR
-        state = recv_ref[y, i * STATE : (i + 1) * STATE, :]
-        other, cols = gated_part(diag_refs, gate_ref, grow_ref, c_ref, state, g, 1 - core)
-        squares = jnp.sum(sums_ref[g] + sum_lanes(other * other), axis=1, keepdims=True)
-        scale = lax.rsqrt(squares * (1.0 / width) + 1e-05)
-        for half, value in ((core, own_ref[g]), (1 - core, other * gain_ref[:, cols])):
-            lanes = pl.ds(pl.multiple_of(half * unit, 128), unit)
-            held[g, :, lanes] = (value * scale).astype(BF16)
-        copy = pltpu.make_async_copy(
-            held.at[g], out_ref.at[:, pl.ds(g * width, width)], sems.at[g]
-        )
-        copy.start()
-        copies.append(copy)
+    for i in range(held.shape[0]):
+        part = slice(i * STATE, (i + 1) * STATE)
+        other, cols = gated_part(*given, enter_ref[part, :], i, 1 - side, 1 - core)
+        squares = sums_ref[i] + sum_lanes(other * other)
+        halves = ((core, gated_ref[i]), (1 - core, other * gain_ref[:, cols]))
+        copies.append(finish_group(held, i, 1 - side, halves, squares, out_ref, sems))
     for copy in copies:
         copy.wait()
 
@@ -630,7 +630,7 @@
 
 
 def plain_call(
-    body, out_shape, *args, smem=(), far=(), after=(), mib=12, nbytes=2**20, scratch=(), out_specs=None
+    body, out_shape, *args, smem=(), far=(), after=(), mib=12, nbytes=2**20, scratch=(), out_specs=None, aliases=None
 ):
     return pl.pallas_call(
         body,
@@ -640,6 +640,7 @@
         + [VMEM_SPEC] * len(args) + [ANY_SPEC] * len(after),
         out_specs=out_specs or jax.tree.map(lambda _: VMEM_SPEC, out_shape),
         scratch_shapes=list(scratch),
+        input_output_aliases=aliases or {},
         compiler_params=pltpu.CompilerParams(vmem_limit_bytes=mib * 2**20),
         cost_estimate=pl.CostEstimate(flops=0, bytes_accessed=nbytes, transcendentals=0),
     )(*smem, *[pltpu.with_memory_space_constraint(a, pltpu.HBM) for a in far], *args, *after)
@@ -850,41 +851,55 @@
     gate = plain_call(
         gate_kernel, near((rows, inner), F32), z_in, smem=(lengths,), after=(final,)
     )
-    half = near((PAIR, state_rows, unit), BF16)
-    send_c = plain_call(chip_kernel, half, stay, recv_y, keep, part_far, part_near, after=(gate, grow))
-    enter_recv = swap(send_c, 1)
+    send_near = plain_call(
+        functools.partial(chip_kernel, own=True),
+        state_out,
+        stay,
+        keep,
+        part_near,
+        after=(gate, grow),
+    )
+    enter_near = swap(send_near, 1)
+    send_far = plain_call(
+        functools.partial(chip_kernel, own=False),
+        state_out,
+        recv_y,
+        keep,
+        part_far,
+        after=(send_near,),
+    )
+    enter_far = swap(send_far, 1)
     gain = ready[-1]
-    gated_own, own_sums = plain_call(
+    held = [pltpu.VMEM((steps, rows, 2 * unit), BF16), dma((steps,))]
+    shared = (*diags, gate, grow, cc)
+    mixed, gated_own, own_sums = plain_call(
         functools.partial(own_kernel, parts=len(diags)),
-        (near((GROUPS, rows, unit), F32), near((GROUPS, rows, 128), F32)),
-        *diags,
-        gate,
-        grow,
-        cc,
+        (
+            pltpu.HBM((rows, inner), BF16),
+            near((steps, rows, unit), F32),
+            near((steps, rows, 128), F32),
+        ),
+        *shared,
         gain,
         stay,
         recv_y,
         keep,
         part_far,
         part_near,
-        after=(send_c,),
-        scratch=[pltpu.VMEM((PAIR, state_rows, unit), BF16)],
-    )
-
+        enter_near,
+        after=(send_far,),
+        out_specs=(ANY_SPEC, VMEM_SPEC, VMEM_SPEC),
+        scratch=[pltpu.VMEM((2, state_rows, unit), BF16)] + held,
+    )
+    operands = (*shared, gated_own, own_sums, enter_far, gain)
     mixed = plain_call(
         functools.partial(out_kernel, parts=len(diags)),
-        jax.ShapeDtypeStruct((rows, inner), BF16),
-        *diags,
-        gate,
-        grow,
-        cc,
-        gated_own,
-        own_sums,
-        enter_recv,
-        gain,
+        pltpu.HBM((rows, inner), BF16),
+        *operands,
+        after=(mixed,),
         out_specs=ANY_SPEC,
-        scratch=[pltpu.VMEM((GROUPS, rows, 2 * unit), BF16), dma((GROUPS,))],
-        mib=16,
+        scratch=held,
+        aliases={len(operands): 0},
         nbytes=4 * 2**20,
     )
 

time: 36.8 us -> 36.4 us (0.989)
  waiting for transfers between devices: 8.64 us -> 7.48 us
  Pallas kernels: 14.2 us -> 14.9 us
    ppermute x8 -> x9, waiting for transfers between devices: 8.63 us -> 7.48 us  [swap(): return lax.ppermute(value, SEQ, [(i, i ^ mask) for i in devices])]
    pallas_call x17 -> x18, Pallas kernels: 14.2 us -> 14.9 us  [plain_call(): pl.pallas_call(body, out_shape=out_shape, in_specs=[pl.BlockSpec(memory_s...]
    ppermute x8 -> x9, starting transfers between devices: 11.8 us -> 11.8 us  [swap(): return lax.ppermute(value, SEQ, [(i, i ^ mask) for i in devices])]
  transfers between devices with their start and end apart: 9 -> 10, of which waited for: 6 -> 5; matrix products, arithmetic and copies ran while one was open for 0% -> 0% of each run, Pallas kernels for 28% -> 31%
where the time goes in v7:
time: 36.4 us; the launch traced here: 36.2 us
  Pallas kernels  14.9 us (41%)
  starting transfers between devices  12.3 us (34%)
  waiting for transfers between devices  7.48 us (21%)
  between operations  1.48 us (4%)
    pallas_call x18, Pallas kernels, plain_call(): pl.pallas_call(body, out_shape=out_shape, in_specs=[pl.BlockSpec(memory_s...  14.9 us
    ppermute x9, starting transfers between devices, swap(): return lax.ppermute(value, SEQ, [(i, i ^ mask) for i in devices])  11.8 us
    ppermute x9, waiting for transfers between devices, swap(): return lax.ppermute(value, SEQ, [(i, i ^ mask) for i in devices])  7.48 us
  transfers between devices with their start and end apart: 10, of which 5 were waited for; matrix products, arithmetic and copies ran while one was open for 0% of the time, Pallas kernels for 31%

profile of v7, /device:TPU:0, one launch (start us, length us, event | category | flops | bytes accessed | tf_op | source)
XLA Modules:
  0.0 36.2 jit_solution(7070922862660656702)
XLA Ops:
  0.6 0.0 copy-start.1
  0.6 1.5 %shard_map.140 = (bf16[3,5120]{1,0:T(4,128)(2,1)S(1)}, bf16[128,4096]{1,0:T(8,128)(2,1)S(1)}, bf16[128,1024]{1,0:T(8,128)(2,1)S(1)}, f32[4,5120]{1,0:T(4,128)S(1...) custom-call(bf16[128,4096]{1,0:T(8,128)(2,1)} %refs_0_.1, ...), custom_call_target="tpu_custom_call" | custom-call | bytes 1048576 | tf_op jit(solution)/shard_map/pallas_call | solution.py:635
  2.1 0.5 %collective-permute-start = (bf16[3,5120]{1,0:T(4,128)(2,1)S(1)}, bf16[3,5120]{1,0:T(4,128)(2,1)S(1)}, u32[]{:S(2)}, u32[]{:S(2)}) collective-permute-start(bf16[3,5120]{1,0:T(4,128)(2,1)S(1)} %get-tuple-element.47.after_ref), channel_id=1, source_target_pairs={{0,1},{1,2},{2,0},{3,4},{4,3},{5,6},{6,5},{7,8},{8,7},{9,10},{10,9... | collective-permute-start | bytes 92168 | tf_op jit(solution)/shard_map/ppermute | solution.py:701
  2.6 2.6 %collective-permute-start.1 = (bf16[3,5120]{1,0:T(4,128)(2,1)S(1)}, bf16[3,5120]{1,0:T(4,128)(2,1)S(1)}, u32[]{:S(2)}, u32[]{:S(2)}) collective-permute-start(bf16[3,5120]{1,0:T(4,128)(2,1)S(1)} %get-tuple-element.47.after_ref), channel_id=1, source_target_pairs={{0,1},{1,0},{2,3},{3,2},{4,5},{5,4},{6,7},{7,6},{8,9},{9,8},{10,11... | collective-permute-start | bytes 92168 | tf_op jit(solution)/shard_map/ppermute | solution.py:614
  5.9 2.2 %shard_map.141 = (bf16[128,4096]{1,0:T(8,128)(2,1)S(1)}, bf16[128,512]{1,0:T(8,128)(2,1)S(1)}, f32[8,4096]{1,0:T(8,128)S(1)}, f32[8,512]{1,0:T(8,128)S(1)}, f32[...) custom-call(s32[1]{0:T(128)S(6)} %copy.17.len_ref, ...), custom_call_target="tpu_custom_call" | custom-call | bytes 4194304 | tf_op jit(solution)/shard_map/pallas_call | solution.py:635
  8.1 0.0 collective-permute-done.near_ref
  8.1 0.0 collective-permute-done.1.core_ref
  8.1 0.0 copy-done.1
  8.1 0.4 %shard_map.142 = (bf16[272,256]{1,0:T(8,128)(2,1)S(1)}, bf16[272,256]{1,0:T(8,128)(2,1)S(1)}, bf16[2,272,256]{2,1,0:T(8,128)(2,1)S(1)}, bf16[16,4096]{1,0:T(8,128)(2,1)S(1)}, bf16[16,512]{1,0:T(8,128)(2,1)S(1)}) custom-call(bf16[3,5120]{1,0:T(4,128)(2,1)S(1)} %collective-permute-done.near_ref, bf16[3,5120]{1,0:T(4,128)(2,1)S(1)} %collective-permute-done.1.core_ref, ...), custom_call_target="tpu_custom_call" | custom-call | bytes 1048576 | tf_op jit(solution)/shard_map/pallas_call | solution.py:635
  8.5 0.1 collective-permute-start.3
  8.6 0.5 %collective-permute-start.2 = (bf16[272,256]{1,0:T(8,128)(2,1)S(1)}, bf16[272,256]{1,0:T(8,128)(2,1)S(1)}, u32[]{:S(2)}, u32[]{:S(2)}) collective-permute-start(bf16[272,256]{1,0:T(8,128)(2,1)S(1)} %get-tuple-element.60), channel_id=1, source_target_pairs={{0,1},{1,0},{2,3},{3,2},{4,5},{5,4},{6,7},{7,6},{8,9},{9,8},{10,11... | collective-permute-start | bytes 417800 | tf_op jit(solution)/shard_map/ppermute | solution.py:614
  9.1 0.8 %collective-permute-done.3.recv_ref.part_ref.refs_9_ = bf16[272,256]{1,0:T(8,128)(2,1)S(1)} collective-permute-done((bf16[272,256]{1,0:T(8,128)(2,1)S(1)}, bf16[272,256]{1,0:T(8,128)(2,1)S(1)}, u32[]{:S(2)}, u32[]{:S(2)}) %collective-permute-start.3) | collective-permute-done | bytes 139296 | tf_op jit(solution)/shard_map/ppermute | solution.py:614
  10.0 0.0 copy-start.2
  10.0 0.1 shard_map.143.rest_0_
  10.0 1.6 %collective-permute-start.4 = (bf16[272,256]{1,0:T(8,128)(2,1)S(1)}, bf16[272,256]{1,0:T(8,128)(2,1)S(1)}, u32[]{:S(2)}, u32[]{:S(2)}) collective-permute-start(bf16[272,256]{1,0:T(8,128)(2,1)S(1)} %shard_map.143.rest_0_), channel_id=1, source_target_pairs={{0,2},{1,3},{2,0},{3,1},{4,6},{5,7},{6,4},{7,5},{8,10},{9,11},{10,... | collective-permute-start | bytes 417800 | tf_op jit(solution)/shard_map/ppermute | solution.py:614
  11.6 0.0 collective-permute-done.2.recv_ref.part_ref.refs_10_
  11.6 0.1 shard_map.144.after_ref.mine_ref.own_ref
  11.7 2.5 %shard_map.146.cache_ref = f32[256,256]{1,0:T(8,128)S(1)} custom-call(f32[32,64,128]{2,1,0:T(8,128)} %bitcast.9, bf16[272,256]{1,0:T(8,128)(2,1)S(1)} %shard_map.144.after_ref.mine_ref.own_ref), custom_call_target="tpu_custom_call" | custom-call | bytes 2097152 | tf_op jit(solution)/shard_map/pallas_call | solution.py:635
  14.2 0.2 shard_map.145
  14.5 1.3 %collective-permute-done.4.other_ref.recv_ref = bf16[272,256]{1,0:T(8,128)(2,1)S(1)} collective-permute-done((bf16[272,256]{1,0:T(8,128)(2,1)S(1)}, bf16[272,256]{1,0:T(8,128)(2,1)S(1)}, u32[]{:S(2)}, u32[]{:S(2)}) %collective-permute-start.4) | collective-permute-done | bytes 139296 | tf_op jit(solution)/shard_map/ppermute | solution.py:614
  15.8 0.1 shard_map.147.after_ref.mine_ref
  15.9 1.6 %collective-permute-start.5 = (bf16[272,256]{1,0:T(8,128)(2,1)S(1)}, bf16[272,256]{1,0:T(8,128)(2,1)S(1)}, u32[]{:S(2)}, u32[]{:S(2)}) collective-permute-start(bf16[272,256]{1,0:T(8,128)(2,1)S(1)} %shard_map.147.after_ref.mine_ref), channel_id=1, source_target_pairs={{0,4},{1,5},{2,6},{3,7},{4,0},{5,1},{6,2},{7,3},{8,12},{9,13},{10,... | collective-permute-start | bytes 417800 | tf_op jit(solution)/shard_map/ppermute | solution.py:614
  17.6 0.0 copy-done.2
  17.6 1.7 %shard_map.148.after_ref.refs_0_ = f32[128,2048]{1,0:T(8,128)S(1)} custom-call(bf16[128,4096]{1,0:T(8,128)(2,1)S(1)} %get-tuple-element.48.xc_ref, bf16[16,4096]{1,0:T(8,128)(2,1)S(1)} %get-tuple-element.55.xfix_ref, bf16[128,512]{1,0:T(8,128)(2,1)S(1)} %get-tuple-element.51.bc_ref.b_ref, bf16[16,512]{1,0:T(8,128)(2,1)S(1)} %get-tuple-element.56.bfix_ref, ...), custom_call_target="tpu_custom_call" | custom-call | bytes 4194304 | tf_op jit(solution)/shard_map/pallas_call | solution.py:635
  19.3 1.7 %collective-permute-done.5.other_ref = bf16[272,256]{1,0:T(8,128)(2,1)S(1)} collective-permute-done((bf16[272,256]{1,0:T(8,128)(2,1)S(1)}, bf16[272,256]{1,0:T(8,128)(2,1)S(1)}, u32[]{:S(2)}, u32[]{:S(2)}) %collective-permute-start.5) | collective-permute-done | bytes 139296 | tf_op jit(solution)/shard_map/ppermute | solution.py:614
  21.0 0.1 shard_map.149
  21.1 0.0 copy-start
  21.1 3.7 %collective-permute-start.6 = (bf16[272,256]{1,0:T(8,128)(2,1)S(1)}, bf16[272,256]{1,0:T(8,128)(2,1)S(1)}, u32[]{:S(2)}, u32[]{:S(2)}) collective-permute-start(bf16[272,256]{1,0:T(8,128)(2,1)S(1)} %get-tuple-element.65.after_ref.mine_ref), channel_id=1, source_target_pairs={{0,12},{1,13},{2,14},{3,15},{4,8},{5,9},{6,10},{7,11},{8,4},{9,5},... | collective-permute-start | bytes 417800 | tf_op jit(solution)/shard_map/ppermute | solution.py:614
  24.8 1.7 %shard_map.150.after_ref.refs_1_ = f32[128,2048]{1,0:T(8,128)S(1)} custom-call(bf16[128,4096]{1,0:T(8,128)(2,1)S(1)} %get-tuple-element.48.xc_ref, bf16[16,4096]{1,0:T(8,128)(2,1)S(1)} %get-tuple-element.55.xfix_ref, bf16[128,512]{1,0:T(8,128)(2,1)S(1)} %get-tuple-element.51.bc_ref.b_ref, bf16[16,512]{1,0:T(8,128)(2,1)S(1)} %get-tuple-element.56.bfix_ref, ...), custom_call_target="tpu_custom_call" | custom-call | bytes 4194304 | tf_op jit(solution)/shard_map/pallas_call | solution.py:635
  26.5 1.6 %collective-permute-done.6.other_ref = bf16[272,256]{1,0:T(8,128)(2,1)S(1)} collective-permute-done((bf16[272,256]{1,0:T(8,128)(2,1)S(1)}, bf16[272,256]{1,0:T(8,128)(2,1)S(1)}, u32[]{:S(2)}, u32[]{:S(2)}) %collective-permute-start.6) | collective-permute-done | bytes 139296 | tf_op jit(solution)/shard_map/ppermute | solution.py:614
  28.2 0.2 shard_map.151
  28.4 1.6 %collective-permute-start.7 = (bf16[256,256]{1,0:T(8,128)(2,1)S(1)}, bf16[256,256]{1,0:T(8,128)(2,1)S(1)}, u32[]{:S(2)}, u32[]{:S(2)}) collective-permute-start(bf16[256,256]{1,0:T(8,128)(2,1)S(1)} %get-tuple-element.73), channel_id=1, source_target_pairs={{0,2},{1,3},{2,0},{3,1},{4,6},{5,7},{6,4},{7,5},{8,10},{9,11},{10,... | collective-permute-start | bytes 393224 | tf_op jit(solution)/shard_map/ppermute | solution.py:614
  30.0 1.0 %shard_map.153 = (f32[128,4096]{1,0:T(8,128)S(1)}, f32[256,64]{1,0:T(8,128)}) custom-call(bf16[4,128,64]{2,1,0:T(8,128)(2,1)S(1)} %get-tuple-element.69.ecum_ref, f32[256,256]{1,0:T(8,128)S(1)} %get-tuple-element.68.after_ref.final_ref), custom_call_target="tpu_custom_call" | custom-call | bytes 5242880 | tf_op jit(solution)/shard_map/pallas_call | solution.py:635
  30.9 0.0 copy-done
  30.9 0.4 %shard_map.152.rest_0_.refs_2_ = f32[128,4096]{1,0:T(8,128)S(1)} custom-call(s32[1]{0:T(128)S(6)} %copy.17.len_ref, bf16[128,4096]{1,0:T(8,128)(2,1)S(1)} %copy-done, f32[256,256]{1,0:T(8,128)S(1)} %get-tuple-element.68.after_ref.final_ref), custom_call_target="tpu_custom_call" | custom-call | bytes 1048576 | tf_op jit(solution)/shard_map/pallas_call | solution.py:635
  31.4 0.1 shard_map.154.rest_0_
  31.4 0.1 collective-permute-start.8
  31.5 1.9 %collective-permute-done.7.source_ref.refs_7_ = bf16[256,256]{1,0:T(8,128)(2,1)S(1)} collective-permute-done((bf16[256,256]{1,0:T(8,128)(2,1)S(1)}, bf16[256,256]{1,0:T(8,128)(2,1)S(1)}, u32[]{:S(2)}, u32[]{:S(2)}) %collective-permute-start.7) | collective-permute-done | bytes 131104 | tf_op jit(solution)/shard_map/ppermute | solution.py:614
  33.5 0.1 collective-permute-start.9
  33.5 0.0 collective-permute-done.8.refs_11_
  33.5 1.4 %shard_map.156 = (bf16[128,4096]{1,0:T(8,128)(2,1)}, f32[4,128,256]{2,1,0:T(8,128)S(1)}, f32[4,128,128]{2,1,0:T(8,128)S(1)}) custom-call(f32[128,2048]{1,0:T(8,128)S(1)} %shard_map.148.after_ref.refs_0_, f32[128,2048]{1,0:T(8,128)S(1)} %shard_map.150.after_ref.refs_1_, f32[128,4096]{1,0:T(8,128)S(1)} %shard_map.152.rest_0_.refs_2_, ...), custom_call_target="tpu_custom_call" | custom-call | bytes 1048576 | tf_op jit(solution)/shard_map/pallas_call | solution.py:635
  34.9 0.0 collective-permute-done.9.refs_7_
  34.9 1.2 %shard_map.157 = bf16[128,4096]{1,0:T(8,128)(2,1)} custom-call(f32[128,2048]{1,0:T(8,128)S(1)} %shard_map.148.after_ref.refs_0_, f32[128,2048]{1,0:T(8,128)S(1)} %shard_map.150.after_ref.refs_1_, f32[128,4096]{1,0:T(8,128)S(1)} %shard_map.152.rest_0_.refs_2_, f32[128,4096]{1,0:T(8,128)S(1)} %get-tuple-element.70.rest_1_.refs_3_, ...), custom_call_target="tpu_custom_call", output_to_operand_aliasing={{}: (9, {})} | custom-call | bytes 4194304 | tf_op jit(solution)/shard_map/pallas_call | solution.py:635
  (1 shorter events, 0.0 us)
Async XLA Ops:
  0.6 7.5 %copy-start.1 = (bf16[3,5120]{1,0:T(4,128)(2,1)S(1)}, bf16[3,5120]{1,0:T(4,128)(2,1)}, u32[]{:S(2)}) copy-start(bf16[3,5120]{1,0:T(4,128)(2,1)} %cache_ref.3) | copy-start | bytes 92164
  2.1 6.0 %collective-permute-start = (bf16[3,5120]{1,0:T(4,128)(2,1)S(1)}, bf16[3,5120]{1,0:T(4,128)(2,1)S(1)}, u32[]{:S(2)}, u32[]{:S(2)}) collective-permute-start(bf16[3,5120]{1,0:T(4,128)(2,1)S(1)} %get-tuple-element.47.after_ref), channel_id=1, source_target_pairs={{0,1},{1,2},{2,0},{3,4},{4,3},{5,6},{6,5},{7,8},{8,7},{9,10},{10,9... | collective-permute-start | bytes 92168 | tf_op jit(solution)/shard_map/ppermute | solution.py:701
  2.6 5.5 %collective-permute-start.1 = (bf16[3,5120]{1,0:T(4,128)(2,1)S(1)}, bf16[3,5120]{1,0:T(4,128)(2,1)S(1)}, u32[]{:S(2)}, u32[]{:S(2)}) collective-permute-start(bf16[3,5120]{1,0:T(4,128)(2,1)S(1)} %get-tuple-element.47.after_ref), channel_id=1, source_target_pairs={{0,1},{1,0},{2,3},{3,2},{4,5},{5,4},{6,7},{7,6},{8,9},{9,8},{10,11... | collective-permute-start | bytes 92168 | tf_op jit(solution)/shard_map/ppermute | solution.py:614
  8.5 1.4 %collective-permute-start.3 = (bf16[272,256]{1,0:T(8,128)(2,1)S(1)}, bf16[272,256]{1,0:T(8,128)(2,1)S(1)}, u32[]{:S(2)}, u32[]{:S(2)}) collective-permute-start(bf16[272,256]{1,0:T(8,128)(2,1)S(1)} %get-tuple-element.61), channel_id=1, source_target_pairs={{0,1},{1,0},{2,3},{3,2},{4,5},{5,4},{6,7},{7,6},{8,9},{9,8},{10,11... | collective-permute-start | bytes 417800 | tf_op jit(solution)/shard_map/ppermute | solution.py:614
  8.6 3.0 %collective-permute-start.2 = (bf16[272,256]{1,0:T(8,128)(2,1)S(1)}, bf16[272,256]{1,0:T(8,128)(2,1)S(1)}, u32[]{:S(2)}, u32[]{:S(2)}) collective-permute-start(bf16[272,256]{1,0:T(8,128)(2,1)S(1)} %get-tuple-element.60), channel_id=1, source_target_pairs={{0,1},{1,0},{2,3},{3,2},{4,5},{5,4},{6,7},{7,6},{8,9},{9,8},{10,11... | collective-permute-start | bytes 417800 | tf_op jit(solution)/shard_map/ppermute | solution.py:614
  10.0 7.6 %copy-start.2 = (f32[128]{0:T(128)S(1)}, f32[128]{0:T(128)}, u32[]{:S(2)}) copy-start(f32[128]{0:T(128)} %param.21) | copy-start | bytes 1540
  10.0 5.8 %collective-permute-start.4 = (bf16[272,256]{1,0:T(8,128)(2,1)S(1)}, bf16[272,256]{1,0:T(8,128)(2,1)S(1)}, u32[]{:S(2)}, u32[]{:S(2)}) collective-permute-start(bf16[272,256]{1,0:T(8,128)(2,1)S(1)} %shard_map.143.rest_0_), channel_id=1, source_target_pairs={{0,2},{1,3},{2,0},{3,1},{4,6},{5,7},{6,4},{7,5},{8,10},{9,11},{10,... | collective-permute-start | bytes 417800 | tf_op jit(solution)/shard_map/ppermute | solution.py:614
  15.9 5.1 %collective-permute-start.5 = (bf16[272,256]{1,0:T(8,128)(2,1)S(1)}, bf16[272,256]{1,0:T(8,128)(2,1)S(1)}, u32[]{:S(2)}, u32[]{:S(2)}) collective-permute-start(bf16[272,256]{1,0:T(8,128)(2,1)S(1)} %shard_map.147.after_ref.mine_ref), channel_id=1, source_target_pairs={{0,4},{1,5},{2,6},{3,7},{4,0},{5,1},{6,2},{7,3},{8,12},{9,13},{10,... | collective-permute-start | bytes 417800 | tf_op jit(solution)/shard_map/ppermute | solution.py:614
  21.1 9.8 %copy-start = (bf16[128,4096]{1,0:T(8,128)(2,1)S(1)}, bf16[128,4096]{1,0:T(8,128)(2,1)}, u32[]{:S(2)}) copy-start(bf16[128,4096]{1,0:T(8,128)(2,1)} %z_ref.1) | copy-start | bytes 3145732
  21.1 7.0 %collective-permute-start.6 = (bf16[272,256]{1,0:T(8,128)(2,1)S(1)}, bf16[272,256]{1,0:T(8,128)(2,1)S(1)}, u32[]{:S(2)}, u32[]{:S(2)}) collective-permute-start(bf16[272,256]{1,0:T(8,128)(2,1)S(1)} %get-tuple-element.65.after_ref.mine_ref), channel_id=1, source_target_pairs={{0,12},{1,13},{2,14},{3,15},{4,8},{5,9},{6,10},{7,11},{8,4},{9,5},... | collective-permute-start | bytes 417800 | tf_op jit(solution)/shard_map/ppermute | solution.py:614
  28.4 5.0 %collective-permute-start.7 = (bf16[256,256]{1,0:T(8,128)(2,1)S(1)}, bf16[256,256]{1,0:T(8,128)(2,1)S(1)}, u32[]{:S(2)}, u32[]{:S(2)}) collective-permute-start(bf16[256,256]{1,0:T(8,128)(2,1)S(1)} %get-tuple-element.73), channel_id=1, source_target_pairs={{0,2},{1,3},{2,0},{3,1},{4,6},{5,7},{6,4},{7,5},{8,10},{9,11},{10,... | collective-permute-start | bytes 393224 | tf_op jit(solution)/shard_map/ppermute | solution.py:614
  31.4 2.1 %collective-permute-start.8 = (bf16[256,256]{1,0:T(8,128)(2,1)S(1)}, bf16[256,256]{1,0:T(8,128)(2,1)S(1)}, u32[]{:S(2)}, u32[]{:S(2)}) collective-permute-start(bf16[256,256]{1,0:T(8,128)(2,1)S(1)} %shard_map.154.rest_0_), channel_id=1, source_target_pairs={{0,1},{1,0},{2,3},{3,2},{4,5},{5,4},{6,7},{7,6},{8,9},{9,8},{10,11... | collective-permute-start | bytes 393224 | tf_op jit(solution)/shard_map/ppermute | solution.py:614
  33.5 1.5 %collective-permute-start.9 = (bf16[256,256]{1,0:T(8,128)(2,1)S(1)}, bf16[256,256]{1,0:T(8,128)(2,1)S(1)}, u32[]{:S(2)}, u32[]{:S(2)}) collective-permute-start(bf16[256,256]{1,0:T(8,128)(2,1)S(1)} %shard_map.155.refs_12_), channel_id=1, source_target_pairs={{0,1},{1,0},{2,3},{3,2},{4,5},{5,4},{6,7},{7,6},{8,9},{9,8},{10,11... | collective-permute-start | bytes 393224 | tf_op jit(solution)/shard_map/ppermute | solution.py:614
